TPU v7x, 32 devices: a whole 2x2x4 slice. The times are simulated.
32 devices in a mesh: seq: 8 (over y, x, core), tp: 4 (over z).
Axes of the slice: x: 2, y: 2, z: 4, core: 2. Of those that a mesh axis runs over, the one named last changes fastest.
Arguments:
- tokens: bfloat16 [6144, 2048], P('seq'), may hold values from -6 to 6
- q_weight: bfloat16 [2048, 2048], P('seq', 'tp'), may hold values from -0.125 to 0.125
- key_matrix: bfloat16 [2048, 1024], P('seq', 'tp'), may hold values from -0.125 to 0.125
- value_matrix: bfloat16 [2048, 1024], P('seq', 'tp'), may hold values from -0.125 to 0.125
- o_weight: bfloat16 [2048, 2048], P('tp', 'seq'), may hold values from -4 to 4
- gate_weight: bfloat16 [2048, 6144], P('seq', 'tp'), may hold values from -0.125 to 0.125
- up_weight: bfloat16 [2048, 6144], P('seq', 'tp'), may hold values from -0.125 to 0.125
- down_weight: bfloat16 [6144, 2048], P('tp', 'seq'), may hold values from -0.078125 to 0.078125
- attn_gain: bfloat16 [2048], P('seq'), may hold values from 0.5 to 1.5
- mlp_gain: bfloat16 [2048], P('seq'), may hold values from 0.5 to 1.5
- query_gain: bfloat16 [128], P('seq'), may hold values from 0.099609375 to 1.8984375
- key_gain: bfloat16 [128], P('seq'), may hold values from 0.099609375 to 1.8984375
- positions: int32 [6144], P('seq'), may hold values from 0 to 5759, as said below
- seq_ids: int32 [6144], replicated, may hold values from 0 to 2, as said below
- cotangent: bfloat16 [6144, 2048], P('seq'), may hold values from -6 to 6
Outputs:
- layer_out: bfloat16 [6144, 2048], P('seq')
- grad_tokens: float32 [6144, 2048], P('seq')
- grad_q_weight: float32 [2048, 2048], P('seq', 'tp')
- grad_k_weight: float32 [2048, 1024], P('seq', 'tp')
- grad_v_weight: float32 [2048, 1024], P('seq', 'tp')
- grad_o_weight: float32 [2048, 2048], P('tp', 'seq')
- grad_gate_weight: float32 [2048, 6144], P('seq', 'tp')
- grad_up_weight: float32 [2048, 6144], P('seq', 'tp')
- grad_down_weight: float32 [6144, 2048], P('tp', 'seq')
- grad_attn_gain: float32 [2048], P('seq')
- grad_mlp_gain: float32 [2048], P('seq')
- grad_query_gain: float32 [128], P('seq')
- grad_key_gain: float32 [128], P('seq')
Inputs may be any that keep to these rules, and one draw needn't show every extreme that they name: `seq_ids`: document 0 starts at the first token and ends inside the last 768 tokens; documents 1 and 2 fill the rest of that block in order, each with one token or more. `positions`: position of each token within its document, counting from 0.
All inputs are finite; a program needn't handle non-finite values.
Results may differ from a plain program's by a relative error of at most 0.025.
Values may be sent and summed in bfloat16 or wider, within the bound.
A program may use at most 192 MiB of HBM per device.

v0:
```python
import math

import jax
import jax.numpy as jnp
from jax import lax
from jax.sharding import PartitionSpec as P

HEAD_SIZE = 128


EPS = 1e-06
BASE = 1000000.0


def norm_rows(values, gain_vec):
    return values * lax.rsqrt(jnp.mean(values * values, axis=-1, keepdims=True) + EPS) * gain_vec


def norm_back(values, gain_vec, grad_out):
    inverse = lax.rsqrt(jnp.mean(values * values, axis=-1, keepdims=True) + EPS)
    normed = values * inverse
    scaled = grad_out * gain_vec
    grad_in = inverse * (scaled - normed * jnp.mean(scaled * normed, axis=-1, keepdims=True))
    return (grad_in, grad_out * normed)


def rope_tables(positions, head_dim):
    half_dim = head_dim // 2
    frequency = BASE ** (-2.0 * jnp.arange(half_dim, dtype=jnp.float32) / head_dim)
    angles = positions.astype(jnp.float32)[:, None] * frequency[None, :]
    return (jnp.cos(angles)[:, None, :], jnp.sin(angles)[:, None, :])


def rotate(values, cosines, sine_values, direction):
    half_dim = values.shape[-1] // 2
    lower_half = values[..., :half_dim]
    upper_half = values[..., half_dim:]
    signed = sine_values * direction
    return jnp.concatenate(
        [lower_half * cosines - upper_half * signed, upper_half * cosines + lower_half * signed],
        axis=-1,
    )


def per_device(
    tokens,
    q_weight,
    key_matrix,
    value_matrix,
    o_weight,
    gate_weight,
    up_weight,
    down_weight,
    attn_gain,
    mlp_gain,
    query_gain,
    key_gain,
    positions,
    seq_ids,
    cotangent,
):
    f32 = jnp.float32
    b16 = jnp.bfloat16
    local_rows = tokens.shape[0]
    q_local = q_weight.shape[1] // HEAD_SIZE
    kv_local = key_matrix.shape[1] // HEAD_SIZE
    heads_per_group = q_local // kv_local
    score_scale = HEAD_SIZE ** (-0.5)
    share_rows = local_rows // lax.axis_size("tp")
    share_start = lax.axis_index("tp") * share_rows
    row_parts = (
        lax.all_gather(q_weight, "seq", axis=0, tiled=True),
        lax.all_gather(key_matrix, "seq", axis=0, tiled=True),
        lax.all_gather(value_matrix, "seq", axis=0, tiled=True),
        lax.all_gather(gate_weight, "seq", axis=0, tiled=True),
        lax.all_gather(up_weight, "seq", axis=0, tiled=True),
        lax.all_gather(attn_gain, "seq", axis=0, tiled=True),
        lax.all_gather(mlp_gain, "seq", axis=0, tiled=True),
        lax.all_gather(query_gain, "seq", axis=0, tiled=True),
        lax.all_gather(key_gain, "seq", axis=0, tiled=True),
    )
    col_parts = (
        lax.all_gather(o_weight, "seq", axis=1, tiled=True),
        lax.all_gather(down_weight, "seq", axis=1, tiled=True),
    )
    full_q, full_k, full_v, full_gate, full_up, gain_attn, gain_mlp, gain_query, gain_key = (
        row_parts
    )
    full_o, full_down = col_parts
    gain_attn = gain_attn.astype(f32)
    gain_mlp = gain_mlp.astype(f32)
    gain_query = gain_query.astype(f32)
    gain_key = gain_key.astype(f32)
    token_f = tokens.astype(f32)
    normalized_input = norm_rows(token_f, gain_attn).astype(b16)
    q_proj = jnp.dot(normalized_input, full_q, preferred_element_type=f32).reshape(
        local_rows, q_local, HEAD_SIZE
    )
    key_projected = jnp.dot(normalized_input, full_k, preferred_element_type=f32).reshape(
        local_rows, kv_local, HEAD_SIZE
    )
    v_local = (
        jnp.dot(normalized_input, full_v, preferred_element_type=f32)
        .astype(b16)
        .reshape(local_rows, kv_local, HEAD_SIZE)
    )
    cosines, sine_values = rope_tables(positions, HEAD_SIZE)
    q_final = rotate(norm_rows(q_proj, gain_query), cosines, sine_values, 1.0).astype(b16)
    k_local = rotate(norm_rows(key_projected, gain_key), cosines, sine_values, 1.0).astype(b16)
    all_keys, all_values = (
        lax.all_gather(k_local, "seq", axis=0, tiled=True),
        lax.all_gather(v_local, "seq", axis=0, tiled=True),
    )
    row_offset = lax.axis_index("seq") * local_rows
    key_rows = all_keys.shape[0]
    key_block = math.gcd(key_rows, 512)
    block_count = key_rows // key_block
    q_docs = lax.dynamic_slice_in_dim(seq_ids, row_offset, local_rows)
    q_places = row_offset + jnp.arange(local_rows, dtype=jnp.int32)
    grouped_queries = q_final.reshape(local_rows, kv_local, heads_per_group, HEAD_SIZE)
    block_ids = jnp.arange(block_count, dtype=jnp.int32)

    def block_scores(keys_blk, block_index):
        offset = block_index * key_block
        k_places = offset + jnp.arange(key_block, dtype=jnp.int32)
        k_docs = lax.dynamic_slice_in_dim(seq_ids, offset, key_block)
        allowed = (k_places[None, :] <= q_places[:, None]) & (k_docs[None, :] == q_docs[:, None])
        scores = (
            jnp.einsum("lkgd,mkd->kglm", grouped_queries, keys_blk, preferred_element_type=f32)
            * score_scale
        )
        return (scores, allowed[None, None])

    keys_blocked = all_keys.reshape(block_count, key_block, kv_local, HEAD_SIZE)
    values_blocked = all_values.reshape(block_count, key_block, kv_local, HEAD_SIZE)

    def stat_step(state_pair, inputs):
        row_max, row_sum = state_pair
        keys_blk, block_index = inputs
        scores, allowed = block_scores(keys_blk, block_index)
        new_max = jnp.maximum(row_max, jnp.max(jnp.where(allowed, scores, -1e30), axis=-1))
        weights = jnp.where(allowed, jnp.exp(scores - new_max[..., None]), 0.0)
        row_sum = row_sum * jnp.exp(row_max - new_max) + jnp.sum(weights, axis=-1)
        return ((new_max, row_sum), None)

    start_state = (
        jnp.full((kv_local, heads_per_group, local_rows), -1e30, f32),
        jnp.zeros((kv_local, heads_per_group, local_rows), f32),
    )
    (row_max, row_sum), _ = lax.scan(stat_step, start_state, (keys_blocked, block_ids))
    log_total = row_max + jnp.log(row_sum)

    def probs_of(keys_blk, block_index):
        scores, allowed = block_scores(keys_blk, block_index)
        return jnp.where(allowed, jnp.exp(scores - log_total[..., None]), 0.0)

    def mix_step(running, inputs):
        keys_blk, values_blk, block_index = inputs
        probability = probs_of(keys_blk, block_index).astype(b16)
        return (
            running
            + jnp.einsum("kglm,mkd->lkgd", probability, values_blk, preferred_element_type=f32),
            None,
        )

    attended, _ = lax.scan(
        mix_step,
        jnp.zeros((local_rows, kv_local, heads_per_group, HEAD_SIZE), f32),
        (keys_blocked, values_blocked, block_ids),
    )
    attended_low = attended.reshape(local_rows, q_local * HEAD_SIZE).astype(b16)
    attn_part = jnp.dot(attended_low, full_o, preferred_element_type=f32)
    after_attn = token_f + lax.psum(attn_part.astype(jnp.bfloat16), "tp").astype(jnp.float32)
    normed_mid = norm_rows(after_attn, gain_mlp).astype(b16)
    gate_pre = jnp.dot(normed_mid, full_gate, preferred_element_type=f32)
    up_pre = jnp.dot(normed_mid, full_up, preferred_element_type=f32)
    sigmoid_g = jax.nn.sigmoid(gate_pre)
    silu_gate = gate_pre * sigmoid_g
    activation = (silu_gate * up_pre).astype(b16)
    mlp_part = jnp.dot(activation, full_down, preferred_element_type=f32)
    layer_out = (
        after_attn + lax.psum(mlp_part.astype(jnp.bfloat16), "tp").astype(jnp.float32)
    ).astype(b16)
    back_rows = (
        lax.all_gather(q_weight, "seq", axis=0, tiled=True),
        lax.all_gather(key_matrix, "seq", axis=0, tiled=True),
        lax.all_gather(value_matrix, "seq", axis=0, tiled=True),
        lax.all_gather(gate_weight, "seq", axis=0, tiled=True),
        lax.all_gather(up_weight, "seq", axis=0, tiled=True),
        lax.all_gather(attn_gain, "seq", axis=0, tiled=True),
        lax.all_gather(mlp_gain, "seq", axis=0, tiled=True),
        lax.all_gather(query_gain, "seq", axis=0, tiled=True),
        lax.all_gather(key_gain, "seq", axis=0, tiled=True),
    )
    back_cols = (
        lax.all_gather(o_weight, "seq", axis=1, tiled=True),
        lax.all_gather(down_weight, "seq", axis=1, tiled=True),
    )
    full_q, full_k, full_v, full_gate, full_up = (
        back_rows[0],
        back_rows[1],
        back_rows[2],
        back_rows[3],
        back_rows[4],
    )
    full_o, full_down = back_cols
    grad_out = cotangent.astype(f32)
    grad_down = jnp.einsum("lf,ld->fd", activation, cotangent, preferred_element_type=f32)
    grad_act = jnp.einsum("ld,fd->lf", cotangent, full_down, preferred_element_type=f32)
    grad_gate = (grad_act * up_pre * sigmoid_g * (1.0 + gate_pre * (1.0 - sigmoid_g))).astype(b16)
    grad_up = (grad_act * silu_gate).astype(b16)
    grad_gate_w = jnp.einsum("ld,lf->df", normed_mid, grad_gate, preferred_element_type=f32)
    grad_up_w = jnp.einsum("ld,lf->df", normed_mid, grad_up, preferred_element_type=f32)
    mid_part = jnp.einsum(
        "lf,df->ld", grad_gate, full_gate, preferred_element_type=f32
    ) + jnp.einsum("lf,df->ld", grad_up, full_up, preferred_element_type=f32)
    grad_mid = lax.psum(mid_part.astype(jnp.bfloat16), "tp").astype(jnp.float32)
    grad_in_mid, mlp_gain_terms = norm_back(after_attn, gain_mlp, grad_mid)
    grad_after = grad_out + grad_in_mid
    mlp_gain_part = jnp.sum(
        lax.dynamic_slice_in_dim(mlp_gain_terms, share_start, share_rows), axis=0
    )
    grad_after_low = grad_after.astype(b16)
    grad_o_w = jnp.einsum("lh,ld->hd", attended_low, grad_after_low, preferred_element_type=f32)
    grad_att = jnp.einsum("ld,hd->lh", grad_after_low, full_o, preferred_element_type=f32).astype(
        b16
    )
    grad_att = grad_att.reshape(local_rows, kv_local, heads_per_group, HEAD_SIZE)
    delta = jnp.einsum("lkgd,lkgd->kgl", grad_att.astype(f32), attended)

    def grad_step(grad_query, inputs):
        keys_blk, values_blk, block_index = inputs
        probability = probs_of(keys_blk, block_index)
        grad_probs = jnp.einsum("lkgd,mkd->kglm", grad_att, values_blk, preferred_element_type=f32)
        grad_scores = (probability * (grad_probs - delta[..., None])).astype(b16)
        grad_query = grad_query + jnp.einsum(
            "kglm,mkd->lkgd", grad_scores, keys_blk, preferred_element_type=f32
        )
        grad_keys_blk = jnp.einsum(
            "kglm,lkgd->mkd", grad_scores, grouped_queries, preferred_element_type=f32
        )
        grad_values_blk = jnp.einsum(
            "kglm,lkgd->mkd", probability.astype(b16), grad_att, preferred_element_type=f32
        )
        return (grad_query, (grad_keys_blk * score_scale, grad_values_blk))

    grad_query, (grad_keys, grad_values) = lax.scan(
        grad_step,
        jnp.zeros((local_rows, kv_local, heads_per_group, HEAD_SIZE), f32),
        (keys_blocked, values_blocked, block_ids),
    )
    grad_query = grad_query.reshape(local_rows, q_local, HEAD_SIZE) * score_scale
    own_keys, own_values = (
        lax.psum_scatter(
            grad_keys.reshape(key_rows, kv_local, HEAD_SIZE).astype(jnp.bfloat16),
            "seq",
            scatter_dimension=0,
            tiled=True,
        ).astype(jnp.float32),
        lax.psum_scatter(
            grad_values.reshape(key_rows, kv_local, HEAD_SIZE).astype(jnp.bfloat16),
            "seq",
            scatter_dimension=0,
            tiled=True,
        ).astype(jnp.float32),
    )
    grad_v_low = own_values.astype(b16).reshape(local_rows, kv_local * HEAD_SIZE)
    grad_k_in, key_gain_terms = norm_back(
        key_projected, gain_key, rotate(own_keys, cosines, sine_values, -1.0)
    )
    grad_q_in, query_gain_terms = norm_back(
        q_proj, gain_query, rotate(grad_query, cosines, sine_values, -1.0)
    )
    grad_k_low = grad_k_in.astype(b16).reshape(local_rows, kv_local * HEAD_SIZE)
    grad_q_low = grad_q_in.astype(b16).reshape(local_rows, q_local * HEAD_SIZE)
    in_part = (
        jnp.einsum("lh,dh->ld", grad_q_low, full_q, preferred_element_type=f32)
        + jnp.einsum("lh,dh->ld", grad_k_low, full_k, preferred_element_type=f32)
        + jnp.einsum("lh,dh->ld", grad_v_low, full_v, preferred_element_type=f32)
    )
    grad_in, grad_mgain, grad_qgain, grad_kgain = (
        lax.psum(in_part.astype(jnp.bfloat16), "tp").astype(jnp.float32),
        lax.psum(mlp_gain_part.astype(jnp.bfloat16), "tp").astype(jnp.float32),
        lax.psum(jnp.sum(query_gain_terms, axis=(0, 1)).astype(jnp.bfloat16), "tp").astype(
            jnp.float32
        ),
        lax.psum(jnp.sum(key_gain_terms, axis=(0, 1)).astype(jnp.bfloat16), "tp").astype(
            jnp.float32
        ),
    )
    grad_in_tok, attn_gain_terms = norm_back(token_f, gain_attn, grad_in)
    grad_tokens = grad_after + grad_in_tok
    grad_q_w = jnp.einsum("ld,lh->dh", normalized_input, grad_q_low, preferred_element_type=f32)
    grad_k_w = jnp.einsum("ld,lh->dh", normalized_input, grad_k_low, preferred_element_type=f32)
    grad_v_w = jnp.einsum("ld,lh->dh", normalized_input, grad_v_low, preferred_element_type=f32)
    owned_rows = (
        lax.psum_scatter(
            grad_q_w.astype(jnp.bfloat16), "seq", scatter_dimension=0, tiled=True
        ).astype(jnp.float32),
        lax.psum_scatter(
            grad_k_w.astype(jnp.bfloat16), "seq", scatter_dimension=0, tiled=True
        ).astype(jnp.float32),
        lax.psum_scatter(
            grad_v_w.astype(jnp.bfloat16), "seq", scatter_dimension=0, tiled=True
        ).astype(jnp.float32),
        lax.psum_scatter(
            grad_gate_w.astype(jnp.bfloat16), "seq", scatter_dimension=0, tiled=True
        ).astype(jnp.float32),
        lax.psum_scatter(
            grad_up_w.astype(jnp.bfloat16), "seq", scatter_dimension=0, tiled=True
        ).astype(jnp.float32),
        lax.psum_scatter(
            jnp.sum(attn_gain_terms, axis=0).astype(jnp.bfloat16),
            "seq",
            scatter_dimension=0,
            tiled=True,
        ).astype(jnp.float32),
        lax.psum_scatter(
            grad_mgain.astype(jnp.bfloat16), "seq", scatter_dimension=0, tiled=True
        ).astype(jnp.float32),
        lax.psum_scatter(
            grad_qgain.astype(jnp.bfloat16), "seq", scatter_dimension=0, tiled=True
        ).astype(jnp.float32),
        lax.psum_scatter(
            grad_kgain.astype(jnp.bfloat16), "seq", scatter_dimension=0, tiled=True
        ).astype(jnp.float32),
    )
    owned_cols = (
        lax.psum_scatter(
            grad_o_w.astype(jnp.bfloat16), "seq", scatter_dimension=1, tiled=True
        ).astype(jnp.float32),
        lax.psum_scatter(
            grad_down.astype(jnp.bfloat16), "seq", scatter_dimension=1, tiled=True
        ).astype(jnp.float32),
    )
    return (
        layer_out,
        grad_tokens,
        owned_rows[0],
        owned_rows[1],
        owned_rows[2],
        owned_cols[0],
        owned_rows[3],
        owned_rows[4],
        owned_cols[1],
        owned_rows[5],
        owned_rows[6],
        owned_rows[7],
        owned_rows[8],
    )


def solution(mesh):
    placed = (
        P("seq", None),
        P("seq", "tp"),
        P("seq", "tp"),
        P("seq", "tp"),
        P("tp", "seq"),
        P("seq", "tp"),
        P("seq", "tp"),
        P("tp", "seq"),
        P("seq"),
        P("seq"),
        P("seq"),
        P("seq"),
        P("seq"),
        P(),
        P("seq", None),
    )
    return jax.shard_map(
        per_device,
        mesh=mesh,
        in_specs=placed,
        out_specs=(
            P("seq", None),
            P("seq", None),
            P("seq", "tp"),
            P("seq", "tp"),
            P("seq", "tp"),
            P("tp", "seq"),
            P("seq", "tp"),
            P("seq", "tp"),
            P("tp", "seq"),
            P("seq"),
            P("seq"),
            P("seq"),
            P("seq"),
        ),
        check_vma=False,
    )
```

profile of v0, /device:TPU:0, one launch (start us, length us, event | category | flops | bytes accessed | tf_op | source)
XLA Modules:
  0.0 1747.8 jit_solution(12738056615508282556)
XLA Ops:
  10.1 10.3 all-gather
  24.2 13.8 all-reduce.7
  66.8 24.6 %all-gather.20.cloned.1.call-done = bf16[2048,512]{1,0:T(8,128)(2,1)} async-done(((bf16[256,512]{1,0:T(8,128)(2,1)}), bf16[2048,512]{1,0:T(8,128)(2,1)}) %all-gather.20.cloned.1.call-update) | async-done | bytes 2097168 | tf_op jit(solution)/shard_map/all_gather | solution.py:72
  98.0 28.1 %all-gather.18.cloned.1.call-done = bf16[6144,2,128]{2,0,1:T(8,128)(2,1)} async-done(((bf16[768,2,128]{2,0,1:T(8,128)(2,1)}), bf16[6144,2,128]{2,0,1:T(8,128)(2,1)}) %all-gather.18.cloned.1.call-update) | async-done | bytes 3145744 | tf_op jit(solution)/shard_map/all_gather | solution.py:111
  130.0 137.9 %while.39 = (s32[]{:T(128)}, f32[2,2,768]{2,1,0:T(2,128)S(1)}, f32[2,2,768]{2,1,0:T(2,128)S(1)}, s32[12]{0:T(128)S(1)}, s32[6144]{0:T(1024)}, /*index=5*/s32[768...) while((s32[]{:T(128)}, f32[2,2,768]{2,1,0:T(2,128)S(1)}, ...), condition=%wide.region_6.7_spmd.clone, body=%wide.region_3.6_spmd.clone.sunk | while | flops 414859520 | bytes 14990554 | solution.py:150
  132.4 4.9 fusion.176
  143.9 4.9 fusion.176
  155.4 4.9 fusion.176
  166.9 4.9 fusion.176
  178.4 4.9 fusion.176
  189.9 4.9 fusion.176
  201.3 4.9 fusion.176
  212.8 4.9 fusion.176
  224.3 4.9 fusion.176
  235.8 4.9 fusion.176
  247.3 4.9 fusion.176
  258.8 4.9 fusion.176
  267.9 66.4 %while.40 = (s32[]{:T(128)}, f32[768,2,2,128]{0,3,2,1:T(8,128)S(1)}, bf16[12,512,2,128]{3,1,0,2:T(8,128)(2,1)}, s32[12]{0:T(128)S(1)}, s32[6144]{0:T(1024)}, /*i...) while((s32[]{:T(128)}, ...), condition=%wide.region_8.9_spmd.clone, body=%wide.region_7.8_spmd.clone.sunk | while | flops 813565184 | bytes 5276380 | solution.py:166
  334.5 5.4 convolution_convert_fusion.3
  342.0 9.3 all-gather.1
  351.3 110.4 %all-reduce.14.cloned.1.call-done = bf16[768,2048]{1,0:T(8,128)(2,1)} async-done(((bf16[768,2048]{1,0:T(8,128)(2,1)}), bf16[768,2048]{1,0:T(8,128)(2,1)}) %all-reduce.14.cloned.1.call-update) | async-done | bytes 3145744 | tf_op jit(solution)/shard_map/psum | solution.py:173
  466.4 5.8 multiply_convert_fusion
  472.2 36.0 %all-gather.24.cloned.1.call-done = bf16[2048,1536]{1,0:T(8,128)(2,1)} async-done(((bf16[256,1536]{1,0:T(8,128)(2,1)}), bf16[2048,1536]{1,0:T(8,128)(2,1)}) %all-gather.24.cloned.1.call-update) | async-done | bytes 6291472 | tf_op jit(solution)/shard_map/all_gather | solution.py:75
  508.2 9.5 fusion.105
  517.7 38.0 %all-gather.26.cloned.1.call-done = bf16[2048,1536]{1,0:T(8,128)(2,1)} async-done(((bf16[256,1536]{1,0:T(8,128)(2,1)}), bf16[2048,1536]{1,0:T(8,128)(2,1)}) %all-gather.26.cloned.1.call-update) | async-done | bytes 6291472 | tf_op jit(solution)/shard_map/all_gather | solution.py:76
  555.6 9.6 fusion.106
  565.2 38.8 %all-gather.28.cloned.1.call-done = bf16[1536,2048]{1,0:T(8,128)(2,1)} async-done(((bf16[1536,256]{1,0:T(8,128)(2,1)}), bf16[1536,2048]{1,0:T(8,128)(2,1)}) %all-gather.28.cloned.1.call-update) | async-done | bytes 6291472 | tf_op jit(solution)/shard_map/all_gather | solution.py:84
  604.1 12.8 multiply_convert_fusion.1
  616.9 8.9 fusion.107
  625.8 6.5 add_convert_fusion.1
  632.4 121.2 %all-reduce.16.cloned.1.call-done = bf16[768,2048]{1,0:T(8,128)(2,1)} async-done(((bf16[768,2048]{1,0:T(8,128)(2,1)}), bf16[768,2048]{1,0:T(8,128)(2,1)}) %all-reduce.16.cloned.1.call-update) | async-done | bytes 3145744 | tf_op jit(solution)/shard_map/psum | solution.py:217
  753.6 4.7 multiply_reduce_fusion
  767.4 248.1 %while.41 = (s32[]{:T(128)}, f32[768,2,2,128]{0,3,2,1:T(8,128)}, bf16[12,512,2,128]{3,1,0,2:T(8,128)(2,1)}, bf16[12,512,2,128]{3,1,0,2:T(8,128)(2,1)}, bf16[12,5...) while((s32[]{:T(128)}, f32[768,2,2,128]{0,3,2,1:T(8,128)}, ...), condition=%wide.region_15.16_spmd.clone, body=%wide.region_14.15_spmd.clone.sunk | while | flops 2031092992 | bytes 72277824 | solution.py:247
  774.5 5.2 fusion.195
  794.7 5.2 fusion.195
  815.4 5.2 fusion.195
  836.2 5.2 fusion.195
  849.7 4.7 fusion.194
  856.9 5.2 fusion.195
  870.5 4.7 fusion.194
  877.6 5.2 fusion.195
  898.3 5.2 fusion.195
  919.0 5.2 fusion.195
  939.8 5.2 fusion.195
  960.5 5.2 fusion.195
  981.2 5.2 fusion.195
  1001.9 5.2 fusion.195
  1024.5 6.6 convolution_convert_fusion.5
  1031.2 9.1 convolution_convert_fusion.2
  1040.4 9.2 convolution_convert_fusion.1
  1049.9 9.1 convolution_convert_fusion
  1074.4 36.5 %reduce-scatter.12.cloned.1.call-done = bf16[768,2,128]{2,0,1:T(8,128)(2,1)} async-done(((bf16[6144,2,128]{2,0,1:T(8,128)(2,1)}), bf16[768,2,128]{2,0,1:T(8,128)(2,1)}) %reduce-scatter.12.cloned.1.call-update) | async-done | bytes 393232 | tf_op jit(solution)/shard_map/reduce_scatter | solution.py:260
  1116.8 9.2 convolution_convert_fusion.4
  1137.4 17.9 %reduce-scatter.14.cloned.1.call-done = bf16[256,512]{1,0:T(8,128)(2,1)} async-done(((bf16[2048,512]{1,0:T(8,128)(2,1)}), bf16[256,512]{1,0:T(8,128)(2,1)}) %reduce-scatter.14.cloned.1.call-update) | async-done | bytes 262160 | tf_op jit(solution)/shard_map/reduce_scatter | solution.py:297
  1157.1 42.9 %reduce-scatter.20.cloned.1.call-done = bf16[512,256]{1,0:T(8,128)(2,1)} async-done(((bf16[512,2048]{1,0:T(8,128)(2,1)}), bf16[512,256]{1,0:T(8,128)(2,1)}) %reduce-scatter.20.cloned.1.call-update) | async-done | bytes 262160 | tf_op jit(solution)/shard_map/reduce_scatter | solution.py:329
  1201.9 63.2 %reduce-scatter.22.cloned.1.call-done = bf16[256,1536]{1,0:T(8,128)(2,1)} async-done(((bf16[2048,1536]{1,0:T(8,128)(2,1)}), bf16[256,1536]{1,0:T(8,128)(2,1)}) %reduce-scatter.22.cloned.1.call-update) | async-done | bytes 786448 | tf_op jit(solution)/shard_map/reduce_scatter | solution.py:306
  1267.5 62.9 %reduce-scatter.24.cloned.1.call-done = bf16[256,1536]{1,0:T(8,128)(2,1)} async-done(((bf16[2048,1536]{1,0:T(8,128)(2,1)}), bf16[256,1536]{1,0:T(8,128)(2,1)}) %reduce-scatter.24.cloned.1.call-update) | async-done | bytes 786448 | tf_op jit(solution)/shard_map/reduce_scatter | solution.py:309
  1332.9 62.5 %reduce-scatter.26.cloned.1.call-done = bf16[1536,256]{1,0:T(8,128)(2,1)} async-done(((bf16[1536,2048]{1,0:T(8,128)(2,1)}), bf16[1536,256]{1,0:T(8,128)(2,1)}) %reduce-scatter.26.cloned.1.call-update) | async-done | bytes 786448 | tf_op jit(solution)/shard_map/reduce_scatter | solution.py:332
  1397.9 37.2 %reduce-scatter.16.cloned.1.call-done = bf16[256,256]{1,0:T(8,128)(2,1)} async-done(((bf16[2048,256]{1,0:T(8,128)(2,1)}), bf16[256,256]{1,0:T(8,128)(2,1)}) %reduce-scatter.16.cloned.1.call-update) | async-done | bytes 131088 | tf_op jit(solution)/shard_map/reduce_scatter | solution.py:300
  1436.7 37.8 %reduce-scatter.18.cloned.1.call-done = bf16[256,256]{1,0:T(8,128)(2,1)} async-done(((bf16[2048,256]{1,0:T(8,128)(2,1)}), bf16[256,256]{1,0:T(8,128)(2,1)}) %reduce-scatter.18.cloned.1.call-update) | async-done | bytes 131088 | tf_op jit(solution)/shard_map/reduce_scatter | solution.py:303
  1476.1 224.7 %all-reduce.18.cloned.1.call-done = (bf16[768,2048]{1,0:T(8,128)(2,1)}, bf16[768,2048]{1,0:T(8,128)(2,1)}) async-done(((bf16[768,2048]{1,0:T(8,128)(2,1)}, bf16[768,2048]{1,0:T(8,128)(2,1)}), (bf16[768,2048]{1,0:T(8,128)(2,1)}, bf16[768,2048]{1,0:T(8,128)(2,1)})) %all-reduce.18.cloned.1.call-update) | async-done | bytes 6291472 | tf_op jit(solution)/shard_map/psum | solution.py:182
  1704.7 14.2 all-reduce.6
  1719.7 9.8 all-reduce.8
  1731.1 9.7 fusion.74
  (662 shorter events, 418.5 us)
Async XLA Ops:
  7.2 38.4 %copy-start.3 = (bf16[768,2048]{1,0:T(8,128)(2,1)S(1)}, bf16[768,2048]{1,0:T(8,128)(2,1)}, u32[]{:S(2)}) copy-start(bf16[768,2048]{1,0:T(8,128)(2,1)} %param.21) | copy-start | bytes 9437188
  7.2 38.4 %all-gather.16.cloned.1.call-start = ((), (), s32[]{:S(2)}) async-start(), calls=%async_computation.11 | async-start | bytes 1179648 | tf_op jit(solution)/shard_map/all_gather | solution.py:73
  7.9 53.7 %all-gather.12.cloned.1.call-start = ((), (), s32[]{:S(2)}) async-start(), calls=%async_computation.9 | async-start | bytes 1179648 | tf_op jit(solution)/shard_map/all_gather | solution.py:74
  8.7 82.8 %all-gather.20.cloned.1.call-start = ((), (), s32[]{:S(2)}) async-start(), calls=%async_computation.13 | async-start | bytes 2359296 | tf_op jit(solution)/shard_map/all_gather | solution.py:72
  9.4 116.7 %all-gather.18.cloned.1.call-start = ((), (), s32[]{:S(2)}) async-start(), calls=%async_computation.12 | async-start | bytes 3538944 | tf_op jit(solution)/shard_map/all_gather | solution.py:111
  20.5 71.0 %copy-start.34 = (f32[8,1,256]{2,1,0:T(1,128)}, f32[8,1,256]{2,1,0:T(1,128)S(1)}, u32[]{:S(2)}) copy-start(f32[8,1,256]{2,1,0:T(1,128)S(1)} %convert_element_type.243) | copy-start | bytes 24580
  42.8 11.8 copy-start.13
  45.5 45.9 %copy-start.36 = (f32[768]{0:T(1024)}, f32[768]{0:T(1024)S(1)}, u32[]{:S(2)}) copy-start(f32[768]{0:T(1024)S(1)} %add_rsqrt_fusion.3) | copy-start | bytes 9220
  45.6 7.6 copy-start.42
  57.0 9.0 copy-start.49
  57.0 210.9 %all-gather.14.cloned.1.call-start = ((), (), s32[]{:S(2)}) async-start(), calls=%async_computation.10 | async-start | bytes 3538944 | tf_op jit(solution)/shard_map/all_gather | solution.py:112
  65.1 269.4 %all-gather.22.cloned.1.call-start = ((), (), s32[]{:S(2)}) async-start(), calls=%async_computation.14 | async-start | bytes 2359296 | tf_op jit(solution)/shard_map/all_gather | solution.py:83
  65.7 396.1 %all-reduce.14.cloned.1.call-start = ((), (), s32[]{:S(2)}) async-start(), calls=%async_computation.15 | async-start | bytes 6291456 | tf_op jit(solution)/shard_map/psum | solution.py:173
  66.0 29.1 %copy-start.40 = (f32[128]{0:T(128)}, f32[128]{0:T(128)S(1)}, u32[]{:S(2)}) copy-start(f32[128]{0:T(128)S(1)} %convert_element_type.194) | copy-start | bytes 1540
  130.0 137.9 %copy-start.24 = (f32[768,2,2,128]{0,3,2,1:T(8,128)S(1)}, f32[768,2,2,128]{0,3,2,1:T(8,128)}, u32[]{:S(2)}) copy-start(f32[768,2,2,128]{0,3,2,1:T(8,128)} %custom-call.2) | copy-start | bytes 4718596
  334.4 5.4 copy-start.29
  339.8 168.3 %all-gather.24.cloned.1.call-start = ((), (), s32[]{:S(2)}) async-start(), calls=%async_computation.16 | async-start | bytes 7077888 | tf_op jit(solution)/shard_map/all_gather | solution.py:75
  340.6 215.0 %all-gather.26.cloned.1.call-start = ((), (), s32[]{:S(2)}) async-start(), calls=%async_computation.17 | async-start | bytes 7077888 | tf_op jit(solution)/shard_map/all_gather | solution.py:76
  341.3 262.7 %all-gather.28.cloned.1.call-start = ((), (), s32[]{:S(2)}) async-start(), calls=%async_computation.18 | async-start | bytes 7077888 | tf_op jit(solution)/shard_map/all_gather | solution.py:84
  341.9 411.6 %all-reduce.16.cloned.1.call-start = ((), (), s32[]{:S(2)}) async-start(), calls=%async_computation.19 | async-start | bytes 6291456 | tf_op jit(solution)/shard_map/psum | solution.py:217
  616.8 8.9 copy-start.51
  616.8 9.0 copy-start.50
  616.8 9.0 copy-start.44
  632.3 429.9 %reduce-scatter.10.cloned.1.call-start = ((), (), s32[]{:S(2)}) async-start(), calls=%async_computation.20 | async-start | bytes 3538944 | tf_op jit(solution)/shard_map/reduce_scatter | solution.py:254
  753.6 4.8 copy-start.8
  753.6 5.6 copy-start.19
  779.7 5.8 copy-start.2
  787.6 4.7 copy-start.47
  799.9 6.3 copy-start.2
  808.3 4.7 copy-start.47
  820.7 6.3 copy-start.2
  829.0 4.7 copy-start.47
  841.4 6.3 copy-start.2
  849.7 4.7 copy-start
  849.7 4.7 copy-start.47
  862.1 6.3 copy-start.2
  870.4 4.7 copy-start.47
  882.8 6.3 copy-start.2
  891.2 4.7 copy-start.47
  903.6 6.3 copy-start.2
  911.9 4.7 copy-start.47
  924.3 6.3 copy-start.2
  932.6 4.7 copy-start.47
  945.0 6.3 copy-start.2
  953.3 4.7 copy-start.47
  965.7 6.3 copy-start.2
  974.0 4.7 copy-start.47
  986.4 6.3 copy-start.2
  994.7 4.7 copy-start.47
  1007.1 6.3 copy-start.2
  1015.5 95.5 %reduce-scatter.12.cloned.1.call-start = ((), (), s32[]{:S(2)}) async-start(), calls=%async_computation.21 | async-start | bytes 3538944 | tf_op jit(solution)/shard_map/reduce_scatter | solution.py:260
  1016.2 139.1 %reduce-scatter.14.cloned.1.call-start = ((), (), s32[]{:S(2)}) async-start(), calls=%async_computation.22 | async-start | bytes 2359296 | tf_op jit(solution)/shard_map/reduce_scatter | solution.py:297
  1024.4 175.6 %reduce-scatter.20.cloned.1.call-start = ((), (), s32[]{:S(2)}) async-start(), calls=%async_computation.25 | async-start | bytes 2359296 | tf_op jit(solution)/shard_map/reduce_scatter | solution.py:329
  1031.1 234.0 %reduce-scatter.22.cloned.1.call-start = ((), (), s32[]{:S(2)}) async-start(), calls=%async_computation.26 | async-start | bytes 7077888 | tf_op jit(solution)/shard_map/reduce_scatter | solution.py:306
  1040.3 290.2 %reduce-scatter.24.cloned.1.call-start = ((), (), s32[]{:S(2)}) async-start(), calls=%async_computation.27 | async-start | bytes 7077888 | tf_op jit(solution)/shard_map/reduce_scatter | solution.py:309
  1049.6 345.8 %reduce-scatter.26.cloned.1.call-start = ((), (), s32[]{:S(2)}) async-start(), calls=%async_computation.28 | async-start | bytes 7077888 | tf_op jit(solution)/shard_map/reduce_scatter | solution.py:332
  1059.1 5.6 copy-start.33
  1059.1 375.9 %reduce-scatter.16.cloned.1.call-start = ((), (), s32[]{:S(2)}) async-start(), calls=%async_computation.23 | async-start | bytes 1179648 | tf_op jit(solution)/shard_map/reduce_scatter | solution.py:300
  1071.3 41.6 %copy-start.38 = (f32[768]{0:T(1024)S(1)}, f32[768]{0:T(1024)}, u32[]{:S(2)}) copy-start(f32[768]{0:T(1024)} %copy-done.36) | copy-start | bytes 9220
  1074.4 400.1 %reduce-scatter.18.cloned.1.call-start = ((), (), s32[]{:S(2)}) async-start(), calls=%async_computation.24 | async-start | bytes 1179648 | tf_op jit(solution)/shard_map/reduce_scatter | solution.py:303
  1116.2 584.6 %all-reduce.18.cloned.1.call-start = ((), (), s32[]{:S(2)}) async-start(), calls=%async_computation.29 | async-start | bytes 12582912 | tf_op jit(solution)/shard_map/psum | solution.py:182
  1116.7 9.2 copy-start.16
  1116.7 9.2 copy-start.20
  1135.8 66.0 %copy-start.43 = (f32[256]{0:T(256)S(1)}, f32[256]{0:T(256)}, u32[]{:S(2)}) copy-start(f32[256]{0:T(256)} %get-tuple-element.595) | copy-start | bytes 3076
  (75 other events, 193.9 us)
Sparse Core Ops, SparseCore 0:
  9.9 26.2 all-gather.15
  38.1 23.4 all-gather.11
  63.5 27.8 all-gather.19
  93.8 32.3 all-gather.17
  128.5 32.3 all-gather.13
  162.5 28.1 all-gather.21
  340.0 121.7 all-reduce.13
  463.6 44.5 all-gather.23
  510.1 45.5 all-gather.25
  557.4 46.6 all-gather.27
  632.4 121.0 all-reduce.15
  1015.6 45.2 reduce-scatter.9
  1064.7 46.2 reduce-scatter.11
  1114.1 41.1 reduce-scatter.13
  1158.8 41.2 reduce-scatter.19
  1203.3 61.7 reduce-scatter.21
  1268.7 61.7 reduce-scatter.23
  1333.7 61.7 reduce-scatter.25
  1399.0 36.0 reduce-scatter.15
  1438.4 36.0 reduce-scatter.17
  1477.6 223.1 all-reduce.17
where the time goes:
time: 1760 us; the launch traced here: 1750 us
  waiting for transfers between devices  993 us (56%)
  matrix products  438 us (25%)
  other arithmetic  137 us (8%)
  local copies, waits for them, and re-layouts  78.1 us (4%)
  blocking collectives  57.4 us (3%)
  loops' own time  25.3 us (1%)
    psum x1, waiting for transfers between devices, per_device(): lax.psum(mlp_part.astype(jnp.bfloat16), 'tp').astype(jnp.float32)  225 us
    psum x1, waiting for transfers between devices, per_device(): grad_mid = lax.psum(mid_part.astype(jnp.bfloat16), 'tp').astype(jnp.float32)  121 us
    dot_general x24, matrix products, block_scores(): jnp.einsum('lkgd,mkd->kglm', grouped_queries, keys_blk, preferred_element...  115 us
    psum x1, waiting for transfers between devices, per_device(): lax.psum(attn_part.astype(jnp.bfloat16), 'tp').astype(jnp.float32)  110 us
    reduce_scatter x1, waiting for transfers between devices, per_device(): lax.psum_scatter(grad_gate_w.astype(jnp.bfloat16), 'seq', scatter_dimensi...  63.2 us
    reduce_scatter x1, waiting for transfers between devices, per_device(): lax.psum_scatter(grad_up_w.astype(jnp.bfloat16), 'seq', scatter_dimension...  62.9 us
    dot_general x12, matrix products, grad_step(): jnp.einsum('lkgd,mkd->kglm', grad_att, values_blk, preferred_element_type...  62.7 us
    reduce_scatter x1, waiting for transfers between devices, per_device(): lax.psum_scatter(grad_down.astype(jnp.bfloat16), 'seq', scatter_dimension...  62.5 us
  transfers between devices with their start and end apart: 21, of which 17 were waited for; matrix products, arithmetic and copies ran while one was open for 20% of the time, Pallas kernels for 0%

commit v1 on v0

--- a/solution.py
+++ b/solution.py
@@ -1,11 +1,175 @@
+import functools
 import math
 
 import jax
 import jax.numpy as jnp
 from jax import lax
+from jax.experimental import pallas as pl
+from jax.experimental.pallas import tpu as pltpu
+
 from jax.sharding import PartitionSpec as P
 
 HEAD_SIZE = 128
+LOG2E = 1.4426950408889634
+VMEM_BYTES = 60 << 20
+NT = (((1,), (1,)), ((), ()))
+TN = (((0,), (0,)), ((), ()))
+
+
+def mm(a, b, dims=(((1,), (0,)), ((), ()))):
+    return lax.dot_general(a, b, dims, preferred_element_type=jnp.float32)
+
+
+def cut(rows, most=256):
+    return math.gcd(rows, most)
+
+
+def attn_fwd_block(q_ref, k_ref, v_ref, out_ref, sum_ref, bias_ref, kv, rows, tile):
+    scale = HEAD_SIZE ** -0.5 * LOG2E
+    all_rows = q_ref.shape[1]
+    for h in range(kv):
+        cols = slice(h * HEAD_SIZE, (h + 1) * HEAD_SIZE)
+        for start in range(0, all_rows, tile):
+            at = start % rows
+            n_keys = rows if bias_ref is None else at + tile
+            scores = mm(q_ref[h, start:start + tile], k_ref[:n_keys, cols], NT) * scale
+            if bias_ref is not None:
+                scores = scores + bias_ref[at:at + tile, :n_keys]
+            weights = jnp.exp2(scores)
+            part = weights[:, :HEAD_SIZE]
+            for c in range(HEAD_SIZE, n_keys, HEAD_SIZE):
+                part = part + weights[:, c:c + HEAD_SIZE]
+            sum_ref[h, start:start + tile] += part
+            out_ref[h, start:start + tile] += mm(weights.astype(jnp.bfloat16), v_ref[:n_keys, cols])
+
+
+def fill_bias(bias_ref, q_docs, k_docs):
+    rows, keys = bias_ref.shape
+    visible = (lax.broadcasted_iota(jnp.int32, (rows, keys), 1)
+               <= lax.broadcasted_iota(jnp.int32, (rows, keys), 0)) & (q_docs == k_docs)
+    bias_ref[...] = jnp.where(visible, 0.0, -1e30)
+
+
+def fwd_kernel(q_ref, k_ref, v_ref, qd_ref, kd_ref, out_ref, lse_ref, acc, total, bias):
+    kv, all_rows, _ = q_ref.shape
+    rows = k_ref.shape[1]
+    me = lax.axis_index("seq")
+    tile = cut(rows)
+    acc[...] = jnp.zeros_like(acc)
+    total[...] = jnp.zeros_like(total)
+    fill_bias(bias, qd_ref[...], kd_ref[...])
+
+    @pl.loop(0, me)
+    def _(j):
+        attn_fwd_block(q_ref, k_ref.at[j], v_ref.at[j], acc, total, None, kv, rows, tile)
+
+    first = jnp.where(qd_ref[...] == 0, 1.0, 0.0)
+    for h in range(kv):
+        for start in range(0, all_rows, rows):
+            acc[h, start:start + rows] *= first
+            total[h, start:start + rows] *= first
+    attn_fwd_block(q_ref, k_ref.at[me], v_ref.at[me], acc, total, bias, kv, rows, tile)
+    for h in range(kv):
+        for start in range(0, all_rows, tile):
+            t = total[h, start:start + tile]
+            s = jnp.sum(t, axis=1, keepdims=True)
+            out_ref[h, start:start + tile] = acc[h, start:start + tile] / s
+            lse_ref[h, :, start:start + tile] = jnp.log2(jnp.sum(t.T, axis=0, keepdims=True))
+
+
+def attention_forward(q, k, v, q_docs, k_docs):
+    kv, all_rows, _ = q.shape
+    n, rows, _ = k.shape
+    vm = pl.BlockSpec(memory_space=pltpu.VMEM)
+    return pl.pallas_call(
+        fwd_kernel,
+        out_shape=(jax.ShapeDtypeStruct(q.shape, jnp.float32),
+                   jax.ShapeDtypeStruct((kv, 1, all_rows), jnp.float32)),
+        in_specs=[vm] * 5, out_specs=(vm, vm),
+        scratch_shapes=[pltpu.VMEM(q.shape, jnp.float32), pltpu.VMEM(q.shape, jnp.float32),
+                        pltpu.VMEM((rows, rows), jnp.float32)],
+        compiler_params=pltpu.CompilerParams(vmem_limit_bytes=VMEM_BYTES),
+        name="attn_fwd",
+    )(q, k, v, q_docs, k_docs)
+
+
+def attn_bwd_block(q_ref, do_ref, lse_ref, delta_ref, k_ref, v_ref, dq_ref, dk_ref, dv_ref, bias_ref, kv, rows, tile):
+    scale = HEAD_SIZE ** -0.5 * LOG2E
+    all_rows = q_ref.shape[1]
+    for h in range(kv):
+        cols = slice(h * HEAD_SIZE, (h + 1) * HEAD_SIZE)
+        dk_ref[:, cols] = jnp.zeros((rows, HEAD_SIZE), jnp.float32)
+        dv_ref[:, cols] = jnp.zeros((rows, HEAD_SIZE), jnp.float32)
+        for start in range(0, all_rows, tile):
+            at = start % rows
+            n_keys = rows if bias_ref is None else at + tile
+            q = q_ref[h, start:start + tile]
+            do = do_ref[h, start:start + tile]
+            k = k_ref[:n_keys, cols]
+            scores = mm(k, q, NT) * scale - lse_ref[h, :, start:start + tile]
+            if bias_ref is not None:
+                scores = scores + bias_ref[:n_keys, at:at + tile]
+            probs = jnp.exp2(scores)
+            grad = mm(v_ref[:n_keys, cols], do, NT)
+            grad = (probs * (grad - delta_ref[h, :, start:start + tile])).astype(jnp.bfloat16)
+            dv_ref[:n_keys, cols] += mm(probs.astype(jnp.bfloat16), do)
+            dk_ref[:n_keys, cols] += mm(grad, q)
+            dq_ref[h, start:start + tile] += mm(grad, k, TN)
+
+
+def bwd_kernel(q_ref, do_ref, o_ref, lse_ref, k_ref, v_ref, kd_ref, qdr_ref, dq_ref, dk_ref, dv_ref,
+               delta, lse_off, dk, dv, bias):
+    kv, all_rows, _ = q_ref.shape
+    n, rows, _ = k_ref.shape
+    me = lax.axis_index("seq")
+    tile = cut(rows)
+    visible = (lax.broadcasted_iota(jnp.int32, (rows, rows), 0)
+               <= lax.broadcasted_iota(jnp.int32, (rows, rows), 1)) & (kd_ref[...] == qdr_ref[...])
+    bias[...] = jnp.where(visible, 0.0, -1e30)
+    dq_ref[...] = jnp.zeros_like(dq_ref)
+    off = jnp.where(qdr_ref[...] == 0, 0.0, 1e30)
+    for h in range(kv):
+        for start in range(0, all_rows, rows):
+            at = slice(start, start + rows)
+            prod = do_ref[h, at].astype(jnp.float32) * o_ref[h, at]
+            delta[h, :, at] = jnp.sum(prod.T, axis=0, keepdims=True)
+            lse_off[h, :, at] = lse_ref[h, :, at] + off
+    scale = HEAD_SIZE ** -0.5
+
+    @pl.loop(0, me)
+    def _(j):
+        attn_bwd_block(q_ref, do_ref, lse_off, delta, k_ref.at[j], v_ref.at[j], dq_ref, dk, dv, None, kv, rows, tile)
+        dk_ref[j] = (dk[...] * scale).astype(jnp.bfloat16)
+        dv_ref[j] = dv[...].astype(jnp.bfloat16)
+
+    attn_bwd_block(q_ref, do_ref, lse_ref, delta, k_ref.at[me], v_ref.at[me], dq_ref, dk, dv, bias, kv, rows, tile)
+    dk_ref[me] = (dk[...] * scale).astype(jnp.bfloat16)
+    dv_ref[me] = dv[...].astype(jnp.bfloat16)
+
+    @pl.loop(me + 1, n)
+    def _(j):
+        dk_ref[j] = jnp.zeros(dk_ref.shape[1:], jnp.bfloat16)
+        dv_ref[j] = jnp.zeros(dv_ref.shape[1:], jnp.bfloat16)
+
+    dq_ref[...] *= scale
+
+
+def attention_backward(q, do, o, lse, k, v, q_docs, k_docs):
+    kv, all_rows, _ = q.shape
+    n, rows, width = k.shape
+    vm = pl.BlockSpec(memory_space=pltpu.VMEM)
+    return pl.pallas_call(
+        bwd_kernel,
+        out_shape=(jax.ShapeDtypeStruct(q.shape, jnp.float32),
+                   jax.ShapeDtypeStruct(k.shape, jnp.bfloat16),
+                   jax.ShapeDtypeStruct(k.shape, jnp.bfloat16)),
+        in_specs=[vm] * 8, out_specs=(vm, vm, vm),
+        scratch_shapes=[pltpu.VMEM((kv, 1, all_rows), jnp.float32), pltpu.VMEM((kv, 1, all_rows), jnp.float32),
+                        pltpu.VMEM((rows, width), jnp.float32), pltpu.VMEM((rows, width), jnp.float32),
+                        pltpu.VMEM((rows, rows), jnp.float32)],
+        compiler_params=pltpu.CompilerParams(vmem_limit_bytes=VMEM_BYTES),
+        name="attn_bwd",
+    )(q, do, o, lse, k, v, q_docs, k_docs)
 
 
 EPS = 1e-06
@@ -65,7 +229,6 @@
     q_local = q_weight.shape[1] // HEAD_SIZE
     kv_local = key_matrix.shape[1] // HEAD_SIZE
     heads_per_group = q_local // kv_local
-    score_scale = HEAD_SIZE ** (-0.5)
     share_rows = local_rows // lax.axis_size("tp")
     share_start = lax.axis_index("tp") * share_rows
     row_parts = (
@@ -112,63 +275,24 @@
         lax.all_gather(v_local, "seq", axis=0, tiled=True),
     )
     row_offset = lax.axis_index("seq") * local_rows
-    key_rows = all_keys.shape[0]
-    key_block = math.gcd(key_rows, 512)
-    block_count = key_rows // key_block
-    q_docs = lax.dynamic_slice_in_dim(seq_ids, row_offset, local_rows)
-    q_places = row_offset + jnp.arange(local_rows, dtype=jnp.int32)
-    grouped_queries = q_final.reshape(local_rows, kv_local, heads_per_group, HEAD_SIZE)
-    block_ids = jnp.arange(block_count, dtype=jnp.int32)
-
-    def block_scores(keys_blk, block_index):
-        offset = block_index * key_block
-        k_places = offset + jnp.arange(key_block, dtype=jnp.int32)
-        k_docs = lax.dynamic_slice_in_dim(seq_ids, offset, key_block)
-        allowed = (k_places[None, :] <= q_places[:, None]) & (k_docs[None, :] == q_docs[:, None])
-        scores = (
-            jnp.einsum("lkgd,mkd->kglm", grouped_queries, keys_blk, preferred_element_type=f32)
-            * score_scale
-        )
-        return (scores, allowed[None, None])
-
-    keys_blocked = all_keys.reshape(block_count, key_block, kv_local, HEAD_SIZE)
-    values_blocked = all_values.reshape(block_count, key_block, kv_local, HEAD_SIZE)
-
-    def stat_step(state_pair, inputs):
-        row_max, row_sum = state_pair
-        keys_blk, block_index = inputs
-        scores, allowed = block_scores(keys_blk, block_index)
-        new_max = jnp.maximum(row_max, jnp.max(jnp.where(allowed, scores, -1e30), axis=-1))
-        weights = jnp.where(allowed, jnp.exp(scores - new_max[..., None]), 0.0)
-        row_sum = row_sum * jnp.exp(row_max - new_max) + jnp.sum(weights, axis=-1)
-        return ((new_max, row_sum), None)
-
-    start_state = (
-        jnp.full((kv_local, heads_per_group, local_rows), -1e30, f32),
-        jnp.zeros((kv_local, heads_per_group, local_rows), f32),
-    )
-    (row_max, row_sum), _ = lax.scan(stat_step, start_state, (keys_blocked, block_ids))
-    log_total = row_max + jnp.log(row_sum)
-
-    def probs_of(keys_blk, block_index):
-        scores, allowed = block_scores(keys_blk, block_index)
-        return jnp.where(allowed, jnp.exp(scores - log_total[..., None]), 0.0)
-
-    def mix_step(running, inputs):
-        keys_blk, values_blk, block_index = inputs
-        probability = probs_of(keys_blk, block_index).astype(b16)
-        return (
-            running
-            + jnp.einsum("kglm,mkd->lkgd", probability, values_blk, preferred_element_type=f32),
-            None,
-        )
-
-    attended, _ = lax.scan(
-        mix_step,
-        jnp.zeros((local_rows, kv_local, heads_per_group, HEAD_SIZE), f32),
-        (keys_blocked, values_blocked, block_ids),
-    )
-    attended_low = attended.reshape(local_rows, q_local * HEAD_SIZE).astype(b16)
+    seq_count = lax.axis_size("seq")
+    own_docs = lax.dynamic_slice_in_dim(seq_ids, row_offset, local_rows)
+    doc_column, doc_row = own_docs[:, None], own_docs[None, :]
+
+    def by_head(flat):
+        heads = flat.reshape(local_rows, kv_local, heads_per_group, HEAD_SIZE)
+        return heads.transpose(1, 2, 0, 3).reshape(kv_local, heads_per_group * local_rows, HEAD_SIZE)
+
+    def by_row(heads):
+        split = heads.reshape(kv_local, heads_per_group, local_rows, HEAD_SIZE)
+        return split.transpose(2, 0, 1, 3).reshape(local_rows, q_local * HEAD_SIZE)
+
+    queries_h = by_head(q_final)
+    keys_b = all_keys.reshape(seq_count, local_rows, kv_local * HEAD_SIZE)
+    values_b = all_values.reshape(seq_count, local_rows, kv_local * HEAD_SIZE)
+    attended_h, lse = attention_forward(queries_h, keys_b, values_b, doc_column, doc_row)
+    attended = by_row(attended_h)
+    attended_low = attended.astype(b16)
     attn_part = jnp.dot(attended_low, full_o, preferred_element_type=f32)
     after_attn = token_f + lax.psum(attn_part.astype(jnp.bfloat16), "tp").astype(jnp.float32)
     normed_mid = norm_rows(after_attn, gain_mlp).astype(b16)
@@ -225,31 +349,11 @@
     grad_att = jnp.einsum("ld,hd->lh", grad_after_low, full_o, preferred_element_type=f32).astype(
         b16
     )
-    grad_att = grad_att.reshape(local_rows, kv_local, heads_per_group, HEAD_SIZE)
-    delta = jnp.einsum("lkgd,lkgd->kgl", grad_att.astype(f32), attended)
-
-    def grad_step(grad_query, inputs):
-        keys_blk, values_blk, block_index = inputs
-        probability = probs_of(keys_blk, block_index)
-        grad_probs = jnp.einsum("lkgd,mkd->kglm", grad_att, values_blk, preferred_element_type=f32)
-        grad_scores = (probability * (grad_probs - delta[..., None])).astype(b16)
-        grad_query = grad_query + jnp.einsum(
-            "kglm,mkd->lkgd", grad_scores, keys_blk, preferred_element_type=f32
-        )
-        grad_keys_blk = jnp.einsum(
-            "kglm,lkgd->mkd", grad_scores, grouped_queries, preferred_element_type=f32
-        )
-        grad_values_blk = jnp.einsum(
-            "kglm,lkgd->mkd", probability.astype(b16), grad_att, preferred_element_type=f32
-        )
-        return (grad_query, (grad_keys_blk * score_scale, grad_values_blk))
-
-    grad_query, (grad_keys, grad_values) = lax.scan(
-        grad_step,
-        jnp.zeros((local_rows, kv_local, heads_per_group, HEAD_SIZE), f32),
-        (keys_blocked, values_blocked, block_ids),
-    )
-    grad_query = grad_query.reshape(local_rows, q_local, HEAD_SIZE) * score_scale
+    grad_query_h, grad_keys, grad_values = attention_backward(
+        queries_h, by_head(grad_att), attended_h, lse, keys_b, values_b, doc_column, doc_row
+    )
+    grad_query = by_row(grad_query_h).reshape(local_rows, q_local, HEAD_SIZE)
+    key_rows = seq_count * local_rows
     own_keys, own_values = (
         lax.psum_scatter(
             grad_keys.reshape(key_rows, kv_local, HEAD_SIZE).astype(jnp.bfloat16),

time: 1760 us -> 1450 us (0.82)
  matrix products: 438 us -> 125 us
  waiting for transfers between devices: 993 us -> 1060 us
  other arithmetic: 137 us -> 87.4 us
  loops' own time: 25.3 us -> 0 us
  Pallas kernels: 0 us -> 20.9 us
    dot_general x84 -> x0, matrix products: 314 us -> none  [the longest x24 115 us: block_scores(): jnp.einsum('lkgd,mkd->kglm', grouped_queries, keys_blk, preferred_element...]
    unnamed x21, waiting for transfers between devices: 5.38 us -> 123 us
    reduce_sum x12 -> x0, other arithmetic: 49.7 us -> none  [stat_step(): row_sum = row_sum * jnp.exp(row_max - new_max) + jnp.sum(weights, axis=-1)]
    dynamic_slice x73 -> x1, local copies, waits for them, and re-layouts: 49.5 us -> 0.78 us  [per_device(): own_docs = lax.dynamic_slice_in_dim(seq_ids, row_offset, local_rows)]
    reduce_scatter x2 -> x0, waiting for transfers between devices: 36.5 us -> none  [the longest x1 36.5 us: per_device(): lax.psum_scatter(grad_values.reshape(key_rows, kv_local, HEAD_SIZE).astyp...]
    all_gather x1, waiting for transfers between devices: 0.02 us -> 28.7 us  [per_device(): lax.all_gather(v_local, 'seq', axis=0, tiled=True)]
    reduce_scatter x1, waiting for transfers between devices: 42.9 us -> 16.9 us  [per_device(): lax.psum_scatter(grad_o_w.astype(jnp.bfloat16), 'seq', scatter_dimension=...]
    reshape x0 -> x5, local copies, waits for them, and re-layouts: none -> 25.4 us  [the longest x1 6.03 us: per_device(): values_b = all_values.reshape(seq_count, local_rows, kv_local * HEAD_SIZE)]
  transfers between devices with their start and end apart: 21 -> 20, of which waited for: 17 -> 18; matrix products, arithmetic and copies ran while one was open for 20% -> 14% of each run, Pallas kernels for 0% -> 1%
where the time goes in v1:
time: 1450 us; the launch traced here: 1440 us
  waiting for transfers between devices  1060 us (73%)
  matrix products  125 us (9%)
  other arithmetic  87.4 us (6%)
  local copies, waits for them, and re-layouts  65.7 us (5%)
  blocking collectives  64.7 us (4%)
  Pallas kernels  20.9 us (1%)
  between operations  17.7 us (1%)
    psum x1, waiting for transfers between devices, per_device(): lax.psum(mlp_part.astype(jnp.bfloat16), 'tp').astype(jnp.float32)  224 us
    unnamed x21, waiting for transfers between devices  123 us
    psum x1, waiting for transfers between devices, per_device(): grad_mid = lax.psum(mid_part.astype(jnp.bfloat16), 'tp').astype(jnp.float32)  121 us
    psum x1, waiting for transfers between devices, per_device(): lax.psum(attn_part.astype(jnp.bfloat16), 'tp').astype(jnp.float32)  110 us
    reduce_scatter x1, waiting for transfers between devices, per_device(): lax.psum_scatter(grad_gate_w.astype(jnp.bfloat16), 'seq', scatter_dimensi...  63.7 us
    reduce_scatter x1, waiting for transfers between devices, per_device(): lax.psum_scatter(grad_down.astype(jnp.bfloat16), 'seq', scatter_dimension...  63.1 us
    reduce_scatter x1, waiting for transfers between devices, per_device(): lax.psum_scatter(grad_up_w.astype(jnp.bfloat16), 'seq', scatter_dimension...  62.6 us
    all_gather x1, waiting for transfers between devices, per_device(): lax.all_gather(down_weight, 'seq', axis=1, tiled=True)  38.8 us
  transfers between devices with their start and end apart: 20, of which 18 were waited for; matrix products, arithmetic and copies ran while one was open for 14% of the time, Pallas kernels for 1%

profile of v1, /device:TPU:0, one launch (start us, length us, event | category | flops | bytes accessed | tf_op | source)
XLA Modules:
  0.0 1443.6 jit_solution(11837692100471348782)
XLA Ops:
  10.1 10.3 all-gather
  24.9 13.8 all-reduce.9
  42.5 2.6 fusion.10
  45.1 4.0 multiply_reduce_fusion.5
  58.4 3.3 all-gather.18.cloned.1.call-done
  61.7 3.2 convolution_convert_fusion.9
  70.6 20.9 %all-gather.12.cloned.1.call-done = bf16[2048,512]{1,0:T(8,128)(2,1)} async-done(((bf16[256,512]{1,0:T(8,128)(2,1)}), bf16[2048,512]{1,0:T(8,128)(2,1)}) %all-gather.12.cloned.1.call-update) | async-done | bytes 2097168 | tf_op jit(solution)/shard_map/all_gather | solution.py:235
  91.5 3.6 multiply_reduce_fusion.3
  102.0 2.7 pad_maximum_fusion.1
  104.7 21.4 %all-gather.16.cloned.1.call-done = bf16[6144,2,128]{2,1,0:T(2,128)(2,1)} async-done(((bf16[768,2,128]{2,1,0:T(2,128)(2,1)}), bf16[6144,2,128]{2,1,0:T(2,128)(2,1)}) %all-gather.16.cloned.1.call-update) | async-done | bytes 3145744 | tf_op jit(solution)/shard_map/all_gather | solution.py:274
  126.2 6.0 reshape.216.k_ref
  132.1 28.7 %all-gather.20.cloned.1.call-done = bf16[6144,2,128]{2,1,0:T(2,128)(2,1)} async-done(((bf16[768,2,128]{2,1,0:T(2,128)(2,1)}), bf16[6144,2,128]{2,1,0:T(2,128)(2,1)}) %all-gather.20.cloned.1.call-update) | async-done | bytes 3145744 | tf_op jit(solution)/shard_map/all_gather | solution.py:275
  160.8 6.0 reshape.218.v_ref
  166.8 7.7 attn_fwd.1
  179.2 11.5 all-gather.22.cloned.1.call-done
  190.8 5.3 convolution_convert_fusion.3
  198.9 16.7 %all-gather.1 = bf16[8,1,256]{2,1,0:T(2,128)(2,1)S(1)} all-gather(bf16[1,1,256]{2,1,0:T(2,128)(2,1)S(1)} %reshape.233), channel_id=1, replica_groups=mesh['seq'=8,'tp'=4] {'seq'}, dimensions={0}, use_global_device_ids=true | all-gather | bytes 4608 | tf_op jit(solution)/shard_map/all_gather | solution.py:241
  216.2 110.1 %all-reduce.18.cloned.1.call-done = bf16[768,2048]{1,0:T(8,128)(2,1)} async-done(((bf16[768,2048]{1,0:T(8,128)(2,1)}), bf16[768,2048]{1,0:T(8,128)(2,1)}) %all-reduce.18.cloned.1.call-update) | async-done | bytes 3145744 | tf_op jit(solution)/shard_map/psum | solution.py:297
  326.3 3.1 multiply_reduce_fusion.1
  330.1 5.6 multiply_convert_fusion
  335.7 37.1 %all-gather.24.cloned.1.call-done = bf16[2048,1536]{1,0:T(8,128)(2,1)} async-done(((bf16[256,1536]{1,0:T(8,128)(2,1)}), bf16[2048,1536]{1,0:T(8,128)(2,1)}) %all-gather.24.cloned.1.call-update) | async-done | bytes 6291472 | tf_op jit(solution)/shard_map/all_gather | solution.py:238
  372.8 10.0 fusion.41
  382.8 37.4 %all-gather.26.cloned.1.call-done = bf16[2048,1536]{1,0:T(8,128)(2,1)} async-done(((bf16[256,1536]{1,0:T(8,128)(2,1)}), bf16[2048,1536]{1,0:T(8,128)(2,1)}) %all-gather.26.cloned.1.call-update) | async-done | bytes 6291472 | tf_op jit(solution)/shard_map/all_gather | solution.py:239
  420.2 9.6 fusion.42
  429.8 38.8 %all-gather.28.cloned.1.call-done = bf16[1536,2048]{1,0:T(8,128)(2,1)} async-done(((bf16[1536,256]{1,0:T(8,128)(2,1)}), bf16[1536,2048]{1,0:T(8,128)(2,1)}) %all-gather.28.cloned.1.call-update) | async-done | bytes 6291472 | tf_op jit(solution)/shard_map/all_gather | solution.py:247
  468.6 12.8 multiply_convert_fusion.1
  481.4 8.9 fusion.43
  490.4 6.5 add_convert_fusion.1
  496.9 121.2 %all-reduce.20.cloned.1.call-done = bf16[768,2048]{1,0:T(8,128)(2,1)} async-done(((bf16[768,2048]{1,0:T(8,128)(2,1)}), bf16[768,2048]{1,0:T(8,128)(2,1)}) %all-reduce.20.cloned.1.call-update) | async-done | bytes 3145744 | tf_op jit(solution)/shard_map/psum | solution.py:341
  618.1 4.8 multiply_reduce_fusion
  623.7 4.5 multiply_add_fusion
  628.2 2.9 fusion.20
  633.5 13.2 attn_bwd.1
  646.7 5.5 reshape.222
  652.2 5.5 reshape.223
  659.1 4.2 fusion.39
  663.3 2.7 copy.125
  666.0 2.7 copy.124
  673.3 3.5 convolution_convert_fusion.6
  676.8 6.2 convolution_convert_fusion.5
  686.5 118.7 %all-reduce.22.cloned.1.call-done = (bf16[6144,2,128]{2,1,0:T(2,128)(2,1)}, bf16[6144,2,128]{2,1,0:T(2,128)(2,1)}) async-done(((bf16[6144,2,128]{2,1,0:T(2,128)(2,1)}, bf16[6144,2,128]{2,1,0:T(2,128)(2,1)}), (bf16[6144,2,128]{2,1,0:T(2,128)(2,1)}, bf16[6144,2,128]{2,1,0:T(2,128)(2,1)})) %all-reduce.22.cloned.1.call-update) | async-done | bytes 6291472
  805.2 2.5 dynamic-slice_convert_fusion
  809.7 5.2 multiply_reduce_fusion.4
  820.5 3.0 convolution_convert_fusion.8
  823.6 3.3 convolution_convert_fusion.7
  827.0 9.2 convolution_convert_fusion.2
  836.2 9.2 convolution_convert_fusion.1
  845.7 9.2 convolution_convert_fusion
  855.0 9.1 convolution_convert_fusion.4
  867.4 2.7 add_convert_fusion
  871.4 2.7 convert_element_type.195
  877.6 16.9 %reduce-scatter.14.cloned.1.call-done = bf16[512,256]{1,0:T(8,128)(2,1)} async-done(((bf16[512,2048]{1,0:T(8,128)(2,1)}), bf16[512,256]{1,0:T(8,128)(2,1)}) %reduce-scatter.14.cloned.1.call-update) | async-done | bytes 262160 | tf_op jit(solution)/shard_map/reduce_scatter | solution.py:433
  896.4 38.2 %reduce-scatter.10.cloned.1.call-done = bf16[256,256]{1,0:T(8,128)(2,1)} async-done(((bf16[2048,256]{1,0:T(8,128)(2,1)}), bf16[256,256]{1,0:T(8,128)(2,1)}) %reduce-scatter.10.cloned.1.call-update) | async-done | bytes 131088 | tf_op jit(solution)/shard_map/reduce_scatter | solution.py:404
  936.2 38.4 %reduce-scatter.12.cloned.1.call-done = bf16[256,256]{1,0:T(8,128)(2,1)} async-done(((bf16[2048,256]{1,0:T(8,128)(2,1)}), bf16[256,256]{1,0:T(8,128)(2,1)}) %reduce-scatter.12.cloned.1.call-update) | async-done | bytes 131088 | tf_op jit(solution)/shard_map/reduce_scatter | solution.py:407
  976.2 63.7 %reduce-scatter.16.cloned.1.call-done = bf16[256,1536]{1,0:T(8,128)(2,1)} async-done(((bf16[2048,1536]{1,0:T(8,128)(2,1)}), bf16[256,1536]{1,0:T(8,128)(2,1)}) %reduce-scatter.16.cloned.1.call-update) | async-done | bytes 786448 | tf_op jit(solution)/shard_map/reduce_scatter | solution.py:410
  1039.9 2.5 convert_element_type.212
  1042.4 62.6 %reduce-scatter.18.cloned.1.call-done = bf16[256,1536]{1,0:T(8,128)(2,1)} async-done(((bf16[2048,1536]{1,0:T(8,128)(2,1)}), bf16[256,1536]{1,0:T(8,128)(2,1)}) %reduce-scatter.18.cloned.1.call-update) | async-done | bytes 786448 | tf_op jit(solution)/shard_map/reduce_scatter | solution.py:413
  1104.9 2.5 convert_element_type.214
  1107.4 63.1 %reduce-scatter.20.cloned.1.call-done = bf16[1536,256]{1,0:T(8,128)(2,1)} async-done(((bf16[1536,2048]{1,0:T(8,128)(2,1)}), bf16[1536,256]{1,0:T(8,128)(2,1)}) %reduce-scatter.20.cloned.1.call-update) | async-done | bytes 786448 | tf_op jit(solution)/shard_map/reduce_scatter | solution.py:436
  1172.9 223.7 %all-reduce.24.cloned.1.call-done = (bf16[768,2048]{1,0:T(8,128)(2,1)}, bf16[768,2048]{1,0:T(8,128)(2,1)}) async-done(((bf16[768,2048]{1,0:T(8,128)(2,1)}, bf16[768,2048]{1,0:T(8,128)(2,1)}), (bf16[768,2048]{1,0:T(8,128)(2,1)}, bf16[768,2048]{1,0:T(8,128)(2,1)})) %all-reduce.24.cloned.1.call-update) | async-done | bytes 6291472 | tf_op jit(solution)/shard_map/psum | solution.py:306
  1396.5 3.8 fusion.9
  1400.4 14.2 all-reduce.8
  1415.4 9.8 all-reduce.11
  1426.8 9.8 fusion.6
  (191 shorter events, 77.4 us)
Async XLA Ops:
  7.2 37.9 %copy-start = (bf16[768,2048]{1,0:T(8,128)(2,1)S(1)}, bf16[768,2048]{1,0:T(8,128)(2,1)}, u32[]{:S(2)}) copy-start(bf16[768,2048]{1,0:T(8,128)(2,1)} %param.15) | copy-start | bytes 9437188
  7.2 37.9 %all-gather.14.cloned.1.call-start = ((), (), s32[]{:S(2)}) async-start(), calls=%async_computation.8 | async-start | bytes 1179648 | tf_op jit(solution)/shard_map/all_gather | solution.py:236
  7.9 53.8 %all-gather.18.cloned.1.call-start = ((), (), s32[]{:S(2)}) async-start(), calls=%async_computation.10 | async-start | bytes 1179648 | tf_op jit(solution)/shard_map/all_gather | solution.py:237
  8.7 82.8 %all-gather.12.cloned.1.call-start = ((), (), s32[]{:S(2)}) async-start(), calls=%async_computation.7 | async-start | bytes 2359296 | tf_op jit(solution)/shard_map/all_gather | solution.py:235
  9.4 116.7 %all-gather.16.cloned.1.call-start = ((), (), s32[]{:S(2)}) async-start(), calls=%async_computation.9 | async-start | bytes 3538944 | tf_op jit(solution)/shard_map/all_gather | solution.py:274
  20.5 71.0 %copy-start.20 = (f32[8,1,256]{2,1,0:T(1,128)}, f32[8,1,256]{2,1,0:T(1,128)S(1)}, u32[]{:S(2)}) copy-start(f32[8,1,256]{2,1,0:T(1,128)S(1)} %convert_element_type.225) | copy-start | bytes 24580
  40.6 8.5 copy-start.9
  40.6 8.5 copy-start.13
  45.0 4.1 copy-start.25
  51.9 6.4 copy-start.23
  58.3 11.8 copy-start.38
  58.3 33.2 %copy-start.26 = (f32[768]{0:T(1024)S(1)}, f32[768]{0:T(1024)}, u32[]{:S(2)}) copy-start(f32[768]{0:T(1024)} %copy-done.25) | copy-start | bytes 9220
  58.3 102.5 %all-gather.20.cloned.1.call-start = ((), (), s32[]{:S(2)}) async-start(), calls=%async_computation.11 | async-start | bytes 3538944 | tf_op jit(solution)/shard_map/all_gather | solution.py:275
  66.9 123.9 %all-gather.22.cloned.1.call-start = ((), (), s32[]{:S(2)}) async-start(), calls=%async_computation.12 | async-start | bytes 2359296 | tf_op jit(solution)/shard_map/all_gather | solution.py:246
  67.5 258.8 %all-reduce.18.cloned.1.call-start = ((), (), s32[]{:S(2)}) async-start(), calls=%async_computation.13 | async-start | bytes 6291456 | tf_op jit(solution)/shard_map/psum | solution.py:297
  91.5 4.8 copy-start.32
  95.1 1.1 copy-start.4
  95.2 1.4 copy-start.10
  95.2 1.5 copy-start.14
  196.1 176.6 %all-gather.24.cloned.1.call-start = ((), (), s32[]{:S(2)}) async-start(), calls=%async_computation.14 | async-start | bytes 7077888 | tf_op jit(solution)/shard_map/all_gather | solution.py:238
  196.9 223.3 %all-gather.26.cloned.1.call-start = ((), (), s32[]{:S(2)}) async-start(), calls=%async_computation.15 | async-start | bytes 7077888 | tf_op jit(solution)/shard_map/all_gather | solution.py:239
  197.6 271.0 %all-gather.28.cloned.1.call-start = ((), (), s32[]{:S(2)}) async-start(), calls=%async_computation.16 | async-start | bytes 7077888 | tf_op jit(solution)/shard_map/all_gather | solution.py:247
  198.2 419.9 %all-reduce.20.cloned.1.call-start = ((), (), s32[]{:S(2)}) async-start(), calls=%async_computation.17 | async-start | bytes 6291456 | tf_op jit(solution)/shard_map/psum | solution.py:341
  326.3 3.7 copy-start.1
  326.3 3.7 copy-start.18
  329.5 0.6 copy-start.28
  481.4 9.0 copy-start.40
  481.4 9.0 copy-start.39
  481.4 9.0 copy-start.36
  496.9 308.3 %all-reduce.22.cloned.1.call-start = ((), (), s32[]{:S(2)}) async-start(), calls=%async_computation.25 | async-start | bytes 12582912
  618.1 4.8 copy-start.2
  618.1 5.6 copy-start.11
  618.1 5.6 copy-start.19
  618.1 5.6 copy-start.29
  623.7 4.5 copy-start.37
  628.2 3.0 copy-start.3
  657.8 218.0 %reduce-scatter.8.cloned.1.call-start = ((), (), s32[]{:S(2)}) async-start(), calls=%async_computation.18 | async-start | bytes 2359296 | tf_op jit(solution)/shard_map/reduce_scatter | solution.py:401
  668.7 2.0 copy-start.5
  668.8 2.0 copy-start.33
  670.5 0.7 copy-start.31
  671.2 2.1 copy-start.21
  672.4 0.9 copy-start.7
  676.7 9.2 copy-start.34
  676.8 217.8 %reduce-scatter.14.cloned.1.call-start = ((), (), s32[]{:S(2)}) async-start(), calls=%async_computation.21 | async-start | bytes 2359296 | tf_op jit(solution)/shard_map/reduce_scatter | solution.py:433
  683.0 251.6 %reduce-scatter.10.cloned.1.call-start = ((), (), s32[]{:S(2)}) async-start(), calls=%async_computation.19 | async-start | bytes 1179648 | tf_op jit(solution)/shard_map/reduce_scatter | solution.py:404
  805.2 4.5 copy-start.6
  809.7 8.5 copy-start.24
  809.7 10.8 copy-start.22
  820.5 3.1 copy-start.27
  823.6 151.0 %reduce-scatter.12.cloned.1.call-start = ((), (), s32[]{:S(2)}) async-start(), calls=%async_computation.20 | async-start | bytes 1179648 | tf_op jit(solution)/shard_map/reduce_scatter | solution.py:407
  826.9 213.0 %reduce-scatter.16.cloned.1.call-start = ((), (), s32[]{:S(2)}) async-start(), calls=%async_computation.22 | async-start | bytes 7077888 | tf_op jit(solution)/shard_map/reduce_scatter | solution.py:410
  836.2 268.8 %reduce-scatter.18.cloned.1.call-start = ((), (), s32[]{:S(2)}) async-start(), calls=%async_computation.23 | async-start | bytes 7077888 | tf_op jit(solution)/shard_map/reduce_scatter | solution.py:413
  845.5 325.0 %reduce-scatter.20.cloned.1.call-start = ((), (), s32[]{:S(2)}) async-start(), calls=%async_computation.24 | async-start | bytes 7077888 | tf_op jit(solution)/shard_map/reduce_scatter | solution.py:436
  854.9 541.6 %all-reduce.24.cloned.1.call-start = ((), (), s32[]{:S(2)}) async-start(), calls=%async_computation.26 | async-start | bytes 12582912 | tf_op jit(solution)/shard_map/psum | solution.py:306
  854.9 9.2 copy-start.8
  855.0 9.2 copy-start.12
  864.1 1.9 copy-start.16
  866.0 1.1 copy-start.15
  866.0 1.4 copy-start.17
  874.1 1.7 copy-start.30
  874.1 22.2 %copy-start.35 = (f32[256]{0:T(256)S(1)}, f32[256]{0:T(256)}, u32[]{:S(2)}) copy-start(f32[256]{0:T(256)} %get-tuple-element.53) | copy-start | bytes 3076
Sparse Core Ops, SparseCore 0:
  9.9 26.3 all-gather.13
  38.2 23.4 all-gather.17
  63.6 27.8 all-gather.11
  93.8 32.3 all-gather.15
  128.5 32.3 all-gather.19
  162.5 28.1 all-gather.21
  196.3 130.0 all-reduce.17
  328.2 44.5 all-gather.23
  374.6 45.5 all-gather.25
  421.9 46.6 all-gather.27
  497.0 121.0 all-reduce.19
  657.9 147.2 all-reduce.21
  808.8 41.3 reduce-scatter.7
  853.3 41.2 reduce-scatter.13
  898.5 36.0 reduce-scatter.9
  938.5 36.0 reduce-scatter.11
  978.1 61.7 reduce-scatter.15
  1043.1 61.7 reduce-scatter.17
  1108.7 61.7 reduce-scatter.19
  1173.3 223.1 all-reduce.23

commit v2 on v0

v2 whole, which is shorter than its diff:
```python
import functools
import math

import jax
import jax.numpy as jnp
from jax import lax
from jax.experimental import pallas as pl
from jax.experimental.pallas import tpu as pltpu

from jax.sharding import PartitionSpec as P

HEAD_SIZE = 128
EPS = 1e-06
BASE = 1000000.0
LOG2E = 1.4426950408889634
VMEM_BYTES = 62 << 20
NT = (((1,), (1,)), ((), ()))
TN = (((0,), (0,)), ((), ()))


def mm(a, b, dims=(((1,), (0,)), ((), ()))):
    return lax.dot_general(a, b, dims, preferred_element_type=jnp.float32)


def cut(rows, most=256):
    return math.gcd(rows, most)


MESH = pl.DeviceIdType.MESH
ANY = pl.BlockSpec(memory_space=pl.ANY)
VM = pl.BlockSpec(memory_space=pltpu.VMEM)


def bit_of(index, bit):
    return lax.rem(index // (1 << bit), 2)


def toggled(index, offset, bits):
    for bit in range(bits):
        if offset >> bit & 1:
            index = index + (1 - 2 * bit_of(index, bit)) * (1 << bit)
    return index


def seq_bits():
    return lax.axis_size("seq").bit_length() - 1


def bit_order(half):
    outer = list(range(1, seq_bits()))
    return (outer if half == 0 else outer[::-1]) + [0]


def last_bit(half, offset):
    return [b for b in bit_order(half) if offset >> b & 1][-1]


def greet(over_seq, over_tp):
    barrier = pltpu.get_barrier_semaphore()
    s, t, count = lax.axis_index("seq"), lax.axis_index("tp"), lax.axis_size("tp")
    expected = 0
    if over_seq:
        for bit in range(seq_bits()):
            pl.semaphore_signal(barrier, inc=1, device_id=(toggled(s, 1 << bit, seq_bits()), t), device_id_type=MESH)
        expected = seq_bits()
    if over_tp:
        @pl.when(t > 0)
        def _():
            pl.semaphore_signal(barrier, inc=1, device_id=(s, t - 1), device_id_type=MESH)

        @pl.when(t < count - 1)
        def _():
            pl.semaphore_signal(barrier, inc=1, device_id=(s, t + 1), device_id_type=MESH)

        expected = expected + jnp.where(t > 0, 1, 0) + jnp.where(t < count - 1, 1, 0)
    pl.semaphore_wait(barrier, expected)


class SeqGather:
    def __init__(self, buf, send, recv, halves=2):
        self.buf, self.send, self.recv, self.halves = buf, send, recv, halves
        self.bits = seq_bits()
        self.n = 1 << self.bits
        self.me, self.t = lax.axis_index("seq"), lax.axis_index("tp")

    def block(self, half, offset):
        rows = self.buf.shape[1] // self.halves
        return self.buf.at[toggled(self.me, offset, self.bits), pl.ds(half * rows, rows)]

    def copy(self, half, offset):
        bit = last_bit(half, offset)
        ref = self.block(half, offset ^ (1 << bit))
        return pltpu.make_async_remote_copy(
            src_ref=ref, dst_ref=ref, send_sem=self.send.at[half, offset], recv_sem=self.recv.at[half, offset],
            device_id=(toggled(self.me, 1 << bit, self.bits), self.t), device_id_type=MESH)

    def start(self, half):
        for bit in bit_order(half):
            self.copy(half, 1 << bit).start()

    def arrive(self, half, offset):
        ref = self.block(half, offset)
        pltpu.make_async_remote_copy(
            src_ref=ref, dst_ref=ref, send_sem=self.send.at[half, offset], recv_sem=self.recv.at[half, offset],
            device_id=(self.me, self.t), device_id_type=MESH).wait_recv()
        order = bit_order(half)
        for bit in order[order.index(last_bit(half, offset)) + 1:]:
            self.copy(half, offset | 1 << bit).start()

    def finish(self):
        for half in range(self.halves):
            for offset in range(1, self.n):
                self.copy(half, offset).wait_send()

    def events(self):
        def due(event):
            half, offset = event
            order = bit_order(half)
            steps = [order.index(b) for b in range(1, self.bits) if offset >> b & 1]
            return (sum(2 ** k for k in steps), offset & 1, half)
        return sorted(((h, r) for h in range(self.halves) for r in range(1, self.n)), key=due)


def gather_sems(halves=2):
    n = lax.axis_size("seq")
    return [pltpu.SemaphoreType.DMA((halves, n)), pltpu.SemaphoreType.DMA((halves, n))]


class LineSum:
    def __init__(self, part, recv, send_sem, recv_sem):
        self.part, self.recv, self.send_sem, self.recv_sem = part, recv, send_sem, recv_sem
        self.m = part.shape[1]
        self.s, self.t = lax.axis_index("seq"), lax.axis_index("tp")

    def copy(self, p, j, slot, to):
        return pltpu.make_async_remote_copy(
            src_ref=self.part.at[p, j], dst_ref=self.recv.at[p, slot], send_sem=self.send_sem.at[p, j],
            recv_sem=self.recv_sem.at[p, slot], device_id=(self.s, to), device_id_type=MESH)

    def add(self, p, j):
        self.copy(p, j, j, self.t).wait_recv()
        self.part[p, j] = (self.part[p, j].astype(jnp.float32) + self.recv[p, j].astype(jnp.float32)).astype(jnp.bfloat16)

    def left(self, p, j):
        @pl.when(self.t > j)
        def _():
            @pl.when(self.t < self.m - 1)
            def _():
                self.add(p, j)

            self.sent(p, j - 1, j > 0)
            if p > 0 and j == 0:
                self.sent(p - 1, self.t - 1, True)
            self.copy(p, j, j, self.t - 1).start()

    def right(self, p, j):
        @pl.when(self.t < j)
        def _():
            @pl.when(self.t > 0)
            def _():
                self.add(p, j)

            self.sent(p, j + 1, j < self.m - 1)
            if p > 0 and j == self.m - 1:
                self.sent(p - 1, self.t + 1, True)
            self.copy(p, j, jnp.where(self.t + 1 == j, self.m, j), self.t + 1).start()

    def sent(self, p, j, some):
        if some:
            self.copy(p, j, j, self.t).wait_send()

    def step(self, p, k):
        self.left(p, k)
        self.right(p, self.m - 1 - k)

    def clear(self, p):
        @pl.when(self.t == self.m - 1)
        def _():
            self.recv[p, self.m - 1] = jnp.zeros(self.recv.shape[2:], self.recv.dtype)

        @pl.when(self.t == 0)
        def _():
            self.recv[p, self.m] = jnp.zeros(self.recv.shape[2:], self.recv.dtype)

    def total(self, p):
        @pl.when(self.t < self.m - 1)
        def _():
            self.copy(p, self.t, self.t, self.t).wait_recv()

        @pl.when(self.t > 0)
        def _():
            self.copy(p, self.t, self.m, self.t).wait_recv()

        f32 = jnp.float32
        return self.part[p, self.t].astype(f32) + (self.recv[p, self.t].astype(f32) + self.recv[p, self.m].astype(f32))

    def finish(self, p):
        @pl.when(self.t > 0)
        def _():
            self.copy(p, self.t - 1, 0, self.t).wait_send()

        @pl.when(self.t < self.m - 1)
        def _():
            self.copy(p, self.t + 1, 0, self.t).wait_send()


class LineGather:
    def __init__(self, buf, send_sem, recv_sem):
        self.buf, self.send_sem, self.recv_sem = buf, send_sem, recv_sem
        self.m = buf.shape[1]
        self.s, self.t = lax.axis_index("seq"), lax.axis_index("tp")

    def copy(self, p, j, way):
        ref = self.buf.at[p, j]
        return pltpu.make_async_remote_copy(
            src_ref=ref, dst_ref=ref, send_sem=self.send_sem.at[p, way, j], recv_sem=self.recv_sem.at[p, j],
            device_id=(self.s, self.t + (2 * way - 1)), device_id_type=MESH)

    def pass_on(self, p, j, way):
        @pl.when(self.t > 0 if way == 0 else self.t < self.m - 1)
        def _():
            self.copy(p, j, way).start()

    def start(self, p):
        self.pass_on(p, self.t, 0)
        self.pass_on(p, self.t, 1)

    def arrive(self, p, distance):
        @pl.when(self.t + distance < self.m)
        def _():
            self.copy(p, self.t + distance, 0).wait_recv()
            self.pass_on(p, self.t + distance, 0)

        @pl.when(self.t >= distance)
        def _():
            self.copy(p, self.t - distance, 1).wait_recv()
            self.pass_on(p, self.t - distance, 1)

    def finish(self, p):
        for j in range(self.m):
            @pl.when((self.t > 0) & (self.t <= j))
            def _(j=j):
                self.copy(p, j, 0).wait_send()

            @pl.when((self.t < self.m - 1) & (self.t >= j))
            def _(j=j):
                self.copy(p, j, 1).wait_send()


def line_sems(pieces):
    m = lax.axis_size("tp")
    return [pltpu.SemaphoreType.DMA((pieces, m)), pltpu.SemaphoreType.DMA((pieces, m + 1)),
            pltpu.SemaphoreType.DMA((pieces, 2, m)), pltpu.SemaphoreType.DMA((pieces, m))]


class Plan:
    def __init__(self):
        self.steps = []

    def at(self, time, step, *args):
        self.steps.append((time, len(self.steps), step, args))

    def run(self):
        for _, _, step, args in sorted(self.steps, key=lambda one: one[:2]):
            step(*args)


def attn_fwd_block(q_ref, kv_ref, out_ref, sum_ref, bias_ref, kv, rows, tile):
    scale = HEAD_SIZE ** -0.5 * LOG2E
    all_rows = q_ref.shape[1]
    for h in range(kv):
        cols = slice(h * HEAD_SIZE, (h + 1) * HEAD_SIZE)
        v_cols = slice((kv + h) * HEAD_SIZE, (kv + h + 1) * HEAD_SIZE)
        for start in range(0, all_rows, tile):
            at = start % rows
            n_keys = rows if bias_ref is None else at + tile
            scores = mm(q_ref[h, start:start + tile], kv_ref[:n_keys, cols], NT) * scale
            if bias_ref is not None:
                scores = scores + bias_ref[at:at + tile, :n_keys]
            weights = jnp.exp2(scores)
            part = weights[:, :HEAD_SIZE]
            for c in range(HEAD_SIZE, n_keys, HEAD_SIZE):
                part = part + weights[:, c:c + HEAD_SIZE]
            sum_ref[h, start:start + tile] += part
            out_ref[h, start:start + tile] += mm(weights.astype(jnp.bfloat16), kv_ref[:n_keys, v_cols])


def rms_inverse(values):
    return lax.rsqrt(jnp.mean(values * values, axis=-1, keepdims=True) + EPS)


def forward_kernel(tok_ref, wq_ref, wk_ref, wv_ref, gain_ref, cos_ref, sin_ref, qd_ref, kd_ref, o_ref, gate_ref,
                   norm_ref, proj_ref, q_ref, kv_ref, att_ref, lse_ref, gains_ref, w, o_all, gate_all,
                   inv, acc, total, bias, local_sem, *sems):
    f32, b16 = jnp.float32, jnp.bfloat16
    n, rows, _ = kv_ref.shape
    kv, all_rows, _ = q_ref.shape
    group = all_rows // rows
    me = lax.axis_index("seq")
    bits = seq_bits()
    tile = cut(rows)
    depth = w.shape[1]
    q_width, k_width = wq_ref.shape[1], wk_ref.shape[1]
    w_gather = SeqGather(w, sems[0], sems[1])
    gain_gather = SeqGather(gains_ref, sems[2], sems[3], halves=1)
    kv_gather = SeqGather(kv_ref, sems[4], sems[5])
    o_gather = SeqGather(o_all, sems[6], sems[7])
    gate_gather = SeqGather(gate_all, sems[8], sems[9])

    own = [pltpu.make_async_copy(wq_ref, w.at[me, :, pl.ds(0, q_width)], local_sem.at[0]),
           pltpu.make_async_copy(wk_ref, w.at[me, :, pl.ds(q_width, k_width)], local_sem.at[1]),
           pltpu.make_async_copy(wv_ref, w.at[me, :, pl.ds(q_width + k_width, k_width)], local_sem.at[2]),
           pltpu.make_async_copy(o_ref, o_all.at[me], local_sem.at[3]),
           pltpu.make_async_copy(gate_ref, gate_all.at[me], local_sem.at[4])]
    for copy in own:
        copy.start()
    gains_ref[me] = gain_ref[...]
    greet(True, False)
    for copy in own[:3]:
        copy.wait()
    w_gather.start(0)
    w_gather.start(1)
    gain_gather.start(0)

    @pl.loop(0, rows // tile)
    def _(i):
        at = pl.ds(i * tile, tile)
        inv[at] = rms_inverse(tok_ref[at].astype(f32))

    visible = (lax.broadcasted_iota(jnp.int32, (rows, rows), 1)
               <= lax.broadcasted_iota(jnp.int32, (rows, rows), 0)) & (qd_ref[...] == kd_ref[...])
    bias[...] = jnp.where(visible, 0.0, -1e30)
    for event in gain_gather.events():
        gain_gather.arrive(*event)

    def project(offset):
        source = toggled(me, offset, bits)
        cols = pl.ds(pl.multiple_of(source * depth, depth), depth)

        @pl.loop(0, rows // tile)
        def _(i):
            at = pl.ds(i * tile, tile)
            block = (tok_ref[at, cols].astype(f32) * inv[at] * gains_ref[source, 0:1, :depth]).astype(b16)
            norm_ref[at, cols] = block
            part = mm(block, w[source])
            if offset == 0:
                proj_ref[at] = part
            else:
                proj_ref[at] += part

    project(0)
    came = {}
    for half, offset in w_gather.events():
        w_gather.arrive(half, offset)
        came[offset] = came.get(offset, 0) + 1
        if came[offset] == 2:
            project(offset)

    gain_q, gain_k = gains_ref[0, 2:3, :HEAD_SIZE], gains_ref[0, 3:4, :HEAD_SIZE]
    for j in range(1, n):
        gain_q = gain_q + gains_ref[j, 2:3, :HEAD_SIZE]
        gain_k = gain_k + gains_ref[j, 3:4, :HEAD_SIZE]

    def rotated(at, first, gain):
        u = proj_ref[at, first:first + HEAD_SIZE]
        u = u * rms_inverse(u) * gain
        return (u * cos_ref[at] + pltpu.roll(u, HEAD_SIZE // 2, 1) * sin_ref[at]).astype(b16)

    @pl.loop(0, rows // tile)
    def _(i):
        at = pl.ds(i * tile, tile)
        for h in range(kv):
            kv_ref[me, at, h * HEAD_SIZE:(h + 1) * HEAD_SIZE] = rotated(at, q_width + h * HEAD_SIZE, gain_k)
        kv_ref[me, at, k_width:] = proj_ref[at, q_width + k_width:].astype(b16)

    kv_gather.start(0)
    kv_gather.start(1)

    @pl.loop(0, rows // tile)
    def _(i):
        at = pl.ds(i * tile, tile)
        for h in range(kv):
            for g in range(group):
                q_ref[h, pl.ds(g * rows + i * tile, tile)] = rotated(at, (h * group + g) * HEAD_SIZE, gain_q)

    acc[...] = jnp.zeros_like(acc)
    total[...] = jnp.zeros_like(total)
    attn_fwd_block(q_ref, kv_ref.at[me], acc.at[0], total.at[0], bias, kv, rows, tile)
    own[3].wait()
    own[4].wait()

    kv_steps = [[] for _ in range(n)]
    seen = set()
    order = kv_gather.events()
    offsets = sorted(range(1, n), key=lambda r: max(order.index((h, r)) for h in range(2)))
    taken = 0
    for k, offset in enumerate(offsets):
        need = max(order.index((h, offset)) for h in range(2)) + 1
        kv_steps[k] = order[taken:max(need, taken)]
        taken = max(need, taken)
    only_first = jnp.where(qd_ref[...] == 0, 1.0, 0.0)

    @pl.loop(0, n - 1)
    def _(k):
        source = 0
        for i, offset in enumerate(offsets):
            source = source + jnp.where(k == i, toggled(me, offset, bits), 0)

            @pl.when(k == i)
            def _(i=i):
                for event in kv_steps[i]:
                    kv_gather.arrive(*event)
                if i == n - 2:
                    for gather in (o_gather, gate_gather):
                        gather.start(0)
                        gather.start(1)

        @pl.when(source < me)
        def _():
            attn_fwd_block(q_ref, kv_ref.at[source], acc.at[1], total.at[1], None, kv, rows, tile)

    for gather in (o_gather, gate_gather):
        for event in gather.events():
            gather.arrive(*event)
    for h in range(kv):
        for g in range(group):
            for start in range(0, rows, tile):
                at = slice(g * rows + start, g * rows + start + tile)
                t = total[0, h, at] + total[1, h, at] * only_first[start:start + tile]
                out = acc[0, h, at] + acc[1, h, at] * only_first[start:start + tile]
                cols = slice((h * group + g) * HEAD_SIZE, (h * group + g + 1) * HEAD_SIZE)
                att_ref[start:start + tile, cols] = (out / jnp.sum(t, axis=1, keepdims=True)).astype(b16)
                lse_ref[h, :, at] = jnp.log2(jnp.sum(t.T, axis=0, keepdims=True))
    for gather in (w_gather, gain_gather, kv_gather, o_gather, gate_gather):
        gather.finish()


def forward_attention(tokens, q_weight, key_matrix, value_matrix, gains, cosines, sines, doc_column, doc_row, o_weight, gate_weight):
    n = lax.axis_size("seq")
    rows, width = tokens.shape
    depth, q_width = q_weight.shape
    k_width = key_matrix.shape[1]
    kv, group = k_width // HEAD_SIZE, q_width // k_width
    f32, b16 = jnp.float32, jnp.bfloat16
    wide = q_width + 2 * k_width
    heads = (kv, group * rows, HEAD_SIZE)
    out = [((rows, width), b16), ((rows, wide), f32), (heads, b16), ((n, rows, 2 * k_width), b16), ((rows, q_width), b16),
           ((kv, 1, group * rows), f32), ((n,) + gains.shape, f32), ((n, depth, wide), b16), ((n,) + o_weight.shape, b16), ((n,) + gate_weight.shape, b16)]
    sems = []
    for halves in (2, 1, 2, 2, 2):
        sems += gather_sems(halves)
    return pl.pallas_call(
        forward_kernel,
        out_shape=[jax.ShapeDtypeStruct(*one) for one in out],
        in_specs=[VM] + [ANY] * 3 + [VM] * 5 + [ANY] * 2,
        out_specs=[VM] * 8 + [ANY] * 2,
        scratch_shapes=[pltpu.VMEM((rows, 1), f32), pltpu.VMEM((2,) + heads, f32),
                        pltpu.VMEM((2,) + heads, f32), pltpu.VMEM((rows, rows), f32), pltpu.SemaphoreType.DMA((5,))] + sems,
        compiler_params=pltpu.CompilerParams(vmem_limit_bytes=VMEM_BYTES, collective_id=1, has_side_effects=True),
        name="forward_attention",
    )(tokens, q_weight, key_matrix, value_matrix, gains, cosines, sines, doc_column, doc_row, o_weight, gate_weight)


class SeqSum:
    def __init__(self, source, loc, near, far, sems):
        self.source, self.loc, self.near, self.far = source, loc, near, far
        self.load_sem, self.near_sem, self.far_sem = sems
        self.bits = seq_bits()
        self.count = 1 << (self.bits - 1)
        self.me, self.t = lax.axis_index("seq"), lax.axis_index("tp")
        self.half_rows = loc.shape[1] // 2

    def first(self, half, e):
        order = bit_order(half)[:-1]
        return min(order.index(b) for b in range(1, self.bits) if 2 * e >> b & 1)

    def load(self, e):
        return pltpu.make_async_copy(self.source(toggled(self.me, 2 * e, self.bits)), self.loc.at[e], self.load_sem.at[e])

    def cross(self, e):
        return pltpu.make_async_remote_copy(
            src_ref=self.source(toggled(self.me, 2 * e + 1, self.bits)), dst_ref=self.near.at[e],
            send_sem=self.near_sem.at[0, e], recv_sem=self.near_sem.at[1, e],
            device_id=(toggled(self.me, 1, self.bits), self.t), device_id_type=MESH)

    def begin(self):
        for e in reversed(range(self.count)):
            self.cross(e).start()
            self.load(e).start()

    def meet(self, e):
        self.load(e).wait()
        self.cross(e).wait_recv()
        self.loc[e] += self.near[e]
        for half in range(2):
            if e and self.first(half, e) == 0:
                self.hop(half, e).start()

    def hop(self, half, e):
        bit = bit_order(half)[self.first(half, e)]
        return pltpu.make_async_remote_copy(
            src_ref=self.loc.at[e, pl.ds(half * self.half_rows, self.half_rows)], dst_ref=self.far.at[half, e - 1],
            send_sem=self.far_sem.at[0, half, e - 1], recv_sem=self.far_sem.at[1, half, e - 1],
            device_id=(toggled(self.me, 1 << bit, self.bits), self.t), device_id_type=MESH)

    def arrive(self, half, e):
        place = self.first(half, e)
        to = (2 * e ^ 1 << bit_order(half)[place]) // 2
        self.hop(half, e).wait_recv()
        self.loc[to, half * self.half_rows:(half + 1) * self.half_rows] += self.far[half, e - 1]
        if to and self.first(half, to) == place + 1:
            self.hop(half, to).start()

    def rounds(self):
        found = [[] for _ in range(self.bits - 1)]
        for e in reversed(range(1, self.count)):
            for half in range(2):
                found[self.first(half, e)].append((half, e))
        return found

    def finish(self):
        for e in range(self.count):
            self.cross(e).wait_send()
            for half in range(2 if e else 0):
                self.hop(half, e).wait_send()


def sum_scratch(rows, columns):
    count = lax.axis_size("seq") // 2
    b16 = jnp.bfloat16
    return [pltpu.VMEM((count, rows, columns), b16), pltpu.VMEM((count, rows, columns), b16),
            pltpu.VMEM((2, max(count - 1, 1), rows // 2, columns), b16), pltpu.SemaphoreType.DMA((count,)),
            pltpu.SemaphoreType.DMA((2, count)), pltpu.SemaphoreType.DMA((2, 2, max(count - 1, 1)))]


SUM_SCRATCH = 6


def seq_sum(source, scratch):
    return SeqSum(source, *scratch[:3], scratch[3:])


def middle_kernel(att_ref, o_all, gate_all, up_ref, down_ref, tok_ref, cot_ref, gains_ref,
                  low_ref, after_grad_ref, mlp_ref, gain_out, grads_ref,
                  up_all, down_all, part, recv, norm_mid, act, gg, gu, after_own, tok_own, stage,
                  local_sem, stage_sem, *sems):
    f32, b16 = jnp.float32, jnp.bfloat16
    pieces, m, sub, width = cot_ref.shape
    n, depth, ff = gate_all.shape
    piece = m * sub
    me, t = lax.axis_index("seq"), lax.axis_index("tp")
    up_gather = SeqGather(up_all, sems[0], sems[1])
    down_gather = SeqGather(down_all, sems[2], sems[3])
    attn_sum = LineSum(part, recv, sems[4], sems[5])
    mid_sum = LineSum(part, recv, sems[8], sems[9])
    norm_gather = LineGather(norm_mid, sems[6], sems[7])
    low_gather = LineGather(low_ref, sems[10], sems[11])

    own = [pltpu.make_async_copy(up_ref, up_all.at[me], local_sem.at[0]),
           pltpu.make_async_copy(down_ref, down_all.at[me], local_sem.at[1])]
    own += [pltpu.make_async_copy(tok_ref.at[p, t], tok_own.at[p], local_sem.at[2 + p]) for p in range(pieces)]
    for copy in own:
        copy.start()
    greet(True, True)
    for copy in own:
        copy.wait()
    for half in range(2):
        up_gather.start(half)
    for p in range(pieces):
        attn_sum.clear(p)
    gain_out[...] = jnp.zeros_like(gain_out)
    plan = Plan()

    def mlp_gain(j):
        return gains_ref[j, 1:2, :depth]

    def project(p):
        rows = att_ref[p * piece:(p + 1) * piece]
        for j in range(n):
            block = mm(rows, o_all[j]).astype(b16)
            part[p, :, :, j * depth:(j + 1) * depth] = block.reshape(m, sub, depth)

    def normalise(p):
        after = tok_own[p].astype(f32) + attn_sum.total(p)
        after_own[p] = after
        normed = after * rms_inverse(after)
        for j in range(n):
            cols = slice(j * depth, (j + 1) * depth)
            norm_mid[p, t, :, cols] = (normed[:, cols] * mlp_gain(j)).astype(b16)
        norm_gather.start(p)

    def hidden(p, first, count):
        rows = slice(p * piece, (p + 1) * piece)
        cols = slice(first, first + count)
        x = norm_mid[p].reshape(piece, width)
        gate = mm(x, gate_all[:, :, cols].reshape(width, count))
        up = mm(x, up_all[:, :, cols].reshape(width, count))
        grad = mm(cot_ref[p, :, :, :depth].reshape(piece, depth), down_all[0, cols], NT)
        for j in range(1, n):
            c = cot_ref[p, :, :, j * depth:(j + 1) * depth].reshape(piece, depth)
            grad = grad + mm(c, down_all[j, cols], NT)
        sig = jax.nn.sigmoid(gate)
        silu = gate * sig
        act[rows, cols] = (silu * up).astype(b16)
        gg[rows, cols] = (grad * up * sig * (1.0 + gate * (1.0 - sig))).astype(b16)
        gu[rows, cols] = (grad * silu).astype(b16)

    def mid(p, first, count):
        rows = slice(p * piece, (p + 1) * piece)
        for j in range(first, first + count):
            block = mm(gg[rows], gate_all[j], NT) + mm(gu[rows], up_all[j], NT)
            part[p, :, :, j * depth:(j + 1) * depth] = block.astype(b16).reshape(m, sub, depth)

    def mlp_out(p):
        rows = slice(p * piece, (p + 1) * piece)
        for j in range(n):
            block = mm(act[rows], down_all[j]).astype(b16)
            mlp_ref[p, :, :, j * depth:(j + 1) * depth] = block.reshape(m, sub, depth)
        mlp_ref[p, t] = (mlp_ref[p, t].astype(f32) + after_own[p]).astype(b16)

    def mid_back(p):
        grad = mid_sum.total(p)
        after = after_own[p]
        inverse = rms_inverse(after)
        normed = after * inverse
        mean = 0.0
        for j in range(n):
            cols = slice(j * depth, (j + 1) * depth)
            gain_out[:, cols] += jnp.sum(grad[:, cols] * normed[:, cols], axis=0, keepdims=True)
            mean = mean + jnp.sum(grad[:, cols] * mlp_gain(j) * normed[:, cols], axis=1, keepdims=True)
        mean = mean * (1.0 / width)
        for j in range(n):
            cols = slice(j * depth, (j + 1) * depth)
            back = inverse * (grad[:, cols] * mlp_gain(j) - normed[:, cols] * mean)
            back = back + cot_ref[p, t, :, cols].astype(f32)
            after_grad_ref[p, :, cols] = back
            low_ref[p, t, :, cols] = back.astype(b16)
        low_gather.start(p)

    def staged(j, slot):
        return pltpu.make_async_copy(stage.at[slot], grads_ref.at[j], stage_sem.at[slot])

    def weight_grads(j):
        slot = j % 2
        if j >= 2:
            staged(j - 2, slot).wait()
        cols = slice(j * depth, (j + 1) * depth)
        x = cot_ref[:, :, :, cols].reshape(pieces * piece, depth)
        stage[slot, 0] = mm(x, act[...], TN).astype(b16)
        x = norm_mid[:, :, :, cols].reshape(pieces * piece, depth)
        stage[slot, 1] = mm(x, gg[...], TN).astype(b16)
        stage[slot, 2] = mm(x, gu[...], TN).astype(b16)
        staged(j, slot).start()

    hop = 6.0
    ready = []
    for p in range(pieces):
        plan.at(2.0 * p, project, p)
        start = 4.0 + 3 * hop * p
        for k in range(m - 1):
            plan.at(start + hop * k, attn_sum.step, p, k)
        start += hop * m
        plan.at(start, normalise, p)
        for d in range(1, m):
            plan.at(start + hop * d, norm_gather.arrive, p, d)
        ready.append(start + hop * m - 3.0)

    def due(gather, event, base):
        half, offset = event
        order = bit_order(half)
        steps = sum(2 ** order.index(b) for b in range(1, gather.bits) if offset >> b & 1)
        return base + 9.0 * max(steps, 0.2)

    def begin_down():
        for half in range(2):
            down_gather.start(half)

    for event in up_gather.events():
        plan.at(due(up_gather, event, 3.0), up_gather.arrive, *event)
    plan.at(22.0, begin_down)
    for event in down_gather.events():
        plan.at(due(down_gather, event, 29.0), down_gather.arrive, *event)

    chunk = cut(ff, 512)
    chunks = ff // chunk
    clock = 58.0
    for p in range(pieces):
        clock = max(clock, ready[p])
        for c in range(chunks):
            plan.at(clock, hidden, p, c * chunk, chunk)
            clock += 2.4

        def reuse(p=p):
            if p == pieces - 1:
                attn_sum.finish(p)
            mid_sum.clear(p)

        plan.at(clock, reuse)
        for half in range(2):
            plan.at(clock, mid, p, half * (n // 2), n // 2)
            clock += 2.2
        start = max(clock, 70.0 + 3 * hop * p)
        for k in range(m - 1):
            plan.at(start + hop * k, mid_sum.step, p, k)
        start += hop * m
        plan.at(start, mid_back, p)
        for d in range(1, m):
            plan.at(start + hop * d, low_gather.arrive, p, d)
    for j in range(n):
        plan.at(clock, weight_grads, j)
        clock += 3.5
    for p in range(pieces):
        plan.at(clock, mlp_out, p)
        clock += 2.2
    plan.run()

    for j in range(n - 2, n):
        staged(j, j % 2).wait()
    up_gather.finish()
    down_gather.finish()
    mid_sum.finish(pieces - 1)
    for p in range(pieces):
        norm_gather.finish(p)
        low_gather.finish(p)


def middle(attended, o_all, gate_all, up_weight, down_weight, tokens, cotangent, gains):
    f32, b16 = jnp.float32, jnp.bfloat16
    pieces, m, sub, width = tokens.shape
    n, depth, ff = gate_all.shape
    rows = pieces * m * sub
    blocks = tokens.shape
    out = [(blocks, b16), ((pieces, sub, width), f32), (blocks, b16), ((1, width), f32), ((n, 3, depth, ff), b16)]
    return pl.pallas_call(
        middle_kernel,
        out_shape=[jax.ShapeDtypeStruct(*one) for one in out],
        in_specs=[VM] * 3 + [ANY] * 3 + [VM] * 2,
        out_specs=[VM] * 4 + [ANY],
        scratch_shapes=[pltpu.VMEM((n, depth, ff), b16), pltpu.VMEM((n, ff, depth), b16), pltpu.VMEM(blocks, b16),
                        pltpu.VMEM((pieces, m + 1, sub, width), b16), pltpu.VMEM(blocks, b16),
                        pltpu.VMEM((rows, ff), b16), pltpu.VMEM((rows, ff), b16), pltpu.VMEM((rows, ff), b16),
                        pltpu.VMEM((pieces, sub, width), f32), pltpu.VMEM((pieces, sub, width), b16),
                        pltpu.VMEM((2, 3, depth, ff), b16), pltpu.SemaphoreType.DMA((2 + pieces,)),
                        pltpu.SemaphoreType.DMA((2,))]
        + gather_sems() + gather_sems() + line_sems(pieces) + line_sems(pieces),
        compiler_params=pltpu.CompilerParams(vmem_limit_bytes=VMEM_BYTES, collective_id=2, has_side_effects=True),
        name="middle",
    )(attended, o_all, gate_all, up_weight, down_weight, tokens, cotangent, gains)


def attn_bwd_block(h, q_ref, do_ref, lse_ref, delta_ref, kv_ref, dq_ref, dk_ref, dv_ref, bias_ref, kv, rows, tile):
    scale = HEAD_SIZE ** -0.5 * LOG2E
    all_rows = q_ref.shape[1]
    k_cols = pl.ds(pl.multiple_of(h * HEAD_SIZE, HEAD_SIZE), HEAD_SIZE)
    v_cols = pl.ds(pl.multiple_of((kv + h) * HEAD_SIZE, HEAD_SIZE), HEAD_SIZE)
    dk_ref[...] = jnp.zeros_like(dk_ref)
    dv_ref[...] = jnp.zeros_like(dv_ref)
    for start in range(0, all_rows, tile):
        at = start % rows
        n_keys = rows if bias_ref is None else at + tile
        q = q_ref[h, start:start + tile]
        do = do_ref[h, start:start + tile]
        k = kv_ref[:n_keys, k_cols]
        scores = mm(k, q, NT) * scale - lse_ref[h, :, start:start + tile]
        if bias_ref is not None:
            scores = scores + bias_ref[:n_keys, at:at + tile]
        probs = jnp.exp2(scores)
        grad = mm(kv_ref[:n_keys, v_cols], do, NT)
        grad = (probs * (grad - delta_ref[h, :, start:start + tile])).astype(jnp.bfloat16)
        dv_ref[:n_keys] += mm(probs.astype(jnp.bfloat16), do)
        dk_ref[:n_keys] += mm(grad, q)
        dq_ref[h, start:start + tile] += mm(grad, k, TN)


def backward_kernel(q_ref, low_ref, o_all, att_ref, lse_ref, kv_ref, kd_ref, qdr_ref, grads_ref,
                    dq_ref, dkv_ref, gate_out, up_out, o_grads, do, delta, lse_off, dk, dv, bias, *scratch):
    f32, b16 = jnp.float32, jnp.bfloat16
    kv, all_rows, _ = q_ref.shape
    n, rows, _ = kv_ref.shape
    group = all_rows // rows
    depth = o_all.shape[2]
    me = lax.axis_index("seq")
    tile = cut(rows)
    scale = HEAD_SIZE ** -0.5
    gate_sum = seq_sum(lambda j: grads_ref.at[j, 1], scratch[:SUM_SCRATCH])
    up_sum = seq_sum(lambda j: grads_ref.at[j, 2], scratch[SUM_SCRATCH:])

    greet(True, False)
    gate_sum.begin()
    dq_ref[...] = jnp.zeros_like(dq_ref)
    off = jnp.where(qdr_ref[...] == 0, 0.0, 1e30)
    visible = (lax.broadcasted_iota(jnp.int32, (rows, rows), 0)
               <= lax.broadcasted_iota(jnp.int32, (rows, rows), 1)) & (kd_ref[...] == qdr_ref[...])
    bias[...] = jnp.where(visible, 0.0, -1e30)
    for start in range(0, rows, tile):
        grad = mm(low_ref[start:start + tile, :depth], o_all[0], NT)
        for j in range(1, n):
            grad = grad + mm(low_ref[start:start + tile, j * depth:(j + 1) * depth], o_all[j], NT)
        grad = grad.astype(b16)
        for h in range(kv):
            for g in range(group):
                cols = slice((h * group + g) * HEAD_SIZE, (h * group + g + 1) * HEAD_SIZE)
                at = slice(g * rows + start, g * rows + start + tile)
                part = grad[:, cols]
                do[h, at] = part
                prod = part.astype(f32) * att_ref[start:start + tile, cols].astype(f32)
                delta[h, :, at] = jnp.sum(prod.T, axis=0, keepdims=True)
    for j in range(n):
        o_grads[j] = mm(low_ref[:, j * depth:(j + 1) * depth], att_ref[...], TN).astype(b16)
    for h in range(kv):
        for g in range(group):
            at = slice(g * rows, (g + 1) * rows)
            lse_off[h, :, at] = lse_ref[h, :, at] + off

    def keep(j, h):
        k_cols = pl.ds(pl.multiple_of(h * HEAD_SIZE, HEAD_SIZE), HEAD_SIZE)
        v_cols = pl.ds(pl.multiple_of((kv + h) * HEAD_SIZE, HEAD_SIZE), HEAD_SIZE)
        dkv_ref[j, :, k_cols] = (dk[...] * scale).astype(b16)
        dkv_ref[j, :, v_cols] = dv[...].astype(b16)

    @pl.loop(0, kv)
    def _(h):
        attn_bwd_block(h, q_ref, do, lse_ref, delta, kv_ref.at[me], dq_ref, dk, dv, bias, kv, rows, tile)
        keep(me, h)

    steps = n * kv
    events = [[] for _ in range(steps)]

    def at_time(time, step, *args):
        events[min(int(time / 3.8), steps - 1)].append((step, args))

    def plan_sum(one, base, share):
        for e in reversed(range(one.count)):
            at_time(base, one.meet, e)
        for k, found in enumerate(one.rounds()):
            for event in found:
                at_time(base + share * 18.0 * (2.0 - 0.5 ** k), one.arrive, *event)

    plan_sum(gate_sum, 0.0, 1.0)
    at_time(4.0, up_sum.begin)
    plan_sum(up_sum, 15.0, 1.0)

    @pl.loop(0, steps)
    def _(i):
        for k in range(steps):
            if events[k]:
                @pl.when(i == k)
                def _(k=k):
                    for step, args in events[k]:
                        step(*args)

        j, h = i // kv, i % kv

        @pl.when(j < me)
        def _():
            attn_bwd_block(h, q_ref, do, lse_off, delta, kv_ref.at[j], dq_ref, dk, dv, None, kv, rows, tile)
            keep(j, h)

    @pl.loop(me + 1, n)
    def _(j):
        dkv_ref[j] = jnp.zeros(dkv_ref.shape[1:], b16)

    dq_ref[...] *= scale
    gate_out[...] = gate_sum.loc[0].astype(f32)
    up_out[...] = up_sum.loc[0].astype(f32)
    gate_sum.finish()
    up_sum.finish()


def attention_backward(queries, low, o_all, attended, lse, all_kv, doc_column, doc_row, grads):
    f32, b16 = jnp.float32, jnp.bfloat16
    kv, all_rows, _ = queries.shape
    n, rows, _ = all_kv.shape
    _, _, depth, ff = grads.shape
    out = [(queries.shape, f32), (all_kv.shape, b16), ((depth, ff), f32), ((depth, ff), f32),
           ((n, depth, attended.shape[1]), b16)]
    return pl.pallas_call(
        backward_kernel,
        out_shape=[jax.ShapeDtypeStruct(*one) for one in out],
        in_specs=[VM] * 8 + [ANY],
        out_specs=[VM] * 5,
        scratch_shapes=[pltpu.VMEM(queries.shape, b16), pltpu.VMEM((kv, 1, all_rows), f32), pltpu.VMEM((kv, 1, all_rows), f32),
                        pltpu.VMEM((rows, HEAD_SIZE), f32), pltpu.VMEM((rows, HEAD_SIZE), f32), pltpu.VMEM((rows, rows), f32)]
        + sum_scratch(depth, ff) + sum_scratch(depth, ff),
        compiler_params=pltpu.CompilerParams(vmem_limit_bytes=VMEM_BYTES, collective_id=3, has_side_effects=True),
        name="attention_backward",
    )(queries, low, o_all, attended, lse, all_kv, doc_column, doc_row, grads)


def final_kernel(dq_ref, proj_ref, norm_ref, w_ref, cos_ref, sin_ref, gains_ref, after_ref, mlp_gain_ref,
                 dkv_ref, grads_ref, o_grads_ref, tok_ref,
                 buf, down_out, o_out, q_out, k_out, v_out, gain_out,
                 dproj, part, recv, tok_own, w_grads, gain_seq, gain_line, local_sem, *scratch):
    f32, b16 = jnp.float32, jnp.bfloat16
    pieces, m, sub, width = part.shape
    n, depth, wide = w_ref.shape
    kv, all_rows, _ = dq_ref.shape
    rows = norm_ref.shape[0]
    group = all_rows // rows
    q_width, k_width = kv * group * HEAD_SIZE, kv * HEAD_SIZE
    piece = m * sub
    me, t = lax.axis_index("seq"), lax.axis_index("tp")
    tile = cut(rows)
    kv_sum = seq_sum(lambda j: dkv_ref.at[j], scratch[:6])
    down_sum = seq_sum(lambda j: grads_ref.at[j, 0], scratch[6:12])
    o_sum = seq_sum(lambda j: o_grads_ref.at[j], scratch[12:18])
    w_sum = seq_sum(lambda j: w_grads.at[j], scratch[18:24])
    in_sum = LineSum(part, recv, scratch[24], scratch[25])
    out_gather = LineGather(buf, scratch[26], scratch[27])
    gain_gather = SeqGather(gain_seq, scratch[28], scratch[29], halves=1)
    gain_total = LineGather(gain_line, scratch[30], scratch[31])

    own = [pltpu.make_async_copy(tok_ref.at[p, t], tok_own.at[p], local_sem.at[p]) for p in range(pieces)]
    for copy in own:
        copy.start()
    greet(True, True)
    kv_sum.begin()
    gain_q, gain_k = gains_ref[0, 2:3, :HEAD_SIZE], gains_ref[0, 3:4, :HEAD_SIZE]
    for j in range(1, n):
        gain_q = gain_q + gains_ref[j, 2:3, :HEAD_SIZE]
        gain_k = gain_k + gains_ref[j, 3:4, :HEAD_SIZE]
    gain_seq[me] = jnp.zeros(gain_seq.shape[1:], f32)
    gain_seq[me, 1:2] = mlp_gain_ref[...]
    for p in range(pieces):
        in_sum.clear(p)
    for copy in own:
        copy.wait()
    plan = Plan()

    def head_back(grad, at, first, gain):
        e = grad * cos_ref[at] - pltpu.roll(grad, HEAD_SIZE // 2, 1) * sin_ref[at]
        u = proj_ref[at, first:first + HEAD_SIZE]
        inverse = rms_inverse(u)
        normed = u * inverse
        scaled = e * gain
        back = inverse * (scaled - normed * jnp.mean(scaled * normed, axis=-1, keepdims=True))
        dproj[at, first:first + HEAD_SIZE] = back.astype(b16)
        return jnp.sum(e * normed, axis=0, keepdims=True)

    def queries_back(h, g):
        terms = jnp.zeros((1, HEAD_SIZE), f32)
        for start in range(0, rows, tile):
            grad = dq_ref[h, g * rows + start:g * rows + start + tile]
            terms += head_back(grad, slice(start, start + tile), (h * group + g) * HEAD_SIZE, gain_q)
        gain_seq[me, 2:3, :HEAD_SIZE] += terms

    def keys_back():
        for h in range(kv):
            cols = slice(h * HEAD_SIZE, (h + 1) * HEAD_SIZE)
            terms = jnp.zeros((1, HEAD_SIZE), f32)
            for start in range(0, rows, tile):
                at = slice(start, start + tile)
                terms += head_back(kv_sum.loc[0, at, cols].astype(f32), at, q_width + h * HEAD_SIZE, gain_k)
            gain_seq[me, 3:4, :HEAD_SIZE] += terms
        dproj[:, q_width + k_width:] = kv_sum.loc[0, :, k_width:]

    def in_part(p):
        for j in range(n):
            block = mm(dproj[p * piece:(p + 1) * piece], w_ref[j], NT)
            part[p, :, :, j * depth:(j + 1) * depth] = block.astype(b16).reshape(m, sub, depth)

    def weight_grads(j):
        w_grads[j] = mm(norm_ref[:, j * depth:(j + 1) * depth], dproj[...], TN).astype(b16)

    def norm_back(p):
        grad = in_sum.total(p)
        tok = tok_own[p].astype(f32)
        inverse = rms_inverse(tok)
        normed = tok * inverse
        mean = 0.0
        for j in range(n):
            cols = slice(j * depth, (j + 1) * depth)
            gain_seq[me, 0:1, cols] += jnp.sum(grad[:, cols] * normed[:, cols], axis=0, keepdims=True)
            mean = mean + jnp.sum(grad[:, cols] * gains_ref[j, 0:1, :depth] * normed[:, cols], axis=1, keepdims=True)
        mean = mean * (1.0 / width)
        for j in range(n):
            cols = slice(j * depth, (j + 1) * depth)
            back = inverse * (grad[:, cols] * gains_ref[j, 0:1, :depth] - normed[:, cols] * mean)
            buf[p, t, :, cols] = (after_ref[p, :, cols] + back).astype(b16)
        out_gather.start(p)

    def plan_sum(one, base, length):
        for e in reversed(range(one.count)):
            plan.at(base, one.meet, e)
        for k, found in enumerate(one.rounds()):
            for event in found:
                plan.at(base + length * (2.0 - 0.5 ** k), one.arrive, *event)

    for h in range(kv):
        for g in range(group):
            plan.at(1.0, queries_back, h, g)
    plan_sum(kv_sum, 7.0, 18.0)
    plan.at(33.0, down_sum.begin)
    plan.at(33.5, o_sum.begin)
    plan.at(43.5, keys_back)
    clock = 44.0
    hop = 8.0
    last = 0.0
    for p in range(pieces):
        plan.at(clock, in_part, p)
        clock += 2.2
        start = 47.0 + 3 * hop * p
        for k in range(m - 1):
            plan.at(start + hop * k, in_sum.step, p, k)
        start += hop * (m - 1) + 1
        plan.at(start, norm_back, p)
        for d in range(1, m):
            last = start + hop * d
            plan.at(last, out_gather.arrive, p, d)
    for j in range(n):
        plan.at(50.0 + 0.8 * j, weight_grads, j)
    plan.at(57.0, w_sum.begin)
    plan_sum(down_sum, 48.0, 18.0)
    plan_sum(o_sum, 49.0, 18.0)
    plan_sum(w_sum, 76.0, 20.0)
    gain_time = last - 3 * hop + 0.5
    plan.at(gain_time, gain_gather.start, 0)
    for k, event in enumerate(gain_gather.events()):
        plan.at(gain_time + 1.0 + 0.5 * k, gain_gather.arrive, *event)

    def over_tp():
        total = gain_seq[0]
        for j in range(1, n):
            total = total + gain_seq[j]
        gain_line[0, t] = total
        gain_total.start(0)

    plan.at(gain_time + 1.0 + 0.5 * n, over_tp)
    for d in range(1, m):
        plan.at(gain_time + 2.0 + 0.5 * n + 2.0 * d, gain_total.arrive, 0, d)
    plan.run()

    total = gain_line[0, 0]
    for j in range(1, m):
        total = total + gain_line[0, j]
    gain_out[...] = total
    down_out[...] = down_sum.loc[0].astype(f32).T
    o_out[...] = o_sum.loc[0].astype(f32).T
    q_out[...] = w_sum.loc[0, :, :q_width].astype(f32)
    k_out[...] = w_sum.loc[0, :, q_width:q_width + k_width].astype(f32)
    v_out[...] = w_sum.loc[0, :, q_width + k_width:].astype(f32)
    for one in (kv_sum, down_sum, o_sum, w_sum, gain_gather):
        one.finish()
    in_sum.finish(pieces - 1)
    for p in range(pieces):
        out_gather.finish(p)
    gain_total.finish(0)


def final(grad_queries, projected, normalized, w_all, cosines, sines, gains, after_grad, mlp_gain, grad_kv, grads, o_grads, tokens):
    f32, b16 = jnp.float32, jnp.bfloat16
    pieces, m, sub, width = tokens.shape
    n, depth, wide = w_all.shape
    kv, all_rows, _ = grad_queries.shape
    rows, k_width = normalized.shape[0], kv * HEAD_SIZE
    q_width = wide - 2 * k_width
    ff = grads.shape[3]
    out = [(tokens.shape, b16), ((ff, depth), f32), ((q_width, depth), f32), ((depth, q_width), f32), ((depth, k_width), f32),
           ((depth, k_width), f32), ((8, width), f32)]
    return pl.pallas_call(
        final_kernel,
        out_shape=[jax.ShapeDtypeStruct(*one) for one in out],
        in_specs=[VM] * 9 + [ANY] * 4,
        out_specs=[VM] * 7,
        scratch_shapes=[pltpu.VMEM((rows, wide), b16), pltpu.VMEM(tokens.shape, b16),
                        pltpu.VMEM((pieces, m + 1, sub, width), b16), pltpu.VMEM((pieces, sub, width), b16),
                        pltpu.VMEM((n, depth, wide), b16), pltpu.VMEM((n, 8, width), f32), pltpu.VMEM((1, m, 8, width), f32),
                        pltpu.SemaphoreType.DMA((pieces,))]
        + sum_scratch(rows, 2 * k_width) + sum_scratch(depth, ff) + sum_scratch(depth, q_width) + sum_scratch(depth, wide)
        + line_sems(pieces) + gather_sems(1) + line_sems(1)[2:],
        compiler_params=pltpu.CompilerParams(vmem_limit_bytes=VMEM_BYTES, collective_id=4, has_side_effects=True),
        name="final",
    )(grad_queries, projected, normalized, w_all, cosines, sines, gains, after_grad, mlp_gain, grad_kv, grads, o_grads, tokens)


def pack_gains(attn_gain, mlp_gain, query_gain, key_gain):
    width = max(attn_gain.shape[0], HEAD_SIZE)
    place = lax.axis_index("seq") * query_gain.shape[0]

    def placed(gain):
        return lax.dynamic_update_slice(jnp.zeros((width,), jnp.float32), gain.astype(jnp.float32), (place,))

    def padded(gain):
        return jnp.pad(gain.astype(jnp.float32), (0, width - gain.shape[0]))

    lines = [padded(attn_gain), padded(mlp_gain), placed(query_gain), placed(key_gain)]
    return jnp.stack(lines + [jnp.zeros((width,), jnp.float32)] * 4)


def norm_rows(values, gain_vec):
    return values * lax.rsqrt(jnp.mean(values * values, axis=-1, keepdims=True) + EPS) * gain_vec


def norm_back(values, gain_vec, grad_out):
    inverse = lax.rsqrt(jnp.mean(values * values, axis=-1, keepdims=True) + EPS)
    normed = values * inverse
    scaled = grad_out * gain_vec
    grad_in = inverse * (scaled - normed * jnp.mean(scaled * normed, axis=-1, keepdims=True))
    return (grad_in, grad_out * normed)


def rope_tables(positions, head_dim):
    half_dim = head_dim // 2
    frequency = BASE ** (-2.0 * jnp.arange(half_dim, dtype=jnp.float32) / head_dim)
    angles = positions.astype(jnp.float32)[:, None] * frequency[None, :]
    return (jnp.cos(angles)[:, None, :], jnp.sin(angles)[:, None, :])


def rotate(values, cosines, sine_values, direction):
    half_dim = values.shape[-1] // 2
    lower_half = values[..., :half_dim]
    upper_half = values[..., half_dim:]
    signed = sine_values * direction
    return jnp.concatenate(
        [lower_half * cosines - upper_half * signed, upper_half * cosines + lower_half * signed],
        axis=-1,
    )


def per_device(
    tokens,
    q_weight,
    key_matrix,
    value_matrix,
    o_weight,
    gate_weight,
    up_weight,
    down_weight,
    attn_gain,
    mlp_gain,
    query_gain,
    key_gain,
    positions,
    seq_ids,
    cotangent,
):
    f32 = jnp.float32
    b16 = jnp.bfloat16
    local_rows = tokens.shape[0]
    q_local = q_weight.shape[1] // HEAD_SIZE
    kv_local = key_matrix.shape[1] // HEAD_SIZE
    heads_per_group = q_local // kv_local
    share_rows = local_rows // lax.axis_size("tp")
    share_start = lax.axis_index("tp") * share_rows
    s = lax.axis_index("seq")
    own_docs = lax.dynamic_slice_in_dim(seq_ids, s * local_rows, local_rows)
    doc_column, doc_row = own_docs[:, None], own_docs[None, :]
    seq_count = lax.axis_size("seq")
    gains = pack_gains(attn_gain, mlp_gain, query_gain, key_gain)
    cosines, sine_values = rope_tables(positions, HEAD_SIZE)
    cos_wide = jnp.concatenate([cosines, cosines], axis=-1).reshape(local_rows, HEAD_SIZE)
    sin_wide = jnp.concatenate([-sine_values, sine_values], axis=-1).reshape(local_rows, HEAD_SIZE)
    (normalized_input, projected, queries_h, all_kv, attended_low, lse, all_gains, w_all, o_all, gate_all) = forward_attention(
        tokens, q_weight, key_matrix, value_matrix, gains, cos_wide, sin_wide, doc_column, doc_row, o_weight, gate_weight)
    model = tokens.shape[1]
    ff = gate_weight.shape[1]
    q_width, k_width = q_local * HEAD_SIZE, kv_local * HEAD_SIZE
    tp_count = lax.axis_size("tp")
    sub = math.gcd(local_rows // tp_count, 64)
    while local_rows // tp_count // sub > 3:
        sub *= 2
    split = (local_rows // tp_count // sub, tp_count, sub, model)
    low_b, after_grad_own, mlp_part, mlp_gain_own, mlp_grads = middle(
        attended_low, o_all, gate_all, up_weight, down_weight, tokens.reshape(split), cotangent.reshape(split), all_gains)
    grad_after_low = low_b.reshape(local_rows, model)
    layer_out = lax.psum(mlp_part, "tp").reshape(local_rows, model)

    grad_query_h, grad_kv, grad_gate_w, grad_up_w, o_grads = attention_backward(
        queries_h, grad_after_low, o_all, attended_low, lse, all_kv, doc_column, doc_row, mlp_grads)
    grad_tokens, grad_down, grad_o_w, grad_q_w, grad_k_w, grad_v_w, gain_sums = final(
        grad_query_h, projected, normalized_input, w_all, cos_wide, sin_wide, all_gains, after_grad_own, mlp_gain_own,
        grad_kv, mlp_grads, o_grads, tokens.reshape(split))

    def own_part(line, width):
        count = width // seq_count
        return lax.dynamic_slice_in_dim(gain_sums[line], s * count, count)

    return (
        layer_out,
        grad_tokens.reshape(local_rows, model).astype(f32),
        grad_q_w,
        grad_k_w,
        grad_v_w,
        grad_o_w,
        grad_gate_w,
        grad_up_w,
        grad_down,
        own_part(0, model),
        own_part(1, model),
        own_part(2, HEAD_SIZE),
        own_part(3, HEAD_SIZE),
    )


def solution(mesh):
    placed = (
        P("seq", None),
        P("seq", "tp"),
        P("seq", "tp"),
        P("seq", "tp"),
        P("tp", "seq"),
        P("seq", "tp"),
        P("seq", "tp"),
        P("tp", "seq"),
        P("seq"),
        P("seq"),
        P("seq"),
        P("seq"),
        P("seq"),
        P(),
        P("seq", None),
    )
    return jax.shard_map(
        per_device,
        mesh=mesh,
        in_specs=placed,
        out_specs=(
            P("seq", None),
            P("seq", None),
            P("seq", "tp"),
            P("seq", "tp"),
            P("seq", "tp"),
            P("tp", "seq"),
            P("seq", "tp"),
            P("seq", "tp"),
            P("tp", "seq"),
            P("seq"),
            P("seq"),
            P("seq"),
            P("seq"),
        ),
        check_vma=False,
    )
```

time: 1760 us -> 703 us (0.40)
  waiting for transfers between devices: 993 us -> 0.02 us
  Pallas kernels: 0 us -> 652 us
  matrix products: 438 us -> 0 us
  other arithmetic: 137 us -> 11.4 us
  local copies, waits for them, and re-layouts: 78.1 us -> 17 us
  blocking collectives: 57.4 us -> 0 us
  loops' own time: 25.3 us -> 0 us
    pallas_call x0 -> x4, Pallas kernels: none -> 652 us  [the longest x1 258 us: middle(): pl.pallas_call(middle_kernel, out_shape=[jax.ShapeDtypeStruct(*one) for o...]
    psum x3 -> x1, waiting for transfers between devices: 456 us -> 0.01 us  [per_device(): layer_out = lax.psum(mlp_part, 'tp').reshape(local_rows, model)]
    dot_general x105 -> x0, matrix products: 438 us -> none  [the longest x24 115 us: block_scores(): jnp.einsum('lkgd,mkd->kglm', grouped_queries, keys_blk, preferred_element...]
    reduce_scatter x9 -> x0, waiting for transfers between devices: 361 us -> none  [the longest x1 63.2 us: per_device(): lax.psum_scatter(grad_gate_w.astype(jnp.bfloat16), 'seq', scatter_dimensi...]
    all_gather x9 -> x0, waiting for transfers between devices: 170 us -> none  [the longest x1 38.8 us: per_device(): lax.all_gather(down_weight, 'seq', axis=1, tiled=True)]
    reduce_sum x23 -> x0, other arithmetic: 72.6 us -> none  [the longest x12 49.7 us: stat_step(): row_sum = row_sum * jnp.exp(row_max - new_max) + jnp.sum(weights, axis=-1)]
    dynamic_slice x73 -> x5, local copies, waits for them, and re-layouts: 49.5 us -> 3.07 us  [the longest x4 2.29 us: own_part(): return lax.dynamic_slice_in_dim(gain_sums[line], s * count, count)]
    unnamed x2 -> x0, blocking collectives: 27.9 us -> none
  transfers between devices with their start and end apart: 21 -> 1, of which waited for: 17 -> 0; matrix products, arithmetic and copies ran while one was open for 20% -> 1% of each run, Pallas kernels for 0% -> 39%
where the time goes in v2:
time: 703 us; the launch traced here: 694 us
  Pallas kernels  652 us (93%)
  local copies, waits for them, and re-layouts  17 us (2%)
  between operations  14.4 us (2%)
  other arithmetic  11.4 us (2%)
    pallas_call x1, Pallas kernels, middle(): pl.pallas_call(middle_kernel, out_shape=[jax.ShapeDtypeStruct(*one) for o...  258 us
    pallas_call x1, Pallas kernels, final(): pl.pallas_call(final_kernel, out_shape=[jax.ShapeDtypeStruct(*one) for on...  193 us
    pallas_call x1, Pallas kernels, forward_attention(): pl.pallas_call(forward_kernel, out_shape=[jax.ShapeDtypeStruct(*one) for...  121 us
    pallas_call x1, Pallas kernels, attention_backward(): pl.pallas_call(backward_kernel, out_shape=[jax.ShapeDtypeStruct(*one) for...  80.6 us
  transfers between devices with their start and end apart: 1, of which 0 were waited for; matrix products, arithmetic and copies ran while one was open for 1% of the time, Pallas kernels for 39%

profile of v2, /device:TPU:0, one launch (start us, length us, event | category | flops | bytes accessed | tf_op | source)
XLA Modules:
  0.0 694.4 jit_solution(3117358688265905632)
XLA Ops:
  7.2 0.0 all-reduce.2.cloned.1.call-start
  7.2 0.8 dynamic_slice.23
  8.0 0.6 broadcast_in_dim.5.kd_ref.qdr_ref
  8.6 0.9 broadcast_in_dim.12.qd_ref.kd_ref
  9.5 0.7 bitcast_convert_fusion.2
  10.2 0.7 bitcast_convert_fusion.1
  10.8 0.7 stack.41
  11.5 0.7 stack.42
  12.2 0.7 convert_element_type.13
  12.8 0.1 dynamic_update_slice.8
  12.9 0.2 dynamic_update_slice.9
  13.1 1.4 fusion
  14.6 1.2 maximum_bitcast_fusion
  15.7 0.6 stack.40.gain_ref
  16.3 120.6 %forward_attention.1 = (bf16[768,2048]{1,0:T(8,128)(2,1)}, f32[768,1024]{1,0:T(8,128)}, bf16[2,1536,128]{2,1,0:T(8,128)(2,1)}, bf16[8,768,512]{2,1,0:T(8,128)(2,...) custom-call(bf16[768,2048]{1,0:T(8,128)(2,1)} %tok_ref.1, ...), custom_call_target="tpu_custom_call" | custom-call | tf_op jit(solution)/shard_map/forward_attention/pallas_call | solution.py:452
  136.9 257.5 %middle.1 = (bf16[3,4,64,2048]{3,2,1,0:T(8,128)(2,1)}, f32[3,64,2048]{2,1,0:T(8,128)}, bf16[3,4,64,2048]{3,2,1,0:T(8,128)(2,1)}, f32[1,2048]{1,0:T(1,128)}, bf16[8,3,256,1536]{3,2,1,0:T(8,128)(2,1)}) custom-call(bf16[768,512]{1,0:T(8,128)(2,1)} %get-tuple-element.40.att_ref, bf16[8,512,256]{2,1,0:T(8,128)(2,1)} %get-tuple-element.41.o_all, ...), custom_call_target="tpu_custom_call" | custom-call | tf_op jit(solution)/shard_map/middle/pallas_call | solution.py:734
  394.4 0.0 all-reduce.2.cloned.1.call-update
  394.5 80.6 %attention_backward.1 = (f32[2,1536,128]{2,1,0:T(8,128)}, bf16[8,768,512]{2,1,0:T(8,128)(2,1)}, f32[256,1536]{1,0:T(8,128)}, f32[256,1536]{1,0:T(8,128)}, bf16[8,256,512]{2,1,0:T(8,128)(2,1)}) custom-call(bf16[2,1536,128]{2,1,0:T(8,128)(2,1)} %get-tuple-element.45.q_ref, bf16[768,2048]{1,0:T(8,128)(2,1)} %bitcast.28, ...), custom_call_target="tpu_custom_call" | custom-call | tf_op jit(solution)/shard_map/attention_backward/pallas_call | solution.py:877
  475.1 192.9 %final.1 = (bf16[3,4,64,2048]{3,2,1,0:T(8,128)(2,1)}, f32[1536,256]{1,0:T(8,128)}, f32[512,256]{1,0:T(8,128)}, f32[256,512]{1,0:T(8,128)}, f32[256,256]{1,0:T(8,...) custom-call(f32[2,1536,128]{2,1,0:T(8,128)} %get-tuple-element.50.dq_ref, f32[768,1024]{1,0:T(8,128)} %get-tuple-element.51.proj_ref, ...), custom_call_target="tpu_custom_call" | custom-call | tf_op jit(solution)/shard_map/final/pallas_call | solution.py:1060
  668.0 1.0 fusion.3
  669.0 0.6 fusion.2
  669.6 0.6 fusion.1
  670.2 0.6 constant_dynamic-slice_fusion.2
  670.8 0.6 constant_dynamic-slice_fusion.3
  671.3 5.4 bitcast_convert_fusion
  676.8 0.0 all-reduce.2.cloned.1.call-done
  676.8 0.0 copy-start.4
  676.8 0.0 copy-start.6
  676.8 0.0 copy-start.5
  676.8 0.0 copy-start.3
  676.8 0.0 copy-start.1
  676.8 4.1 copy.41
  680.9 0.0 copy-done.4
  680.9 0.0 copy-start
  680.9 0.8 copy.42
  681.7 0.0 copy-done.6
  681.7 0.7 copy.43
  682.4 0.0 copy-done.5
  682.4 0.7 copy.44
  683.1 0.0 copy-done.3
  683.1 0.8 copy.45
  683.9 0.0 copy-done.1
  683.9 0.0 copy-start.2
  683.9 1.1 copy.46
  685.1 0.0 copy-done
  685.1 1.1 copy.47
  686.2 0.0 copy-done.2
  686.2 1.1 copy.48
  (4 shorter events, 0.0 us)
Async XLA Ops:
  7.2 669.6 %all-reduce.2.cloned.1.call-start = ((), (), s32[]{:S(2)}) async-start(), calls=%async_computation | async-start | bytes 6291456 | tf_op jit(solution)/shard_map/psum | solution.py:1166
  676.8 4.2 copy-start.4
  676.8 4.9 copy-start.6
  676.8 5.7 copy-start.5
  676.8 6.4 copy-start.3
  676.8 7.1 %copy-start.1 = (f32[256,1536]{1,0:T(8,128)S(1)}, f32[256,1536]{1,0:T(8,128)}, u32[]{:S(2)}) copy-start(f32[256,1536]{1,0:T(8,128)} %get-tuple-element.95) | copy-start | bytes 4718596
  680.9 4.2 copy-start
  683.9 2.3 copy-start.2
Sparse Core Ops, SparseCore 0:
  394.6 120.1 all-reduce.1

commit v3 on v2

--- a/solution.py
+++ b/solution.py
@@ -63,7 +63,13 @@
         for bit in range(seq_bits()):
             pl.semaphore_signal(barrier, inc=1, device_id=(toggled(s, 1 << bit, seq_bits()), t), device_id_type=MESH)
         expected = seq_bits()
-    if over_tp:
+    if over_tp == "all":
+        for j in range(count):
+            @pl.when(t != j)
+            def _(j=j):
+                pl.semaphore_signal(barrier, inc=1, device_id=(s, j), device_id_type=MESH)
+        expected = expected + count - 1
+    elif over_tp:
         @pl.when(t > 0)
         def _():
             pl.semaphore_signal(barrier, inc=1, device_id=(s, t - 1), device_id_type=MESH)
@@ -112,12 +118,13 @@
             for offset in range(1, self.n):
                 self.copy(half, offset).wait_send()
 
+    def level(self, half, offset):
+        order = bit_order(half)
+        return sum(2 ** order.index(b) for b in range(1, self.bits) if offset >> b & 1)
+
     def events(self):
         def due(event):
-            half, offset = event
-            order = bit_order(half)
-            steps = [order.index(b) for b in range(1, self.bits) if offset >> b & 1]
-            return (sum(2 ** k for k in steps), offset & 1, half)
+            return self.level(*event), event[1] & 1, event[0]
         return sorted(((h, r) for h in range(self.halves) for r in range(1, self.n)), key=due)
 
 
@@ -202,6 +209,38 @@
         @pl.when(self.t < self.m - 1)
         def _():
             self.copy(p, self.t + 1, 0, self.t).wait_send()
+
+
+class DirectSum:
+    def __init__(self, part, recv, send_sem, recv_sem):
+        self.part, self.recv, self.send_sem, self.recv_sem = part, recv, send_sem, recv_sem
+        self.m = part.shape[1]
+        self.s, self.t = lax.axis_index("seq"), lax.axis_index("tp")
+
+    def copy(self, p, j, sender):
+        return pltpu.make_async_remote_copy(
+            src_ref=self.part.at[p, j], dst_ref=self.recv.at[p, sender], send_sem=self.send_sem.at[p, j],
+            recv_sem=self.recv_sem.at[p, sender], device_id=(self.s, j), device_id_type=MESH)
+
+    def others(self, act):
+        for j in range(self.m):
+            @pl.when(self.t != j)
+            def _(j=j):
+                act(j)
+
+    def start(self, p):
+        self.others(lambda j: self.copy(p, j, self.t).start())
+        self.recv[p, self.t] = self.part[p, self.t]
+
+    def total(self, p):
+        self.others(lambda j: self.copy(p, j, j).wait_recv())
+        total = self.recv[p, 0].astype(jnp.float32)
+        for j in range(1, self.m):
+            total = total + self.recv[p, j].astype(jnp.float32)
+        return total
+
+    def finish(self, p):
+        self.others(lambda j: self.copy(p, j, self.t).wait_send())
 
 
 class LineGather:
@@ -290,7 +329,7 @@
 
 
 def forward_kernel(tok_ref, wq_ref, wk_ref, wv_ref, gain_ref, cos_ref, sin_ref, qd_ref, kd_ref, o_ref, gate_ref,
-                   norm_ref, proj_ref, q_ref, kv_ref, att_ref, lse_ref, gains_ref, w, o_all, gate_all,
+                   norm_ref, proj_ref, q_ref, kv_ref, att_all, lse_ref, gains_ref, w, o_all, gate_all,
                    inv, acc, total, bias, local_sem, *sems):
     f32, b16 = jnp.float32, jnp.bfloat16
     n, rows, _ = kv_ref.shape
@@ -306,21 +345,27 @@
     kv_gather = SeqGather(kv_ref, sems[4], sems[5])
     o_gather = SeqGather(o_all, sems[6], sems[7])
     gate_gather = SeqGather(gate_all, sems[8], sems[9])
+    o_line = LineGather(o_all.at[pl.ds(me, 1)], sems[10], sems[11])
+    att_gather = LineGather(att_all, sems[12], sems[13])
+    t, m = lax.axis_index("tp"), lax.axis_size("tp")
+    pieces, _, piece, _ = att_all.shape
 
     own = [pltpu.make_async_copy(wq_ref, w.at[me, :, pl.ds(0, q_width)], local_sem.at[0]),
            pltpu.make_async_copy(wk_ref, w.at[me, :, pl.ds(q_width, k_width)], local_sem.at[1]),
            pltpu.make_async_copy(wv_ref, w.at[me, :, pl.ds(q_width + k_width, k_width)], local_sem.at[2]),
-           pltpu.make_async_copy(o_ref, o_all.at[me], local_sem.at[3]),
+           pltpu.make_async_copy(o_ref, o_all.at[me, t], local_sem.at[3]),
            pltpu.make_async_copy(gate_ref, gate_all.at[me], local_sem.at[4])]
     for copy in own:
         copy.start()
     gains_ref[me] = gain_ref[...]
-    greet(True, False)
+    greet(True, True)
     for copy in own[:3]:
         copy.wait()
     w_gather.start(0)
     w_gather.start(1)
     gain_gather.start(0)
+    own[3].wait()
+    o_line.start(0)
 
     @pl.loop(0, rows // tile)
     def _(i):
@@ -350,12 +395,16 @@
 
     project(0)
     came = {}
-    for half, offset in w_gather.events():
+    hops = [len(w_gather.events()) * d // m for d in range(1, m)]
+    for i, (half, offset) in enumerate(w_gather.events()):
+        if i in hops:
+            o_line.arrive(0, hops.index(i) + 1)
         w_gather.arrive(half, offset)
         came[offset] = came.get(offset, 0) + 1
         if came[offset] == 2:
             project(offset)
 
+    own[4].wait()
     gain_q, gain_k = gains_ref[0, 2:3, :HEAD_SIZE], gains_ref[0, 3:4, :HEAD_SIZE]
     for j in range(1, n):
         gain_q = gain_q + gains_ref[j, 2:3, :HEAD_SIZE]
@@ -386,9 +435,6 @@
     acc[...] = jnp.zeros_like(acc)
     total[...] = jnp.zeros_like(total)
     attn_fwd_block(q_ref, kv_ref.at[me], acc.at[0], total.at[0], bias, kv, rows, tile)
-    own[3].wait()
-    own[4].wait()
-
     kv_steps = [[] for _ in range(n)]
     seen = set()
     order = kv_gather.events()
@@ -400,6 +446,19 @@
         taken = max(need, taken)
     only_first = jnp.where(qd_ref[...] == 0, 1.0, 0.0)
 
+    def attended(p):
+        for h in range(kv):
+            for g in range(group):
+                for start in range(p * piece, (p + 1) * piece, tile):
+                    at = slice(g * rows + start, g * rows + start + tile)
+                    total_row = total[0, h, at] + total[1, h, at] * only_first[start:start + tile]
+                    out = acc[0, h, at] + acc[1, h, at] * only_first[start:start + tile]
+                    cols = slice((h * group + g) * HEAD_SIZE, (h * group + g + 1) * HEAD_SIZE)
+                    out = (out / jnp.sum(total_row, axis=1, keepdims=True)).astype(b16)
+                    att_all[p, t, start - p * piece:start - p * piece + tile, cols] = out
+                    lse_ref[h, :, at] = jnp.log2(jnp.sum(total_row.T, axis=0, keepdims=True))
+        att_gather.start(p)
+
     @pl.loop(0, n - 1)
     def _(k):
         source = 0
@@ -410,7 +469,7 @@
             def _(i=i):
                 for event in kv_steps[i]:
                     kv_gather.arrive(*event)
-                if i == n - 2:
+                if i == max(n - 6, 0):
                     for gather in (o_gather, gate_gather):
                         gather.start(0)
                         gather.start(1)
@@ -419,24 +478,24 @@
         def _():
             attn_fwd_block(q_ref, kv_ref.at[source], acc.at[1], total.at[1], None, kv, rows, tile)
 
+    plan = Plan()
+    for p in range(pieces):
+        plan.at(p, attended, p)
+        for d in range(1, m):
+            plan.at(pieces + 6.0 * (pieces * (d - 1) + p + 1), att_gather.arrive, p, d)
     for gather in (o_gather, gate_gather):
         for event in gather.events():
-            gather.arrive(*event)
-    for h in range(kv):
-        for g in range(group):
-            for start in range(0, rows, tile):
-                at = slice(g * rows + start, g * rows + start + tile)
-                t = total[0, h, at] + total[1, h, at] * only_first[start:start + tile]
-                out = acc[0, h, at] + acc[1, h, at] * only_first[start:start + tile]
-                cols = slice((h * group + g) * HEAD_SIZE, (h * group + g + 1) * HEAD_SIZE)
-                att_ref[start:start + tile, cols] = (out / jnp.sum(t, axis=1, keepdims=True)).astype(b16)
-                lse_ref[h, :, at] = jnp.log2(jnp.sum(t.T, axis=0, keepdims=True))
+            plan.at((4.0, 25.0, 42.0, 48.0)[min(gather.level(*event), 3)], gather.arrive, *event)
+    plan.run()
+    o_line.finish(0)
+    for p in range(pieces):
+        att_gather.finish(p)
     for gather in (w_gather, gain_gather, kv_gather, o_gather, gate_gather):
         gather.finish()
 
 
-def forward_attention(tokens, q_weight, key_matrix, value_matrix, gains, cosines, sines, doc_column, doc_row, o_weight, gate_weight):
-    n = lax.axis_size("seq")
+def forward_attention(tokens, q_weight, key_matrix, value_matrix, gains, cosines, sines, doc_column, doc_row, o_weight, gate_weight, pieces):
+    n, m = lax.axis_size("seq"), lax.axis_size("tp")
     rows, width = tokens.shape
     depth, q_width = q_weight.shape
     k_width = key_matrix.shape[1]
@@ -444,11 +503,12 @@
     f32, b16 = jnp.float32, jnp.bfloat16
     wide = q_width + 2 * k_width
     heads = (kv, group * rows, HEAD_SIZE)
-    out = [((rows, width), b16), ((rows, wide), f32), (heads, b16), ((n, rows, 2 * k_width), b16), ((rows, q_width), b16),
-           ((kv, 1, group * rows), f32), ((n,) + gains.shape, f32), ((n, depth, wide), b16), ((n,) + o_weight.shape, b16), ((n,) + gate_weight.shape, b16)]
+    out = [((rows, width), b16), ((rows, wide), f32), (heads, b16), ((n, rows, 2 * k_width), b16), ((pieces, m, rows // pieces, q_width), b16),
+           ((kv, 1, group * rows), f32), ((n,) + gains.shape, f32), ((n, depth, wide), b16), ((n, m) + o_weight.shape, b16), ((n,) + gate_weight.shape, b16)]
     sems = []
     for halves in (2, 1, 2, 2, 2):
         sems += gather_sems(halves)
+    sems += line_sems(1)[2:] + line_sems(pieces)[2:]
     return pl.pallas_call(
         forward_kernel,
         out_shape=[jax.ShapeDtypeStruct(*one) for one in out],
@@ -540,10 +600,10 @@
     return SeqSum(source, *scratch[:3], scratch[3:])
 
 
-def middle_kernel(att_ref, o_all, gate_all, up_ref, down_ref, tok_ref, cot_ref, gains_ref,
-                  low_ref, after_grad_ref, mlp_ref, gain_out, grads_ref,
-                  up_all, down_all, part, recv, norm_mid, act, gg, gu, after_own, tok_own, stage,
-                  local_sem, stage_sem, *sems):
+def middle_kernel(att_ref, o_ref, gate_ref, up_ref, down_ref, tok_ref, cot_in, gains_ref,
+                  low_ref, after_grad_ref, do_ref, gain_out, mlp_ref, grads_ref,
+                  o_all, gate_all, up_all, down_all, cot_ref, part, recv, norm_mid, act, gg, gu, after, after_own, att, rows_buf,
+                  do_send, stage, local_sem, att_sem, rows_sem, stage_sem, do_send_sem, do_recv_sem, *sems):
     f32, b16 = jnp.float32, jnp.bfloat16
     pieces, m, sub, width = cot_ref.shape
     n, depth, ff = gate_all.shape
@@ -551,23 +611,34 @@
     me, t = lax.axis_index("seq"), lax.axis_index("tp")
     up_gather = SeqGather(up_all, sems[0], sems[1])
     down_gather = SeqGather(down_all, sems[2], sems[3])
-    attn_sum = LineSum(part, recv, sems[4], sems[5])
-    mid_sum = LineSum(part, recv, sems[8], sems[9])
-    norm_gather = LineGather(norm_mid, sems[6], sems[7])
-    low_gather = LineGather(low_ref, sems[10], sems[11])
-
-    own = [pltpu.make_async_copy(up_ref, up_all.at[me], local_sem.at[0]),
-           pltpu.make_async_copy(down_ref, down_all.at[me], local_sem.at[1])]
-    own += [pltpu.make_async_copy(tok_ref.at[p, t], tok_own.at[p], local_sem.at[2 + p]) for p in range(pieces)]
-    for copy in own:
+    mid_sum = DirectSum(part, recv, sems[4], sems[5])
+
+    whole = [pltpu.make_async_copy(up_ref, up_all.at[me], local_sem.at[0]),
+             pltpu.make_async_copy(down_ref, down_all.at[me], local_sem.at[1]),
+             pltpu.make_async_copy(o_ref, o_all, local_sem.at[2]),
+             pltpu.make_async_copy(gate_ref, gate_all, local_sem.at[3]),
+             pltpu.make_async_copy(cot_in, cot_ref, local_sem.at[4])]
+
+    def att_copy(p):
+        return pltpu.make_async_copy(att_ref.at[p], att, att_sem.at[0])
+
+    def tok_copy(p):
+        return pltpu.make_async_copy(tok_ref.at[p], rows_buf.at[p % 2], rows_sem.at[p % 2])
+
+    def mlp_copy(p):
+        return pltpu.make_async_copy(rows_buf.at[p % 2], mlp_ref.at[p], rows_sem.at[p % 2])
+
+    for copy in whole:
         copy.start()
-    greet(True, True)
-    for copy in own:
+    att_copy(0).start()
+    for p in range(min(2, pieces)):
+        tok_copy(p).start()
+    greet(True, "all")
+    for copy in whole[:2]:
         copy.wait()
-    for half in range(2):
-        up_gather.start(half)
-    for p in range(pieces):
-        attn_sum.clear(p)
+    for gather in (up_gather, down_gather):
+        for half in range(2):
+            gather.start(half)
     gain_out[...] = jnp.zeros_like(gain_out)
     plan = Plan()
 
@@ -575,19 +646,27 @@
         return gains_ref[j, 1:2, :depth]
 
     def project(p):
-        rows = att_ref[p * piece:(p + 1) * piece]
-        for j in range(n):
-            block = mm(rows, o_all[j]).astype(b16)
-            part[p, :, :, j * depth:(j + 1) * depth] = block.reshape(m, sub, depth)
-
-    def normalise(p):
-        after = tok_own[p].astype(f32) + attn_sum.total(p)
-        after_own[p] = after
-        normed = after * rms_inverse(after)
+        if p == 0:
+            whole[2].wait()
+        att_copy(p).wait()
+        tok_copy(p).wait()
+        squares = jnp.zeros((piece, 1), f32)
         for j in range(n):
             cols = slice(j * depth, (j + 1) * depth)
-            norm_mid[p, t, :, cols] = (normed[:, cols] * mlp_gain(j)).astype(b16)
-        norm_gather.start(p)
+            block = rows_buf[p % 2, :, :, cols].reshape(piece, depth).astype(f32)
+            for k in range(m):
+                block = block + mm(att[k], o_all[j, k])
+            after[:, cols] = block
+            squares = squares + jnp.sum(block * block, axis=1, keepdims=True)
+        if p + 1 < pieces:
+            att_copy(p + 1).start()
+        inverse = lax.rsqrt(squares * (1.0 / width) + EPS)
+        for j in range(n):
+            cols = slice(j * depth, (j + 1) * depth)
+            norm_mid[p, :, :, cols] = (after[:, cols] * inverse * mlp_gain(j)).astype(b16).reshape(m, sub, depth)
+        after_own[p] = after[pl.ds(pl.multiple_of(t * sub, sub), sub)]
+        if p + 2 < pieces:
+            tok_copy(p + 2).start()
 
     def hidden(p, first, count):
         rows = slice(p * piece, (p + 1) * piece)
@@ -612,11 +691,37 @@
             part[p, :, :, j * depth:(j + 1) * depth] = block.astype(b16).reshape(m, sub, depth)
 
     def mlp_out(p):
+        if p >= 2:
+            mlp_copy(p - 2).wait()
         rows = slice(p * piece, (p + 1) * piece)
         for j in range(n):
             block = mm(act[rows], down_all[j]).astype(b16)
-            mlp_ref[p, :, :, j * depth:(j + 1) * depth] = block.reshape(m, sub, depth)
-        mlp_ref[p, t] = (mlp_ref[p, t].astype(f32) + after_own[p]).astype(b16)
+            rows_buf[p % 2, :, :, j * depth:(j + 1) * depth] = block.reshape(m, sub, depth)
+        rows_buf[p % 2, t] = (rows_buf[p % 2, t].astype(f32) + after_own[p]).astype(b16)
+        mlp_copy(p).start()
+
+    def do_copy(p, j):
+        return pltpu.make_async_remote_copy(
+            src_ref=do_send.at[p, j], dst_ref=do_ref.at[p, t], send_sem=do_send_sem.at[p, j], recv_sem=do_recv_sem.at[p, t],
+            device_id=(me, j), device_id_type=MESH)
+
+    def do_arrival(p, j):
+        return pltpu.make_async_remote_copy(
+            src_ref=do_send.at[p, j], dst_ref=do_ref.at[p, j], send_sem=do_send_sem.at[p, j], recv_sem=do_recv_sem.at[p, j],
+            device_id=(me, j), device_id_type=MESH)
+
+    def attended_back(p):
+        for k in range(m):
+            grad = mm(o_all[0, k], low_ref[p, :, :depth], NT)
+            for j in range(1, n):
+                grad = grad + mm(o_all[j, k], low_ref[p, :, j * depth:(j + 1) * depth], NT)
+            do_send[p, k] = grad.T.astype(b16)
+
+            @pl.when(t != k)
+            def _(k=k):
+                do_copy(p, k).start()
+
+        do_ref[p, t] = do_send[p, t]
 
     def mid_back(p):
         grad = mid_sum.total(p)
@@ -634,94 +739,68 @@
             back = inverse * (grad[:, cols] * mlp_gain(j) - normed[:, cols] * mean)
             back = back + cot_ref[p, t, :, cols].astype(f32)
             after_grad_ref[p, :, cols] = back
-            low_ref[p, t, :, cols] = back.astype(b16)
-        low_gather.start(p)
+            low_ref[p, :, cols] = back.astype(b16)
+        attended_back(p)
 
     def staged(j, slot):
-        return pltpu.make_async_copy(stage.at[slot], grads_ref.at[j], stage_sem.at[slot])
+        return pltpu.make_async_copy(stage.at[slot], grads_ref.at[j, slot], stage_sem.at[slot])
 
     def weight_grads(j):
-        slot = j % 2
-        if j >= 2:
-            staged(j - 2, slot).wait()
         cols = slice(j * depth, (j + 1) * depth)
-        x = cot_ref[:, :, :, cols].reshape(pieces * piece, depth)
-        stage[slot, 0] = mm(x, act[...], TN).astype(b16)
-        x = norm_mid[:, :, :, cols].reshape(pieces * piece, depth)
-        stage[slot, 1] = mm(x, gg[...], TN).astype(b16)
-        stage[slot, 2] = mm(x, gu[...], TN).astype(b16)
-        staged(j, slot).start()
-
-    hop = 6.0
-    ready = []
+        for slot, terms in enumerate((act, gg, gu)):
+            if slot < 2:
+                x = (cot_ref if slot == 0 else norm_mid)[:, :, :, cols].reshape(pieces * piece, depth)
+            if j:
+                staged(j - 1, slot).wait()
+            stage[slot] = mm(x, terms[...], TN).astype(b16)
+            staged(j, slot).start()
+
     for p in range(pieces):
-        plan.at(2.0 * p, project, p)
-        start = 4.0 + 3 * hop * p
-        for k in range(m - 1):
-            plan.at(start + hop * k, attn_sum.step, p, k)
-        start += hop * m
-        plan.at(start, normalise, p)
-        for d in range(1, m):
-            plan.at(start + hop * d, norm_gather.arrive, p, d)
-        ready.append(start + hop * m - 3.0)
-
-    def due(gather, event, base):
-        half, offset = event
-        order = bit_order(half)
-        steps = sum(2 ** order.index(b) for b in range(1, gather.bits) if offset >> b & 1)
-        return base + 9.0 * max(steps, 0.2)
-
-    def begin_down():
-        for half in range(2):
-            down_gather.start(half)
-
-    for event in up_gather.events():
-        plan.at(due(up_gather, event, 3.0), up_gather.arrive, *event)
-    plan.at(22.0, begin_down)
-    for event in down_gather.events():
-        plan.at(due(down_gather, event, 29.0), down_gather.arrive, *event)
+        plan.at(3.0 * p, project, p)
+
+    def loaded():
+        for copy in whole[3:]:
+            copy.wait()
+
+    plan.at(3.0 * pieces, loaded)
+    for gather in (up_gather, down_gather):
+        for event in gather.events():
+            plan.at(10.0 + gather.level(*event), gather.arrive, *event)
 
     chunk = cut(ff, 512)
     chunks = ff // chunk
     clock = 58.0
     for p in range(pieces):
-        clock = max(clock, ready[p])
         for c in range(chunks):
             plan.at(clock, hidden, p, c * chunk, chunk)
-            clock += 2.4
-
-        def reuse(p=p):
-            if p == pieces - 1:
-                attn_sum.finish(p)
-            mid_sum.clear(p)
-
-        plan.at(clock, reuse)
+            clock += 1.8
         for half in range(2):
             plan.at(clock, mid, p, half * (n // 2), n // 2)
-            clock += 2.2
-        start = max(clock, 70.0 + 3 * hop * p)
-        for k in range(m - 1):
-            plan.at(start + hop * k, mid_sum.step, p, k)
-        start += hop * m
-        plan.at(start, mid_back, p)
-        for d in range(1, m):
-            plan.at(start + hop * d, low_gather.arrive, p, d)
+            clock += 1.7
+        plan.at(clock, mid_sum.start, p)
+        arrived = 92.0 + 25.0 * p
+        plan.at(arrived, mid_back, p)
     for j in range(n):
         plan.at(clock, weight_grads, j)
-        clock += 3.5
+        clock += 2.0
     for p in range(pieces):
         plan.at(clock, mlp_out, p)
-        clock += 2.2
+        clock += 2.0
     plan.run()
 
-    for j in range(n - 2, n):
-        staged(j, j % 2).wait()
+    for slot in range(3):
+        staged(n - 1, slot).wait()
+    for p in range(max(pieces - 2, 0), pieces):
+        mlp_copy(p).wait()
     up_gather.finish()
     down_gather.finish()
-    mid_sum.finish(pieces - 1)
     for p in range(pieces):
-        norm_gather.finish(p)
-        low_gather.finish(p)
+        mid_sum.finish(p)
+        for j in range(m):
+            @pl.when(t != j)
+            def _(p=p, j=j):
+                do_arrival(p, j).wait_recv()
+                do_copy(p, j).wait_send()
 
 
 def middle(attended, o_all, gate_all, up_weight, down_weight, tokens, cotangent, gains):
@@ -730,19 +809,24 @@
     n, depth, ff = gate_all.shape
     rows = pieces * m * sub
     blocks = tokens.shape
-    out = [(blocks, b16), ((pieces, sub, width), f32), (blocks, b16), ((1, width), f32), ((n, 3, depth, ff), b16)]
+    heads = attended.shape[3]
+    out = [((pieces, sub, width), b16), ((pieces, sub, width), f32), ((pieces, m, sub, heads), b16), ((1, width), f32),
+           (blocks, b16), ((n, 3, depth, ff), b16)]
+    dma = pltpu.SemaphoreType.DMA
     return pl.pallas_call(
         middle_kernel,
         out_shape=[jax.ShapeDtypeStruct(*one) for one in out],
-        in_specs=[VM] * 3 + [ANY] * 3 + [VM] * 2,
-        out_specs=[VM] * 4 + [ANY],
-        scratch_shapes=[pltpu.VMEM((n, depth, ff), b16), pltpu.VMEM((n, ff, depth), b16), pltpu.VMEM(blocks, b16),
-                        pltpu.VMEM((pieces, m + 1, sub, width), b16), pltpu.VMEM(blocks, b16),
+        in_specs=[ANY] * 7 + [VM],
+        out_specs=[VM] * 4 + [ANY] * 2,
+        scratch_shapes=[pltpu.VMEM(o_all.shape, b16), pltpu.VMEM((n, depth, ff), b16), pltpu.VMEM((n, depth, ff), b16),
+                        pltpu.VMEM((n, ff, depth), b16), pltpu.VMEM(blocks, b16), pltpu.VMEM(blocks, b16),
+                        pltpu.VMEM(blocks, b16), pltpu.VMEM(blocks, b16),
                         pltpu.VMEM((rows, ff), b16), pltpu.VMEM((rows, ff), b16), pltpu.VMEM((rows, ff), b16),
-                        pltpu.VMEM((pieces, sub, width), f32), pltpu.VMEM((pieces, sub, width), b16),
-                        pltpu.VMEM((2, 3, depth, ff), b16), pltpu.SemaphoreType.DMA((2 + pieces,)),
-                        pltpu.SemaphoreType.DMA((2,))]
-        + gather_sems() + gather_sems() + line_sems(pieces) + line_sems(pieces),
+                        pltpu.VMEM((m * sub, width), f32), pltpu.VMEM((pieces, sub, width), f32),
+                        pltpu.VMEM(attended.shape[1:], b16), pltpu.VMEM((2, m, sub, width), b16),
+                        pltpu.VMEM((pieces, m, sub, heads), b16), pltpu.VMEM((3, depth, ff), b16),
+                        dma((5,)), dma((2,)), dma((2,)), dma((3,)), dma((pieces, m)), dma((pieces, m))]
+        + gather_sems() + gather_sems() + [dma((pieces, m)), dma((pieces, m))],
         compiler_params=pltpu.CompilerParams(vmem_limit_bytes=VMEM_BYTES, collective_id=2, has_side_effects=True),
         name="middle",
     )(attended, o_all, gate_all, up_weight, down_weight, tokens, cotangent, gains)
@@ -772,18 +856,26 @@
         dq_ref[h, start:start + tile] += mm(grad, k, TN)
 
 
-def backward_kernel(q_ref, low_ref, o_all, att_ref, lse_ref, kv_ref, kd_ref, qdr_ref, grads_ref,
-                    dq_ref, dkv_ref, gate_out, up_out, o_grads, do, delta, lse_off, dk, dv, bias, *scratch):
+def backward_kernel(q_ref, do_ref, lse_ref, kv_ref, kd_ref, qdr_ref, low_ref, att_ref, grads_ref,
+                    dq_ref, dkv_ref, gate_out, up_out, down_out, o_grads, do, delta, lse_off, dk, dv, bias, att, att_rows, stage,
+                    local_sem, stage_sem, *scratch):
     f32, b16 = jnp.float32, jnp.bfloat16
     kv, all_rows, _ = q_ref.shape
     n, rows, _ = kv_ref.shape
     group = all_rows // rows
-    depth = o_all.shape[2]
-    me = lax.axis_index("seq")
+    pieces, m, sub, heads = att_rows.shape
+    piece = m * sub
+    depth = grads_ref.shape[2]
+    me, t = lax.axis_index("seq"), lax.axis_index("tp")
+    copies = [pltpu.make_async_copy(att_ref.at[:, t], att, local_sem.at[0]),
+              pltpu.make_async_copy(att_ref.at[:, :, pl.ds(pl.multiple_of(t * sub, sub), sub)], att_rows, local_sem.at[1])]
+    for copy in copies:
+        copy.start()
     tile = cut(rows)
     scale = HEAD_SIZE ** -0.5
     gate_sum = seq_sum(lambda j: grads_ref.at[j, 1], scratch[:SUM_SCRATCH])
-    up_sum = seq_sum(lambda j: grads_ref.at[j, 2], scratch[SUM_SCRATCH:])
+    up_sum = seq_sum(lambda j: grads_ref.at[j, 2], scratch[SUM_SCRATCH:2 * SUM_SCRATCH])
+    down_sum = seq_sum(lambda j: grads_ref.at[j, 0], scratch[2 * SUM_SCRATCH:])
 
     greet(True, False)
     gate_sum.begin()
@@ -792,21 +884,29 @@
     visible = (lax.broadcasted_iota(jnp.int32, (rows, rows), 0)
                <= lax.broadcasted_iota(jnp.int32, (rows, rows), 1)) & (kd_ref[...] == qdr_ref[...])
     bias[...] = jnp.where(visible, 0.0, -1e30)
-    for start in range(0, rows, tile):
-        grad = mm(low_ref[start:start + tile, :depth], o_all[0], NT)
-        for j in range(1, n):
-            grad = grad + mm(low_ref[start:start + tile, j * depth:(j + 1) * depth], o_all[j], NT)
-        grad = grad.astype(b16)
+    for copy in copies:
+        copy.wait()
+    for p in range(pieces):
         for h in range(kv):
             for g in range(group):
                 cols = slice((h * group + g) * HEAD_SIZE, (h * group + g + 1) * HEAD_SIZE)
-                at = slice(g * rows + start, g * rows + start + tile)
-                part = grad[:, cols]
-                do[h, at] = part
-                prod = part.astype(f32) * att_ref[start:start + tile, cols].astype(f32)
+                at = slice(g * rows + p * piece, g * rows + (p + 1) * piece)
+                grad = do_ref[p * piece:(p + 1) * piece, cols]
+                do[h, at] = grad
+                prod = grad.astype(f32) * att[p, :, cols].astype(f32)
                 delta[h, :, at] = jnp.sum(prod.T, axis=0, keepdims=True)
+
+    def staged(j):
+        return pltpu.make_async_copy(stage.at[j % 2], o_grads.at[j], stage_sem.at[j % 2])
+
     for j in range(n):
-        o_grads[j] = mm(low_ref[:, j * depth:(j + 1) * depth], att_ref[...], TN).astype(b16)
+        if j >= 2:
+            staged(j - 2).wait()
+        rows_low = low_ref[:, :, j * depth:(j + 1) * depth].reshape(pieces * sub, depth)
+        for k in range(m):
+            rows_att = att_rows[:, k].reshape(pieces * sub, heads)
+            stage[j % 2, :, k * heads:(k + 1) * heads] = mm(rows_low, rows_att, TN).astype(b16)
+        staged(j).start()
     for h in range(kv):
         for g in range(group):
             at = slice(g * rows, (g + 1) * rows)
@@ -824,21 +924,23 @@
         keep(me, h)
 
     steps = n * kv
-    events = [[] for _ in range(steps)]
+    events = [[] for _ in range(steps + 1)]
 
     def at_time(time, step, *args):
-        events[min(int(time / 3.8), steps - 1)].append((step, args))
-
-    def plan_sum(one, base, share):
+        events[min(int(time / 3.8), steps)].append((step, args))
+
+    def plan_sum(one, meet, *arrivals):
         for e in reversed(range(one.count)):
-            at_time(base, one.meet, e)
+            at_time(meet, one.meet, e)
         for k, found in enumerate(one.rounds()):
             for event in found:
-                at_time(base + share * 18.0 * (2.0 - 0.5 ** k), one.arrive, *event)
-
-    plan_sum(gate_sum, 0.0, 1.0)
+                at_time(arrivals[min(k, 1)] + k, one.arrive, *event)
+
+    plan_sum(gate_sum, 0.0, 22.0, 34.0)
     at_time(4.0, up_sum.begin)
-    plan_sum(up_sum, 15.0, 1.0)
+    plan_sum(up_sum, 15.0, 42.0, 52.0)
+    at_time(23.0, down_sum.begin)
+    plan_sum(down_sum, 34.0, 61.0, 70.0)
 
     @pl.loop(0, steps)
     def _(i):
@@ -856,41 +958,51 @@
             attn_bwd_block(h, q_ref, do, lse_off, delta, kv_ref.at[j], dq_ref, dk, dv, None, kv, rows, tile)
             keep(j, h)
 
+    for step, args in events[steps]:
+        step(*args)
+
     @pl.loop(me + 1, n)
     def _(j):
         dkv_ref[j] = jnp.zeros(dkv_ref.shape[1:], b16)
 
     dq_ref[...] *= scale
-    gate_out[...] = gate_sum.loc[0].astype(f32)
-    up_out[...] = up_sum.loc[0].astype(f32)
-    gate_sum.finish()
-    up_sum.finish()
-
-
-def attention_backward(queries, low, o_all, attended, lse, all_kv, doc_column, doc_row, grads):
+    gate_out[...] = gate_sum.loc[0]
+    up_out[...] = up_sum.loc[0]
+    down_out[...] = down_sum.loc[0]
+    for one in (gate_sum, up_sum, down_sum):
+        one.finish()
+    for j in range(max(n - 2, 0), n):
+        staged(j).wait()
+
+
+def attention_backward(queries, grad_attended, lse, all_kv, doc_column, doc_row, low, attended, grads):
     f32, b16 = jnp.float32, jnp.bfloat16
     kv, all_rows, _ = queries.shape
     n, rows, _ = all_kv.shape
     _, _, depth, ff = grads.shape
-    out = [(queries.shape, f32), (all_kv.shape, b16), ((depth, ff), f32), ((depth, ff), f32),
-           ((n, depth, attended.shape[1]), b16)]
+    pieces, m, piece, heads = attended.shape
+    out = [(queries.shape, f32), (all_kv.shape, b16), ((depth, ff), b16), ((depth, ff), b16), ((depth, ff), b16),
+           ((n, depth, m * heads), b16)]
+    dma = pltpu.SemaphoreType.DMA
     return pl.pallas_call(
         backward_kernel,
         out_shape=[jax.ShapeDtypeStruct(*one) for one in out],
-        in_specs=[VM] * 8 + [ANY],
-        out_specs=[VM] * 5,
+        in_specs=[VM] * 7 + [ANY] * 2,
+        out_specs=[VM] * 5 + [ANY],
         scratch_shapes=[pltpu.VMEM(queries.shape, b16), pltpu.VMEM((kv, 1, all_rows), f32), pltpu.VMEM((kv, 1, all_rows), f32),
-                        pltpu.VMEM((rows, HEAD_SIZE), f32), pltpu.VMEM((rows, HEAD_SIZE), f32), pltpu.VMEM((rows, rows), f32)]
-        + sum_scratch(depth, ff) + sum_scratch(depth, ff),
+                        pltpu.VMEM((rows, HEAD_SIZE), f32), pltpu.VMEM((rows, HEAD_SIZE), f32), pltpu.VMEM((rows, rows), f32),
+                        pltpu.VMEM((pieces, piece, heads), b16), pltpu.VMEM((pieces, m, piece // m, heads), b16),
+                        pltpu.VMEM((2, depth, m * heads), b16), dma((2,)), dma((2,))]
+        + sum_scratch(depth, ff) + sum_scratch(depth, ff) + sum_scratch(depth, ff),
         compiler_params=pltpu.CompilerParams(vmem_limit_bytes=VMEM_BYTES, collective_id=3, has_side_effects=True),
         name="attention_backward",
-    )(queries, low, o_all, attended, lse, all_kv, doc_column, doc_row, grads)
-
-
-def final_kernel(dq_ref, proj_ref, norm_ref, w_ref, cos_ref, sin_ref, gains_ref, after_ref, mlp_gain_ref,
-                 dkv_ref, grads_ref, o_grads_ref, tok_ref,
-                 buf, down_out, o_out, q_out, k_out, v_out, gain_out,
-                 dproj, part, recv, tok_own, w_grads, gain_seq, gain_line, local_sem, *scratch):
+    )(queries, grad_attended, lse, all_kv, doc_column, doc_row, low, attended, grads)
+
+
+def final_kernel(dq_in, proj_in, norm_in, w_in, cos_in, sin_in, after_in, gains_ref, mlp_gain_ref,
+                 dkv_ref, o_grads_ref, tok_ref,
+                 buf, o_out, w_out, gain_out, dq_ref, proj_ref, norm_ref, w_ref, cos_ref, sin_ref, after_ref,
+                 dproj, part, recv, tok_own, w_grads, gain_seq, gain_line, o_part, o_recv, local_sem, *scratch):
     f32, b16 = jnp.float32, jnp.bfloat16
     pieces, m, sub, width = part.shape
     n, depth, wide = w_ref.shape
@@ -902,18 +1014,21 @@
     me, t = lax.axis_index("seq"), lax.axis_index("tp")
     tile = cut(rows)
     kv_sum = seq_sum(lambda j: dkv_ref.at[j], scratch[:6])
-    down_sum = seq_sum(lambda j: grads_ref.at[j, 0], scratch[6:12])
-    o_sum = seq_sum(lambda j: o_grads_ref.at[j], scratch[12:18])
-    w_sum = seq_sum(lambda j: w_grads.at[j], scratch[18:24])
-    in_sum = LineSum(part, recv, scratch[24], scratch[25])
-    out_gather = LineGather(buf, scratch[26], scratch[27])
-    gain_gather = SeqGather(gain_seq, scratch[28], scratch[29], halves=1)
-    gain_total = LineGather(gain_line, scratch[30], scratch[31])
+    o_sum = seq_sum(lambda j: o_grads_ref.at[j], scratch[6:12])
+    w_sum = seq_sum(lambda j: w_grads.at[j], scratch[12:18])
+    in_sum = LineSum(part, recv, scratch[18], scratch[19])
+    out_gather = LineGather(buf, scratch[20], scratch[21])
+    gain_gather = SeqGather(gain_seq, scratch[22], scratch[23], halves=1)
+    gain_total = LineGather(gain_line, scratch[24], scratch[25])
+    o_total = DirectSum(o_part, o_recv, scratch[26], scratch[27])
 
     own = [pltpu.make_async_copy(tok_ref.at[p, t], tok_own.at[p], local_sem.at[p]) for p in range(pieces)]
-    for copy in own:
+    loads = [pltpu.make_async_copy(source, into, local_sem.at[pieces + i]) for i, (source, into) in enumerate((
+        (dq_in, dq_ref), (proj_in, proj_ref), (cos_in, cos_ref), (sin_in, sin_ref), (norm_in, norm_ref), (w_in, w_ref),
+        (after_in, after_ref)))]
+    for copy in own + loads:
         copy.start()
-    greet(True, True)
+    greet(True, "all")
     kv_sum.begin()
     gain_q, gain_k = gains_ref[0, 2:3, :HEAD_SIZE], gains_ref[0, 3:4, :HEAD_SIZE]
     for j in range(1, n):
@@ -923,7 +1038,7 @@
     gain_seq[me, 1:2] = mlp_gain_ref[...]
     for p in range(pieces):
         in_sum.clear(p)
-    for copy in own:
+    for copy in own + loads:
         copy.wait()
     plan = Plan()
 
@@ -990,8 +1105,7 @@
         for g in range(group):
             plan.at(1.0, queries_back, h, g)
     plan_sum(kv_sum, 7.0, 18.0)
-    plan.at(33.0, down_sum.begin)
-    plan.at(33.5, o_sum.begin)
+    plan.at(30.0, o_sum.begin)
     plan.at(43.5, keys_back)
     clock = 44.0
     hop = 8.0
@@ -1010,9 +1124,16 @@
     for j in range(n):
         plan.at(50.0 + 0.8 * j, weight_grads, j)
     plan.at(57.0, w_sum.begin)
-    plan_sum(down_sum, 48.0, 18.0)
-    plan_sum(o_sum, 49.0, 18.0)
-    plan_sum(w_sum, 76.0, 20.0)
+    plan_sum(o_sum, 56.0, 34.0)
+    plan_sum(w_sum, 90.0, 22.0)
+
+    def o_over_tp():
+        heads = o_part.shape[3]
+        for k in range(m):
+            o_part[0, k] = o_sum.loc[0, :, k * heads:(k + 1) * heads]
+        o_total.start(0)
+
+    plan.at(108.5, o_over_tp)
     gain_time = last - 3 * hop + 0.5
     plan.at(gain_time, gain_gather.start, 0)
     for k, event in enumerate(gain_gather.events()):
@@ -1034,43 +1155,78 @@
     for j in range(1, m):
         total = total + gain_line[0, j]
     gain_out[...] = total
-    down_out[...] = down_sum.loc[0].astype(f32).T
-    o_out[...] = o_sum.loc[0].astype(f32).T
-    q_out[...] = w_sum.loc[0, :, :q_width].astype(f32)
-    k_out[...] = w_sum.loc[0, :, q_width:q_width + k_width].astype(f32)
-    v_out[...] = w_sum.loc[0, :, q_width + k_width:].astype(f32)
-    for one in (kv_sum, down_sum, o_sum, w_sum, gain_gather):
+    o_out[...] = o_total.total(0).T
+    w_out[...] = w_sum.loc[0]
+    for one in (kv_sum, o_sum, w_sum, gain_gather):
         one.finish()
     in_sum.finish(pieces - 1)
     for p in range(pieces):
         out_gather.finish(p)
     gain_total.finish(0)
-
-
-def final(grad_queries, projected, normalized, w_all, cosines, sines, gains, after_grad, mlp_gain, grad_kv, grads, o_grads, tokens):
+    o_total.finish(0)
+
+
+def final(grad_queries, projected, normalized, w_all, cosines, sines, after_grad, gains, mlp_gain, grad_kv, o_grads, tokens):
     f32, b16 = jnp.float32, jnp.bfloat16
     pieces, m, sub, width = tokens.shape
     n, depth, wide = w_all.shape
     kv, all_rows, _ = grad_queries.shape
     rows, k_width = normalized.shape[0], kv * HEAD_SIZE
     q_width = wide - 2 * k_width
-    ff = grads.shape[3]
-    out = [(tokens.shape, b16), ((ff, depth), f32), ((q_width, depth), f32), ((depth, q_width), f32), ((depth, k_width), f32),
-           ((depth, k_width), f32), ((8, width), f32)]
+    out = [(tokens.shape, b16), ((q_width, depth), f32), ((depth, wide), b16), ((8, width), f32)]
+    held = (grad_queries, projected, normalized, w_all, cosines, sines, after_grad)
     return pl.pallas_call(
         final_kernel,
         out_shape=[jax.ShapeDtypeStruct(*one) for one in out],
-        in_specs=[VM] * 9 + [ANY] * 4,
-        out_specs=[VM] * 7,
-        scratch_shapes=[pltpu.VMEM((rows, wide), b16), pltpu.VMEM(tokens.shape, b16),
+        in_specs=[ANY] * 7 + [VM] * 2 + [ANY] * 3,
+        out_specs=[VM] * 4,
+        scratch_shapes=[pltpu.VMEM(one.shape, one.dtype) for one in held] + [pltpu.VMEM((rows, wide), b16), pltpu.VMEM(tokens.shape, b16),
                         pltpu.VMEM((pieces, m + 1, sub, width), b16), pltpu.VMEM((pieces, sub, width), b16),
                         pltpu.VMEM((n, depth, wide), b16), pltpu.VMEM((n, 8, width), f32), pltpu.VMEM((1, m, 8, width), f32),
-                        pltpu.SemaphoreType.DMA((pieces,))]
-        + sum_scratch(rows, 2 * k_width) + sum_scratch(depth, ff) + sum_scratch(depth, q_width) + sum_scratch(depth, wide)
-        + line_sems(pieces) + gather_sems(1) + line_sems(1)[2:],
+                        pltpu.VMEM((1, m, depth, q_width), b16), pltpu.VMEM((1, m, depth, q_width), b16),
+                        pltpu.SemaphoreType.DMA((pieces + 7,))]
+        + sum_scratch(rows, 2 * k_width) + sum_scratch(depth, m * q_width) + sum_scratch(depth, wide)
+        + line_sems(pieces) + gather_sems(1) + line_sems(1)[2:]
+        + [pltpu.SemaphoreType.DMA((1, m)), pltpu.SemaphoreType.DMA((1, m))],
         compiler_params=pltpu.CompilerParams(vmem_limit_bytes=VMEM_BYTES, collective_id=4, has_side_effects=True),
         name="final",
-    )(grad_queries, projected, normalized, w_all, cosines, sines, gains, after_grad, mlp_gain, grad_kv, grads, o_grads, tokens)
+    )(grad_queries, projected, normalized, w_all, cosines, sines, after_grad, gains, mlp_gain, grad_kv, o_grads, tokens)
+
+
+def finish_kernel(tokens_ref, layer_ref, gate_ref, up_ref, down_ref, o_ref, w_ref,
+                  tokens_out, layer_out, gate_out, up_out, down_out, o_out, q_out, k_out, v_out):
+    f32 = jnp.float32
+    tile = cut(tokens_ref.shape[0], 128)
+
+    @pl.loop(0, tokens_ref.shape[0] // tile)
+    def _(i):
+        at = pl.ds(i * tile, tile)
+        tokens_out[at] = tokens_ref[at].astype(f32)
+        layer_out[at] = layer_ref[at]
+
+    gate_out[...] = gate_ref[...].astype(f32)
+    up_out[...] = up_ref[...].astype(f32)
+    down_out[...] = down_ref[...].astype(f32).T
+    o_out[...] = o_ref[...]
+    first = 0
+    for out in (q_out, k_out, v_out):
+        out[...] = w_ref[:, first:first + out.shape[1]].astype(f32)
+        first += out.shape[1]
+
+
+def finish(tokens, layer, gate, up, down, o, w, q_width):
+    f32 = jnp.float32
+    depth, ff = gate.shape
+    k_width = (w.shape[1] - q_width) // 2
+    out = [(tokens.shape, f32), (layer.shape, layer.dtype), (gate.shape, f32), (up.shape, f32), ((ff, depth), f32), (o.shape, f32),
+           ((depth, q_width), f32), ((depth, k_width), f32), ((depth, k_width), f32)]
+    return pl.pallas_call(
+        finish_kernel,
+        out_shape=[jax.ShapeDtypeStruct(*one) for one in out],
+        in_specs=[VM] * 7, out_specs=[VM] * 9,
+        compiler_params=pltpu.CompilerParams(vmem_limit_bytes=VMEM_BYTES),
+        name="finish",
+    )(tokens, layer, gate, up, down, o, w)
 
 
 def pack_gains(attn_gain, mlp_gain, query_gain, key_gain):
@@ -1150,26 +1306,28 @@
     cosines, sine_values = rope_tables(positions, HEAD_SIZE)
     cos_wide = jnp.concatenate([cosines, cosines], axis=-1).reshape(local_rows, HEAD_SIZE)
     sin_wide = jnp.concatenate([-sine_values, sine_values], axis=-1).reshape(local_rows, HEAD_SIZE)
-    (normalized_input, projected, queries_h, all_kv, attended_low, lse, all_gains, w_all, o_all, gate_all) = forward_attention(
-        tokens, q_weight, key_matrix, value_matrix, gains, cos_wide, sin_wide, doc_column, doc_row, o_weight, gate_weight)
     model = tokens.shape[1]
-    ff = gate_weight.shape[1]
-    q_width, k_width = q_local * HEAD_SIZE, kv_local * HEAD_SIZE
     tp_count = lax.axis_size("tp")
     sub = math.gcd(local_rows // tp_count, 64)
     while local_rows // tp_count // sub > 3:
         sub *= 2
     split = (local_rows // tp_count // sub, tp_count, sub, model)
-    low_b, after_grad_own, mlp_part, mlp_gain_own, mlp_grads = middle(
-        attended_low, o_all, gate_all, up_weight, down_weight, tokens.reshape(split), cotangent.reshape(split), all_gains)
-    grad_after_low = low_b.reshape(local_rows, model)
+    (normalized_input, projected, queries_h, all_kv, attended_all, lse, all_gains, w_all, o_all, gate_all) = forward_attention(
+        tokens, q_weight, key_matrix, value_matrix, gains, cos_wide, sin_wide, doc_column, doc_row, o_weight, gate_weight, split[0])
+    ff = gate_weight.shape[1]
+    q_width, k_width = q_local * HEAD_SIZE, kv_local * HEAD_SIZE
+    low_own, after_grad_own, grad_attended, mlp_gain_own, mlp_part, mlp_grads = middle(
+        attended_all, o_all, gate_all, up_weight, down_weight, tokens.reshape(split), cotangent.reshape(split), all_gains)
     layer_out = lax.psum(mlp_part, "tp").reshape(local_rows, model)
 
-    grad_query_h, grad_kv, grad_gate_w, grad_up_w, o_grads = attention_backward(
-        queries_h, grad_after_low, o_all, attended_low, lse, all_kv, doc_column, doc_row, mlp_grads)
-    grad_tokens, grad_down, grad_o_w, grad_q_w, grad_k_w, grad_v_w, gain_sums = final(
-        grad_query_h, projected, normalized_input, w_all, cos_wide, sin_wide, all_gains, after_grad_own, mlp_gain_own,
-        grad_kv, mlp_grads, o_grads, tokens.reshape(split))
+    q_width = q_local * HEAD_SIZE
+    grad_query_h, grad_kv, gate_sum, up_sum, down_sum, o_grads = attention_backward(
+        queries_h, grad_attended.reshape(local_rows, q_width), lse, all_kv, doc_column, doc_row, low_own, attended_all, mlp_grads)
+    token_blocks, grad_o, grad_w, gain_sums = final(
+        grad_query_h, projected, normalized_input, w_all, cos_wide, sin_wide, after_grad_own, all_gains, mlp_gain_own,
+        grad_kv, o_grads, tokens.reshape(split))
+    (grad_tokens, layer_out, grad_gate_w, grad_up_w, grad_down, grad_o_w, grad_q_w, grad_k_w, grad_v_w) = finish(
+        token_blocks.reshape(local_rows, model), layer_out, gate_sum, up_sum, down_sum, grad_o, grad_w, q_width)
 
     def own_part(line, width):
         count = width // seq_count
@@ -1177,7 +1335,7 @@
 
     return (
         layer_out,
-        grad_tokens.reshape(local_rows, model).astype(f32),
+        grad_tokens,
         grad_q_w,
         grad_k_w,
         grad_v_w,

time: 703 us -> 625 us (0.89)
  Pallas kernels: 652 us -> 595 us
  local copies, waits for them, and re-layouts: 17 us -> 6.45 us
    pallas_call x1, Pallas kernels: 258 us -> 155 us  [middle(): pl.pallas_call(middle_kernel, out_shape=[jax.ShapeDtypeStruct(*one) for o...]
    pallas_call x1, Pallas kernels: 121 us -> 143 us  [forward_attention(): pl.pallas_call(forward_kernel, out_shape=[jax.ShapeDtypeStruct(*one) for...]
    pallas_call x1, Pallas kernels: 80.6 us -> 100 us  [attention_backward(): pl.pallas_call(backward_kernel, out_shape=[jax.ShapeDtypeStruct(*one) for...]
    unnamed x22 -> x0, local copies, waits for them, and re-layouts: 10.6 us -> none
    pallas_call x0 -> x1, Pallas kernels: none -> 9.97 us  [finish(): pl.pallas_call(finish_kernel, out_shape=[jax.ShapeDtypeStruct(*one) for o...]
  transfers between devices with their start and end apart: 1 -> 1, of which waited for: 0 -> 0; matrix products, arithmetic and copies ran while one was open for 1% -> 1% of each run, Pallas kernels for 39% -> 46%
where the time goes in v3:
time: 625 us; the launch traced here: 622 us
  Pallas kernels  595 us (95%)
  between operations  14.3 us (2%)
  local copies, waits for them, and re-layouts  6.45 us (1%)
    pallas_call x1, Pallas kernels, final(): pl.pallas_call(final_kernel, out_shape=[jax.ShapeDtypeStruct(*one) for on...  187 us
    pallas_call x1, Pallas kernels, middle(): pl.pallas_call(middle_kernel, out_shape=[jax.ShapeDtypeStruct(*one) for o...  155 us
    pallas_call x1, Pallas kernels, forward_attention(): pl.pallas_call(forward_kernel, out_shape=[jax.ShapeDtypeStruct(*one) for...  143 us
    pallas_call x1, Pallas kernels, attention_backward(): pl.pallas_call(backward_kernel, out_shape=[jax.ShapeDtypeStruct(*one) for...  100 us
  transfers between devices with their start and end apart: 1, of which 0 were waited for; matrix products, arithmetic and copies ran while one was open for 1% of the time, Pallas kernels for 46%

profile of v3, /device:TPU:0, one launch (start us, length us, event | category | flops | bytes accessed | tf_op | source)
XLA Modules:
  0.0 621.9 jit_solution(11300756142907931334)
XLA Ops:
  7.2 0.0 all-reduce.2.cloned.1.call-start
  7.2 0.8 dynamic_slice.23
  8.0 0.6 broadcast_in_dim.5.kd_ref.qdr_ref
  8.6 0.9 broadcast_in_dim.12.qd_ref.kd_ref
  9.5 0.7 bitcast_convert_fusion.1
  10.2 0.7 bitcast_convert_fusion
  10.8 0.7 stack.41
  11.5 0.7 stack.42
  12.2 0.7 convert_element_type.2
  12.8 0.1 dynamic_update_slice.8
  12.9 0.2 dynamic_update_slice.9
  13.1 1.4 fusion
  14.6 1.2 maximum_bitcast_fusion
  15.7 0.6 stack.40.gain_ref
  16.3 143.1 %forward_attention.1 = (bf16[768,2048]{1,0:T(8,128)(2,1)}, f32[768,1024]{1,0:T(8,128)}, bf16[2,1536,128]{2,1,0:T(8,128)(2,1)}, bf16[8,768,512]{2,1,0:T(8,128)(2,...) custom-call(bf16[768,2048]{1,0:T(8,128)(2,1)} %tok_ref.1, ...), custom_call_target="tpu_custom_call" | custom-call | tf_op jit(solution)/shard_map/forward_attention/pallas_call | solution.py:512
  159.4 154.6 %middle.1 = (bf16[3,64,2048]{2,1,0:T(8,128)(2,1)}, f32[3,64,2048]{2,1,0:T(8,128)}, bf16[3,4,64,512]{3,2,1,0:T(8,128)(2,1)}, f32[1,2048]{1,0:T(1,128)}, bf16[3,4,...) custom-call(bf16[3,4,256,512]{3,2,1,0:T(8,128)(2,1)} %get-tuple-element.49.att_ref, ...), custom_call_target="tpu_custom_call" | custom-call | tf_op jit(solution)/shard_map/middle/pallas_call | solution.py:816
  314.0 0.0 all-reduce.2.cloned.1.call-update
  314.1 100.3 %attention_backward.1 = (f32[2,1536,128]{2,1,0:T(8,128)}, bf16[8,768,512]{2,1,0:T(8,128)(2,1)}, bf16[256,1536]{1,0:T(8,128)(2,1)}, bf16[256,1536]{1,0:T(8,128)(2...) custom-call(bf16[2,1536,128]{2,1,0:T(8,128)(2,1)} %get-tuple-element.48.q_ref, bf16[768,512]{1,0:T(8,128)(2,1)} %bitcast.28, ...), custom_call_target="tpu_custom_call" | custom-call | tf_op jit(solution)/shard_map/attention_backward/pallas_call | solution.py:987
  414.4 187.2 %final.1 = (bf16[3,4,64,2048]{3,2,1,0:T(8,128)(2,1)}, f32[512,256]{1,0:T(8,128)}, bf16[256,1024]{1,0:T(8,128)(2,1)}, f32[8,2048]{1,0:T(8,128)}) custom-call(f32[2,1536,128]{2,1,0:T(8,128)} %get-tuple-element.58.dq_in, f32[768,1024]{1,0:T(8,128)} %get-tuple-element.59.proj_in, bf16[768,2048]{1,0:T(8,128)(2,1)} %get-tuple-element.60.norm_in, ...), custom_call_target="tpu_custom_call" | custom-call | tf_op jit(solution)/shard_map/final/pallas_call | solution.py:1178
  601.6 1.0 fusion.3
  602.6 0.6 fusion.2
  603.2 0.6 fusion.1
  603.8 0.6 constant_dynamic-slice_fusion.2
  604.3 0.6 constant_dynamic-slice_fusion.3
  604.9 0.0 all-reduce.2.cloned.1.call-done.layer_ref
  604.9 10.0 %finish.1 = (f32[768,2048]{1,0:T(8,128)}, bf16[768,2048]{1,0:T(8,128)(2,1)}, f32[256,1536]{1,0:T(8,128)}, f32[256,1536]{1,0:T(8,128)}, f32[1536,256]{1,0:T(8,128...) custom-call(bf16[768,2048]{1,0:T(8,128)(2,1)} %bitcast.27, ...), custom_call_target="tpu_custom_call" | custom-call | tf_op jit(solution)/shard_map/finish/pallas_call | solution.py:1223
  (4 shorter events, 0.0 us)
Async XLA Ops:
  7.2 597.7 %all-reduce.2.cloned.1.call-start = ((), (), s32[]{:S(2)}) async-start(), calls=%async_computation | async-start | bytes 6291456 | tf_op jit(solution)/shard_map/psum | solution.py:1321
Sparse Core Ops, SparseCore 0:
  314.2 120.5 all-reduce.1

commit v4 on v3

--- a/solution.py
+++ b/solution.py
@@ -328,9 +328,9 @@
     return lax.rsqrt(jnp.mean(values * values, axis=-1, keepdims=True) + EPS)
 
 
-def forward_kernel(tok_ref, wq_ref, wk_ref, wv_ref, gain_ref, cos_ref, sin_ref, qd_ref, kd_ref, o_ref, gate_ref,
-                   norm_ref, proj_ref, q_ref, kv_ref, att_all, lse_ref, gains_ref, w, o_all, gate_all,
-                   inv, acc, total, bias, local_sem, *sems):
+def forward_kernel(tok_in, wq_ref, wk_ref, wv_ref, gain_ref, cos_ref, sin_ref, qd_ref, kd_ref, o_ref, gate_ref,
+                   norm_out, proj_out, q_ref, kv_out, att_all, lse_ref, gains_ref, w_out, o_all, gate_all,
+                   tok_ref, norm_ref, proj_ref, kv_ref, w, inv, acc, total, bias, local_sem, *sems):
     f32, b16 = jnp.float32, jnp.bfloat16
     n, rows, _ = kv_ref.shape
     kv, all_rows, _ = q_ref.shape
@@ -355,7 +355,10 @@
            pltpu.make_async_copy(wv_ref, w.at[me, :, pl.ds(q_width + k_width, k_width)], local_sem.at[2]),
            pltpu.make_async_copy(o_ref, o_all.at[me, t], local_sem.at[3]),
            pltpu.make_async_copy(gate_ref, gate_all.at[me], local_sem.at[4])]
-    for copy in own:
+    tok_copy = pltpu.make_async_copy(tok_in, tok_ref, local_sem.at[5])
+    results = [pltpu.make_async_copy(here, there, local_sem.at[6 + i]) for i, (here, there) in enumerate(
+        ((norm_ref, norm_out), (proj_ref, proj_out), (w, w_out), (kv_ref, kv_out)))]
+    for copy in own + [tok_copy]:
         copy.start()
     gains_ref[me] = gain_ref[...]
     greet(True, True)
@@ -367,6 +370,8 @@
     own[3].wait()
     o_line.start(0)
 
+    tok_copy.wait()
+
     @pl.loop(0, rows // tile)
     def _(i):
         at = pl.ds(i * tile, tile)
@@ -432,6 +437,8 @@
             for g in range(group):
                 q_ref[h, pl.ds(g * rows + i * tile, tile)] = rotated(at, (h * group + g) * HEAD_SIZE, gain_q)
 
+    for copy in results[:3]:
+        copy.start()
     acc[...] = jnp.zeros_like(acc)
     total[...] = jnp.zeros_like(total)
     attn_fwd_block(q_ref, kv_ref.at[me], acc.at[0], total.at[0], bias, kv, rows, tile)
@@ -478,6 +485,7 @@
         def _():
             attn_fwd_block(q_ref, kv_ref.at[source], acc.at[1], total.at[1], None, kv, rows, tile)
 
+    results[3].start()
     plan = Plan()
     for p in range(pieces):
         plan.at(p, attended, p)
@@ -487,6 +495,8 @@
         for event in gather.events():
             plan.at((4.0, 25.0, 42.0, 48.0)[min(gather.level(*event), 3)], gather.arrive, *event)
     plan.run()
+    for copy in results:
+        copy.wait()
     o_line.finish(0)
     for p in range(pieces):
         att_gather.finish(p)
@@ -512,10 +522,11 @@
     return pl.pallas_call(
         forward_kernel,
         out_shape=[jax.ShapeDtypeStruct(*one) for one in out],
-        in_specs=[VM] + [ANY] * 3 + [VM] * 5 + [ANY] * 2,
-        out_specs=[VM] * 8 + [ANY] * 2,
-        scratch_shapes=[pltpu.VMEM((rows, 1), f32), pltpu.VMEM((2,) + heads, f32),
-                        pltpu.VMEM((2,) + heads, f32), pltpu.VMEM((rows, rows), f32), pltpu.SemaphoreType.DMA((5,))] + sems,
+        in_specs=[ANY] * 4 + [VM] * 5 + [ANY] * 2,
+        out_specs=[ANY, ANY, VM, ANY, VM, VM, VM, ANY, ANY, ANY],
+        scratch_shapes=[pltpu.VMEM((rows, width), b16), pltpu.VMEM((rows, width), b16), pltpu.VMEM((rows, wide), f32),
+                        pltpu.VMEM((n, rows, 2 * k_width), b16), pltpu.VMEM((n, depth, wide), b16), pltpu.VMEM((rows, 1), f32), pltpu.VMEM((2,) + heads, f32),
+                        pltpu.VMEM((2,) + heads, f32), pltpu.VMEM((rows, rows), f32), pltpu.SemaphoreType.DMA((10,))] + sems,
         compiler_params=pltpu.CompilerParams(vmem_limit_bytes=VMEM_BYTES, collective_id=1, has_side_effects=True),
         name="forward_attention",
     )(tokens, q_weight, key_matrix, value_matrix, gains, cosines, sines, doc_column, doc_row, o_weight, gate_weight)

time: 625 us -> 619 us (level)
  transfers between devices with their start and end apart: 1 -> 1, of which waited for: 0 -> 0; matrix products, arithmetic and copies ran while one was open for 1% -> 1% of each run, Pallas kernels for 46% -> 47%
where the time goes in v4:
time: 619 us; the launch traced here: 616 us
  Pallas kernels  589 us (95%)
  between operations  14.3 us (2%)
  local copies, waits for them, and re-layouts  6.45 us (1%)
    pallas_call x1, Pallas kernels, final(): pl.pallas_call(final_kernel, out_shape=[jax.ShapeDtypeStruct(*one) for on...  187 us
    pallas_call x1, Pallas kernels, middle(): pl.pallas_call(middle_kernel, out_shape=[jax.ShapeDtypeStruct(*one) for o...  155 us
    pallas_call x1, Pallas kernels, forward_attention(): pl.pallas_call(forward_kernel, out_shape=[jax.ShapeDtypeStruct(*one) for...  137 us
    pallas_call x1, Pallas kernels, attention_backward(): pl.pallas_call(backward_kernel, out_shape=[jax.ShapeDtypeStruct(*one) for...  100 us
  transfers between devices with their start and end apart: 1, of which 0 were waited for; matrix products, arithmetic and copies ran while one was open for 1% of the time, Pallas kernels for 47%

profile of v4, /device:TPU:0, one launch (start us, length us, event | category | flops | bytes accessed | tf_op | source)
XLA Modules:
  0.0 615.8 jit_solution(10506048251400151938)
XLA Ops:
  7.2 0.0 all-reduce.2.cloned.1.call-start
  7.2 0.8 dynamic_slice.23
  8.0 0.6 broadcast_in_dim.5.kd_ref.qdr_ref
  8.6 0.9 broadcast_in_dim.12.qd_ref.kd_ref
  9.5 0.7 bitcast_convert_fusion.1
  10.2 0.7 bitcast_convert_fusion
  10.8 0.7 stack.41
  11.5 0.7 stack.42
  12.2 0.7 convert_element_type.2
  12.8 0.1 dynamic_update_slice.8
  12.9 0.2 dynamic_update_slice.9
  13.1 1.4 fusion
  14.6 1.2 maximum_bitcast_fusion
  15.7 0.6 stack.40.gain_ref
  16.3 136.9 %forward_attention.1 = (bf16[768,2048]{1,0:T(8,128)(2,1)}, f32[768,1024]{1,0:T(8,128)}, bf16[2,1536,128]{2,1,0:T(8,128)(2,1)}, bf16[8,768,512]{2,1,0:T(8,128)(2,...) custom-call(bf16[768,2048]{1,0:T(8,128)(2,1)} %tok_in.1, ...), custom_call_target="tpu_custom_call" | custom-call | tf_op jit(solution)/shard_map/forward_attention/pallas_call | solution.py:522
  153.2 154.7 %middle.1 = (bf16[3,64,2048]{2,1,0:T(8,128)(2,1)}, f32[3,64,2048]{2,1,0:T(8,128)}, bf16[3,4,64,512]{3,2,1,0:T(8,128)(2,1)}, f32[1,2048]{1,0:T(1,128)}, bf16[3,4,...) custom-call(bf16[3,4,256,512]{3,2,1,0:T(8,128)(2,1)} %get-tuple-element.49.att_ref, ...), custom_call_target="tpu_custom_call" | custom-call | tf_op jit(solution)/shard_map/middle/pallas_call | solution.py:827
  307.9 0.0 all-reduce.2.cloned.1.call-update
  307.9 100.3 %attention_backward.1 = (f32[2,1536,128]{2,1,0:T(8,128)}, bf16[8,768,512]{2,1,0:T(8,128)(2,1)}, bf16[256,1536]{1,0:T(8,128)(2,1)}, bf16[256,1536]{1,0:T(8,128)(2...) custom-call(bf16[2,1536,128]{2,1,0:T(8,128)(2,1)} %get-tuple-element.48.q_ref, bf16[768,512]{1,0:T(8,128)(2,1)} %bitcast.28, ...), custom_call_target="tpu_custom_call" | custom-call | tf_op jit(solution)/shard_map/attention_backward/pallas_call | solution.py:998
  408.3 187.2 %final.1 = (bf16[3,4,64,2048]{3,2,1,0:T(8,128)(2,1)}, f32[512,256]{1,0:T(8,128)}, bf16[256,1024]{1,0:T(8,128)(2,1)}, f32[8,2048]{1,0:T(8,128)}) custom-call(f32[2,1536,128]{2,1,0:T(8,128)} %get-tuple-element.58.dq_in, f32[768,1024]{1,0:T(8,128)} %get-tuple-element.59.proj_in, bf16[768,2048]{1,0:T(8,128)(2,1)} %get-tuple-element.60.norm_in, ...), custom_call_target="tpu_custom_call" | custom-call | tf_op jit(solution)/shard_map/final/pallas_call | solution.py:1189
  595.5 1.0 fusion.3
  596.5 0.6 fusion.2
  597.1 0.6 fusion.1
  597.7 0.6 constant_dynamic-slice_fusion.2
  598.2 0.6 constant_dynamic-slice_fusion.3
  598.8 0.0 all-reduce.2.cloned.1.call-done.layer_ref
  598.8 10.0 %finish.1 = (f32[768,2048]{1,0:T(8,128)}, bf16[768,2048]{1,0:T(8,128)(2,1)}, f32[256,1536]{1,0:T(8,128)}, f32[256,1536]{1,0:T(8,128)}, f32[1536,256]{1,0:T(8,128...) custom-call(bf16[768,2048]{1,0:T(8,128)(2,1)} %bitcast.27, ...), custom_call_target="tpu_custom_call" | custom-call | tf_op jit(solution)/shard_map/finish/pallas_call | solution.py:1234
  (4 shorter events, 0.0 us)
Async XLA Ops:
  7.2 591.6 %all-reduce.2.cloned.1.call-start = ((), (), s32[]{:S(2)}) async-start(), calls=%async_computation | async-start | bytes 6291456 | tf_op jit(solution)/shard_map/psum | solution.py:1332
Sparse Core Ops, SparseCore 0:
  308.1 120.5 all-reduce.1
